TPU v7x, 32 devices: a whole 2x2x4 slice. The times are simulated.
32 devices in a mesh: dp: 16 (over z, y, x), ctx: 2 (over core).
Axes of the slice: x: 2, y: 2, z: 4, core: 2. Of those that a mesh axis runs over, the one named last changes fastest.
Arguments:
- tokens_in: bfloat16 [16, 1024, 768], P('dp', 'ctx'), may hold values from -6 to 6
- cond_vec: bfloat16 [16, 128], P('dp'), may hold values from -6 to 6
- positions: int32 [16, 1024], P('dp', 'ctx'), may hold values from 0 to 3069, as said below
- absorbed: int32 [16, 1024], P('dp', 'ctx'), may hold values 0 or 1
- cotangent: bfloat16 [16, 1024, 768], P('dp', 'ctx'), may hold values from -6 to 6
- norm1_gain: bfloat16 [768], replicated, may hold values from 0.5 to 1.5
- qkv_weight: bfloat16 [768, 2304], replicated, may hold values from -0.21875 to 0.21875
- out_weight: bfloat16 [768, 768], replicated, may hold values from -0.875 to 0.875
- norm2_gain: bfloat16 [768], replicated, may hold values from 0.5 to 1.5
- fc1_weight: bfloat16 [768, 3072], replicated, may hold values from -0.21875 to 0.21875
- fc1_bias: bfloat16 [3072], replicated, may hold values from -1.75 to 1.75
- fc2_weight: bfloat16 [3072, 768], replicated, may hold values from -0.109375 to 0.109375
- fc2_bias: bfloat16 [768], replicated, may hold values from -1.75 to 1.75
- ada_weight: bfloat16 [128, 4608], replicated, may hold values from -0.25 to 0.25
- ada_bias: bfloat16 [4608], replicated, may hold values from -1.75 to 1.75
Outputs:
- mixed: bfloat16 [16, 1024, 768], P('dp', 'ctx')
- input_grad: bfloat16 [16, 1024, 768], P('dp', 'ctx')
- cond_grad: float32 [16, 128], P('dp')
- norm1_gain_grad: float32 [768], P('dp')
- qkv_grad: float32 [768, 2304], P('dp')
- out_grad: float32 [768, 768], P('dp')
- norm2_gain_grad: float32 [768], P('dp')
- fc1_grad: float32 [768, 3072], P('dp')
- fc1_bias_grad: float32 [3072], P('dp')
- fc2_grad: float32 [3072, 768], P('dp')
- fc2_bias_grad: float32 [768], P('dp')
- ada_grad: float32 [128, 4608], P(None, 'dp')
- ada_bias_grad: float32 [4608], P('dp')
Inputs may be any that keep to these rules, and one draw needn't show every extreme that they name: In each sequence the positions start at 0 and rise by 1 to 3 from one token to the next.
All inputs are finite; a program needn't handle non-finite values. No bound on the sum of `absorbed` on one device may be relied on, other than what follows from the above.
Results may differ from a plain program's by a relative error of at most 0.019.
Values may be sent and summed in bfloat16 or wider, within the bound.
No kernel may reach another device: no remote copies, remote signals or barrier semaphores. Data moves between devices by JAX's collectives and lax.ppermute only.
A program may use at most 192 MiB of HBM per device.

v0:
```python
import functools

import jax
import jax.numpy as jnp
import numpy as np
from jax import lax
from jax.experimental import pallas as pl
from jax.experimental.pallas import tpu as pltpu
from jax.sharding import PartitionSpec as P

HEADS = 12
HEAD_DIM = 64
EPS = 1e-05
SCORE_SCALE = 0.125
NEG_START = -1e30
F32, BF16 = jnp.float32, jnp.bfloat16
COST = 2e8
MLP_COLS = 1536
BWD_BLK = 512


def dot(a, b):
    return jnp.dot(a, b, preferred_element_type=F32)


def dot_tn(a, b):
    return lax.dot_general(a, b, (((0,), (0,)), ((), ())), preferred_element_type=F32)


def dot_nt(a, b):
    return lax.dot_general(a, b, (((1,), (1,)), ((), ())), preferred_element_type=F32)


def sds(shape, dtype):
    return jax.ShapeDtypeStruct(shape, dtype)


def hbm(x):
    return pltpu.with_memory_space_constraint(x, pltpu.HBM)


class Order:
    def __init__(self, place):
        self.place, self.token = place, None

    def call(
        self, body, args, grid, in_specs, out_specs, out_shape, scratch=(), mb=32, us=1.0, aliases=None, after=(),
        name=None,
    ):
        after = list(after) + ([] if self.token is None else [self.token])
        extra, n_in, n_out = len(after), 1 + len(args), len(out_shape)

        def inner(*refs):
            outs = refs[n_in + extra :]
            body(*refs[:n_in], *outs[:n_out], *outs[n_out + 1 :])

        *outs, self.token = pl.pallas_call(
            inner,
            grid_spec=pltpu.PrefetchScalarGridSpec(
                num_scalar_prefetch=1,
                grid=grid,
                in_specs=list(in_specs) + [ANY] * extra,
                out_specs=list(out_specs) + [ANY],
                scratch_shapes=list(scratch),
            ),
            out_shape=list(out_shape) + [sds((8, 128), F32)],
            input_output_aliases=aliases or {},
            compiler_params=pltpu.CompilerParams(vmem_limit_bytes=mb << 20),
            cost_estimate=pl.CostEstimate(flops=int(us * COST), bytes_accessed=1 << 16, transcendentals=0),
            name=name,
        )(self.place, *args, *after)
        return outs


ANY = pl.BlockSpec(memory_space=pl.ANY)


def whole(shape):
    return pl.BlockSpec(shape, lambda *a: (0,) * len(shape))


def layer_stats(stream):
    row_mean = jnp.mean(stream, axis=-1, keepdims=True)
    centred = stream - row_mean
    variance = jnp.mean(centred * centred, axis=-1, keepdims=True)
    inv = lax.rsqrt(variance + EPS)
    return centred * inv, inv


def swap_lanes(x):
    lane = lax.broadcasted_iota(jnp.int32, x.shape, 1) % HEAD_DIM
    half = HEAD_DIM // 2
    return jnp.where(lane < half, pltpu.roll(x, 128 - half, 1), pltpu.roll(x, half, 1))


def mask_half(value, head):
    lane = lax.broadcasted_iota(jnp.int32, value.shape, 1)
    keep = (lane < HEAD_DIM) if head == 0 else (lane >= HEAD_DIM)
    return jnp.where(keep, value, jnp.zeros_like(value))


def attend_body(
    s_ref, ta_ref, tb_ref, cond_ref, ada_ref, adab_ref, gain_ref, wq_ref, wk_ref, wv_ref, pa_ref, pb_ref, freq_ref,
    cot_ref, abs_ref,
    n1_out, q_out, k_out, v_out, cost_ref, sint_ref,
    out_ref, prob_ref, inv_ref, mod_ref, wtd_ref, scores_ref, top_ref, vt_ref, n1_ref, q_ref, k_ref, v_ref,
):
    pair, step = pl.program_id(0), pl.program_id(1)
    span, width = ta_ref.shape
    blk = out_ref.shape[1]

    @pl.when((pair == 0) & (step == 0))
    def _():
        kept = jnp.broadcast_to(abs_ref[...].astype(F32), (128, span)).T[:, 0:1]
        wtd_ref[...] = (cot_ref[...].astype(F32) * kept).astype(BF16)
        cond = jnp.broadcast_to(cond_ref[...].astype(F32), (16, cond_ref.shape[1])).astype(BF16)
        mod_ref[...] = dot(cond, ada_ref[...])[:8] + adab_ref[...].astype(F32)[None, :]
        shift, scale = mod_ref[0:1, 0:width], mod_ref[0:1, width : 2 * width]
        gain = gain_ref[...].astype(F32)[None, :] * (1.0 + scale)
        for half, (t_ref, p_ref) in enumerate(((ta_ref, pa_ref), (tb_ref, pb_ref))):
            rows = slice(half * span, (half + 1) * span)
            angles = freq_ref[...] * p_ref[...].astype(F32)
            cos_h, sin_h = jnp.cos(angles), jnp.sin(angles)
            cos_t, sin_t = rotation(cos_h, sin_h)
            cost_ref[:, rows] = cos_h
            sint_ref[:, rows] = sin_h
            cos_n, sin_n = cos_t.T, sin_t.T
            a_one, _ = layer_stats(t_ref[...].astype(F32))
            normed = (a_one * gain + shift).astype(BF16)
            n1_ref[rows, :] = a_one.astype(BF16)
            q_pre = dot(normed, wq_ref[...])
            k_pre = dot(normed, wk_ref[...])
            v_ref[rows, :] = dot(normed, wv_ref[...]).astype(BF16)
            for p in range(q_pre.shape[1] // 128):
                at = slice(p * 128, (p + 1) * 128)
                part = q_pre[:, at]
                q_ref[rows, at] = (SCORE_SCALE * (part * cos_n + swap_lanes(part) * sin_n)).astype(BF16)
                part = k_pre[:, at]
                k_ref[rows, at] = (part * cos_n + swap_lanes(part) * sin_n).astype(BF16)

    pairs, blocks = pl.num_programs(0), pl.num_programs(1)
    lanes = lambda p: pl.ds(pl.multiple_of(p * 128, 128), 128)
    piece = jnp.minimum(pair * blocks + step, n1_ref.shape[0] // n1_out.shape[0] - 1)
    n1_out[...] = n1_ref[pl.ds(pl.multiple_of(piece * n1_out.shape[0], 128), n1_out.shape[0]), :]
    length = k_ref.shape[0]
    cut = 512

    def queries(p, i, head):
        return mask_half(q_ref[pl.ds(pl.multiple_of(i * blk, blk), blk), lanes(p)], head)

    def top_rows(scores):
        return jnp.max(scores.reshape(scores.shape[0] // 8, 8, blk), axis=0)

    @pl.when((pair == 0) & (step == 0))
    def _():
        vt_ref[...] = v_ref[...].T
        q_0 = queries(0, 0, 0)
        top = None
        for at in range(0, length, cut):
            scores = dot_nt(k_ref[at : at + cut, 0:128], q_0)
            scores_ref[0, at : at + cut] = scores
            top = top_rows(scores) if top is None else jnp.maximum(top, top_rows(scores))
        top_ref[0] = top

    @pl.when(step == 0)
    def _():
        q_out[...] = q_ref[:, lanes(pair)]
        k_out[...] = k_ref[:, lanes(pair)]
        v_out[...] = v_ref[:, lanes(pair)]

    for head in (0, 1):
        if head == 0:
            next_pair, next_step = pair, step
        else:
            wrap = step == blocks - 1
            next_step = jnp.where(wrap, 0, step + 1)
            next_pair = jnp.minimum(jnp.where(wrap, pair + 1, pair), pairs - 1)
        q_next = queries(next_pair, next_step, 1 - head)
        top = jnp.max(top_ref[head], axis=0, keepdims=True)
        rows = pl.ds(pl.multiple_of(pair * 128 + head * HEAD_DIM, HEAD_DIM), HEAD_DIM)
        next_top = sums = part = None
        for at in range(0, length, cut):
            here = slice(at, at + cut)
            scores = dot_nt(k_ref[here, lanes(next_pair)], q_next)
            scores_ref[1 - head, here] = scores
            new_top = top_rows(scores)
            raised = jnp.exp(scores_ref[head, here] - top)
            new_sums = jnp.sum(raised.reshape(cut // 8, 8, blk), axis=0)
            prob = raised.astype(BF16)
            prob_ref[head, here] = prob
            new_part = dot(vt_ref[rows, here], prob)
            next_top = new_top if next_top is None else jnp.maximum(next_top, new_top)
            sums = new_sums if sums is None else sums + new_sums
            part = new_part if part is None else part + new_part
        top_ref[1 - head] = next_top
        inverse = 1.0 / jnp.sum(sums, axis=0, keepdims=True)
        inv_ref[0, head : head + 1, :] = inverse
        out_ref[head * HEAD_DIM : (head + 1) * HEAD_DIM, :] = (part * inverse).astype(BF16)


def attend_call(order, tok, tok_o, cond, ada, adab, gain, qkv_weight, pos, pos_o, cot, absorbed):
    span, width = tok.shape
    length, hw = 2 * span, width // 2
    pairs, blk = hw // 128, 512
    freq = np.power(10000.0, -np.arange(0, HEAD_DIM, 2) / HEAD_DIM).astype(np.float32)[:, None]
    wspec = lambda j: pl.BlockSpec((width, hw), lambda p, i, s: (0, 2 * j + s[0]))
    col = pl.BlockSpec((length, 128), lambda p, i, s: (0, p))
    return order.call(
        attend_body,
        [hbm(tok), tok_o, hbm(cond), hbm(ada), hbm(adab), hbm(gain), *[hbm(qkv_weight)] * 3, hbm(pos), pos_o, hbm(jnp.asarray(freq)), hbm(cot), hbm(absorbed)],
        (pairs, length // blk),
        [whole(tok.shape), whole(tok.shape), whole(cond.shape), whole(ada.shape), whole(adab.shape), whole(gain.shape), wspec(0), wspec(1), wspec(2),
         whole(pos.shape), whole(pos.shape), whole(freq.shape), whole(cot.shape), whole(absorbed.shape)],
        [pl.BlockSpec((length // 4, width), lambda p, i, s: (jnp.minimum(p * (length // blk) + i, 3), 0)),
         col, col, col, whole((HEAD_DIM // 2, length)), whole((HEAD_DIM // 2, length)),
         pl.BlockSpec((128, blk), lambda p, i, s: (p, i)),
         pl.BlockSpec((2, length, blk), lambda p, i, s: (p, 0, i)),
         pl.BlockSpec((1, 8, blk), lambda p, i, s: (p, 0, i)), whole((8, ada.shape[1])), whole(tok.shape)],
        [sds((length, width), BF16)] + [sds((length, hw), BF16)] * 3
        + [sds((HEAD_DIM // 2, length), F32)] * 2
        + [sds((hw, length), BF16), pltpu.HBM((2 * pairs, length, length), BF16), sds((pairs, 8, length), F32),
           sds((8, ada.shape[1]), F32), sds(tok.shape, BF16)],
        scratch=[pltpu.VMEM((2, length, blk), F32), pltpu.VMEM((2, 8, blk), F32), pltpu.VMEM((hw, length), BF16),
                 pltpu.VMEM((length, width), BF16)] + [pltpu.VMEM((length, hw), BF16)] * 3,
        mb=40, us=20, name="attend",
    )


def swap_rows(x):
    half = HEAD_DIM // 2
    return jnp.concatenate([x[half * j : half * (j + 1)] for j in (1, 0, 3, 2)], axis=0)


def rotation(cos_h, sin_h):
    return jnp.concatenate([cos_h] * 4, axis=0), jnp.concatenate([-sin_h, sin_h, -sin_h, sin_h], axis=0)


def attn_bwd_body(
    r, s_ref, prob_ref, inv_ref, gt_ref, out_ref, q_ref, k_ref, v_ref, cost_ref, sint_ref, a_ref,
    mod_ref, gain_ref, wq_ref, wk_ref, wv_ref,
    g_ref, sum_ref, keep_ref, send_ref, vm_ref, kt_ref, dk_acc, dv_acc, acc_ref,
):
    step = pl.program_id(1)
    blk = q_ref.shape[0]

    @pl.when(step == 0)
    def _():
        values = v_ref[...]
        for head in (0, 1):
            vm_ref[head] = mask_half(values, head)
        kt_ref[...] = k_ref[...].T

    queries = q_ref[...]
    grad_t = gt_ref[...].astype(jnp.float32)
    row_id = lax.broadcasted_iota(jnp.int32, (128, blk), 0)
    inverse = jnp.where(row_id < HEAD_DIM, inv_ref[0, 0:1, :], inv_ref[0, 1:2, :])
    grad_t = grad_t * inverse
    product = grad_t * out_ref[...].astype(jnp.float32)
    grad_b = grad_t.astype(jnp.bfloat16)
    dk_new = None
    dq_parts = []
    for head in (0, 1):
        rows = slice(head * HEAD_DIM, (head + 1) * HEAD_DIM)
        delta = jnp.sum(product[rows], axis=0, keepdims=True)
        keep = (row_id < HEAD_DIM) if head == 0 else (row_id >= HEAD_DIM)
        grad_m = jnp.where(keep, grad_b, jnp.zeros_like(grad_b))
        grad_p = jnp.dot(vm_ref[head], grad_b, preferred_element_type=jnp.float32)
        prob = prob_ref[head]
        grad_s = (prob.astype(jnp.float32) * (grad_p - delta)).astype(jnp.bfloat16)
        dv_h = dot_nt(prob, grad_m)
        dk_h = dot(grad_s, mask_half(queries, head))
        if dk_new is None:
            dk_new, dv_new = dk_h, dv_h
        else:
            dk_new, dv_new = dk_new + dk_h, dv_new + dv_h
        dq_parts.append(dot(kt_ref[rows, :], grad_s) * SCORE_SCALE)
    dq_t = jnp.concatenate(dq_parts, axis=0)
    here = pl.ds(pl.multiple_of(step * blk, blk), blk)
    cos_t, sin_t = rotation(cost_ref[:, here], sint_ref[:, here])
    dq_t = dq_t * cos_t - swap_rows(dq_t) * sin_t
    g_ref[here, 0:128] = dq_t.T.astype(jnp.bfloat16)

    @pl.when(step == 0)
    def _():
        dk_acc[...] = dk_new
        dv_acc[...] = dv_new

    @pl.when(step > 0)
    def _():
        dk_acc[...] += dk_new
        dv_acc[...] += dv_new

    @pl.when(step == pl.num_programs(1) - 1)
    def _():
        dk = dk_acc[...]
        cos_t, sin_t = rotation(cost_ref[...], sint_ref[...])
        g_ref[:, 128:256] = (dk * cos_t.T - swap_lanes(dk) * sin_t.T).astype(jnp.bfloat16)
        g_ref[:, 256:384] = dv_acc[...].astype(jnp.bfloat16)
        grads = g_ref[...]
        product = dot_tn(a_ref[...], grads)
        width = a_ref.shape[1]
        column = lambda row: jnp.broadcast_to(row, (128, width)).T
        gain = column(gain_ref[...].astype(F32)[None, :] * (1.0 + mod_ref[0:1, width : 2 * width]))
        shift = column(mod_ref[0:1, 0:width])
        tokens = jnp.sum(grads.astype(F32), axis=0, keepdims=True)
        high = tokens.astype(BF16)
        low = (tokens - high.astype(F32)).astype(BF16)
        row_id = lax.broadcasted_iota(jnp.int32, (16, 384), 0)
        terms = jnp.where(row_id == 0, high, jnp.where(row_id == 1, low, jnp.zeros_like(high)))
        against = None
        for j, w_ref in enumerate((wq_ref, wk_ref, wv_ref)):
            at = slice(j * 128, (j + 1) * 128)
            part = product[:, at]
            acc_ref[:, at] = (part * gain + shift * tokens[:, at]).astype(BF16)
            weights = w_ref[...]
            scaled = part * weights.astype(F32)
            shifted = dot_nt(terms[:, at], weights)
            against = scaled if against is None else against + scaled
            shifts = shifted if j == 0 else shifts + shifted
        new = jnp.concatenate(
            [jnp.sum(shifts, axis=0, keepdims=True), jnp.sum(against.T, axis=0, keepdims=True)], axis=0
        )

        @pl.when(pl.program_id(0) == 0)
        def _():
            sum_ref[0:2, :] = new

        @pl.when(pl.program_id(0) > 0)
        def _():
            sum_ref[0:2, :] += new

        store_parts(s_ref, acc_ref, r, keep_ref, send_ref)


def attn_bwd(
    order, start, count, prob, inverse, grad_t, out_t, queries, keys, values, cos_t, sin_t, a_one,
    mod, gain, qkv_weight, old, block, blocks,
):
    length = keys.shape[0]
    width = a_one.shape[1]
    hw = width // 2
    wspec = lambda j: pl.BlockSpec((width, 128), lambda p, i, s: (0, (2 * j + s[0]) * (hw // 128) + p + start))
    blk = BWD_BLK
    r = width // 16
    col = pl.BlockSpec((length, 128), lambda p, i, s: (0, p + start))
    rowt = pl.BlockSpec((128, blk), lambda p, i, s: (p + start, i))
    out = pl.BlockSpec((2, 4, r, 384), lambda p, i, s: (0, 0, 0, p + block))
    args = [prob, inverse, grad_t, out_t, queries, keys, values, cos_t, sin_t, a_one, mod, gain, qkv_weight, qkv_weight, qkv_weight]
    aliases = {}
    after = []
    if old is not None:
        aliases = {1 + len(args) + j: 2 + j for j in range(2)}
        after = list(old)
    return order.call(
        functools.partial(attn_bwd_body, r), args, (count, length // blk),
        [
            pl.BlockSpec((2, length, blk), lambda p, i, s: (p + start, 0, i)),
            pl.BlockSpec((1, 8, blk), lambda p, i, s: (p + start, 0, i)),
            rowt, rowt,
            pl.BlockSpec((blk, 128), lambda p, i, s: (i, p + start)),
            col, col, whole(cos_t.shape), whole(cos_t.shape), whole(a_one.shape),
            whole(mod.shape), whole(gain.shape), wspec(0), wspec(1), wspec(2),
        ],
        [pl.BlockSpec((length, 384), lambda p, i, s: (0, p)), whole((8, width))] + [out] * 2,
        [sds((length, 384 * count), BF16), sds((8, width), F32)] + [sds((2, 4, r, 384 * blocks), BF16)] * 2,
        scratch=[
            pltpu.VMEM((2, length, 128), BF16),
            pltpu.VMEM((128, length), BF16),
            pltpu.VMEM((length, 128), F32),
            pltpu.VMEM((length, 128), F32),
            pltpu.VMEM((width, 384), BF16),
        ],
        mb=36, us=8.0 * count, aliases=aliases, after=after, name="attn_bwd",
    )


def mix_body(s_ref, own_ref, got_ref, mid_ref, mod_ref, bias_ref, out_ref):
    width = mid_ref.shape[1]
    branch = own_ref[...] + got_ref[...].astype(F32) + bias_ref[...].astype(F32)[None, :]
    out_ref[...] = (mid_ref[...] + mod_ref[0:1, 5 * width : 6 * width] * branch).astype(BF16)


def mix_call(order, own, got, mid, mod, bias):
    span, width = mid.shape
    blk = 256
    row = pl.BlockSpec((blk, width), lambda i, s: (i, 0))
    return order.call(
        mix_body, [own, got, mid, mod, bias], (span // blk,),
        [row] * 3 + [whole(mod.shape), whole(bias.shape)],
        [row], [sds((span, width), BF16)], mb=12, us=2.5, name="mix",
    )[0]


def post_body(s_ref, att_ref, oth_ref, wm_ref, wo_ref, tok_ref, mod_ref, gain_ref, mid_ref, br_ref, n2_ref):
    width = tok_ref.shape[1]
    branch = dot_tn(att_ref[...], wm_ref[...]) + dot_tn(oth_ref[...], wo_ref[...])
    br_ref[...] = branch
    middle = tok_ref[...].astype(F32) + mod_ref[0:1, 2 * width : 3 * width] * branch
    mid_ref[...] = middle
    a_two, _ = layer_stats(middle)
    scale = mod_ref[0:1, 4 * width : 5 * width]
    n2_ref[...] = (
        a_two * (gain_ref[...].astype(F32)[None, :] * (1.0 + scale)) + mod_ref[0:1, 3 * width : 4 * width]
    ).astype(BF16)


def post_call(order, att_t, att_o, out_weight, tok, mod, gain):
    span, width = tok.shape
    hw = width // 2
    blk = 512
    n = span // blk
    row = pl.BlockSpec((blk, width), lambda i, s: (i, 0))
    return order.call(
        post_body, [att_t, att_o, out_weight, out_weight, tok, mod, gain], (n,),
        [
            pl.BlockSpec((hw, blk), lambda i, s: (0, i)),
            pl.BlockSpec((hw, blk), lambda i, s: (0, i + n)),
            pl.BlockSpec((hw, width), lambda i, s: (s[0], 0)),
            pl.BlockSpec((hw, width), lambda i, s: (1 - s[0], 0)),
            row, whole(mod.shape), whole(gain.shape),
        ],
        [row, row, row],
        [sds((span, width), F32), sds((span, width), F32), sds((span, width), BF16)],
        mb=12, us=3, name="post",
    )


def mlp_body(
    s_ref, n2a_ref, n2b_ref, wa_ref, wb_ref, mod_ref, w1_ref, b1_ref, w2_ref,
    hid_ref, pre_ref, b1g_ref, b2g_ref,
):
    step = pl.program_id(0)
    first = step < pl.num_programs(0) // 2
    width = n2a_ref.shape[1]
    x = jnp.where(first, n2a_ref[...], n2b_ref[...])
    wtd = jnp.where(first, wa_ref[...], wb_ref[...]).astype(F32)
    g_mlp = (wtd * mod_ref[0:1, 5 * width : 6 * width]).astype(BF16)
    bias = b1_ref[...].astype(F32)[None, :]
    hf = w1_ref.shape[1]
    bias = jnp.where(s_ref[0] == 0, bias[:, :hf], bias[:, hf:])
    c0 = 0.7978845608028654
    c1 = c0 * 0.044715
    parts = []
    for at in range(0, hf, MLP_COLS):
        cols = slice(at, at + MLP_COLS)
        v = dot(x, w1_ref[:, cols]) + bias[:, cols]
        gh = dot_nt(g_mlp, w2_ref[cols, :])
        v2 = v * v
        th = jnp.tanh(v * (c0 + c1 * v2))
        up = 0.5 + 0.5 * th
        hid_ref[:, cols] = (v * up).astype(BF16)
        slope = up + v * (0.5 - 0.5 * (th * th)) * (c0 + 3.0 * c1 * v2)
        pre = (gh * slope).astype(BF16)
        pre_ref[:, cols] = pre
        parts.append(jnp.sum(pre.astype(F32), axis=0, keepdims=True))
    b1_part = jnp.concatenate(parts, axis=1)
    b2_part = jnp.sum(g_mlp.astype(F32), axis=0, keepdims=True)

    @pl.when(step == 0)
    def _():
        b1g_ref[...] = b1_part
        b2g_ref[...] = b2_part

    @pl.when(step > 0)
    def _():
        b1g_ref[...] += b1_part
        b2g_ref[...] += b2_part


def halves(blk, width, n):
    return [
        pl.BlockSpec((blk, width), lambda i, s: (jnp.minimum(i, n - 1), 0)),
        pl.BlockSpec((blk, width), lambda i, s: (jnp.maximum(i - n, 0), 0)),
    ]


def mlp_call(order, n2a, n2b, wa, wb, mod, w1, b1, w2):
    span, width = n2a.shape
    hf = w1.shape[1] // 2
    blk = 512
    n = span // blk
    row = lambda w: pl.BlockSpec((blk, w), lambda i, s: (i, 0))
    return order.call(
        mlp_body, [n2a, n2b, wa, wb, mod, w1, b1, w2], (2 * n,),
        halves(blk, width, n) + halves(blk, width, n)
        + [
            whole(mod.shape),
            pl.BlockSpec((width, hf), lambda i, s: (0, s[0])),
            whole(b1.shape),
            pl.BlockSpec((hf, width), lambda i, s: (s[0], 0)),
        ],
        [row(hf), row(hf), whole((1, hf)), whole((1, width))],
        [sds((2 * span, hf), BF16), sds((2 * span, hf), BF16),
         sds((1, hf), F32), sds((1, width), F32)],
        mb=24, us=9.6, name="mlp",
    )


def store_parts(s_ref, acc_ref, r, keep_ref, send_ref):
    for i in range(8):
        rest = sum(((i >> (2 - j)) & 1) * s_ref[6 + j] for j in range(3))
        for ref, bit in ((keep_ref, s_ref[1]), (send_ref, 1 - s_ref[1])):
            at = pl.ds(pl.multiple_of((rest + bit * s_ref[5]) * r, 16), r)
            ref[i // 4, i % 4] = acc_ref[at, :]


def wgrad_body(r, s_ref, la_ref, lb_ref, g_ref, keep_ref, send_ref, acc_ref):
    span = la_ref.shape[0]
    acc_ref[...] = (dot_tn(la_ref[...], g_ref[:span]) + dot_tn(lb_ref[...], g_ref[span:])).astype(BF16)
    store_parts(s_ref, acc_ref, r, keep_ref, send_ref)


def wgrad_call(order, left_a, left_b, right, blk):
    rows, cols = left_a.shape[1], right.shape[1]
    length = right.shape[0]
    r = rows // 16
    out = pl.BlockSpec((2, 4, r, blk), lambda i, s: (0, 0, 0, i))
    return order.call(
        functools.partial(wgrad_body, r), [left_a, left_b, right], (cols // blk,),
        [whole(left_a.shape), whole(left_b.shape), pl.BlockSpec((length, blk), lambda i, s: (0, i))],
        [out] * 2, [sds((2, 4, r, cols), BF16)] * 2,
        scratch=[pltpu.VMEM((rows, blk), BF16)], mb=16, us=4.2, name="wgrad_fc1",
    )


def wgrad2_body(
    r, s_ref, lm_ref, lo_ref, wa_ref, wb_ref, mod_ref, w2_ref, bias_ref, keep_ref, send_ref, gate_ref, acc_ref
):
    step, n = pl.program_id(0), pl.num_programs(0)
    mine = lax.div(step, n // 2) == s_ref[0]
    span, half = wa_ref.shape
    width = 2 * half
    here = pl.ds(pl.multiple_of(s_ref[0] * half, 128), half)
    own, oth = wa_ref[...], wb_ref[...]

    @pl.when(mine)
    def _():
        acc_ref[...] = dot_tn(lm_ref[:span], own) + dot_tn(lm_ref[span:], oth)

    @pl.when(jnp.logical_not(mine))
    def _():
        acc_ref[...] = dot_tn(lo_ref[:span], oth) + dot_tn(lo_ref[span:], own)

    part = jnp.sum(acc_ref[...] * w2_ref[...].astype(F32), axis=0, keepdims=True)

    @pl.when(step == 0)
    def _():
        tokens = jnp.sum(own.astype(F32), axis=0, keepdims=True) + jnp.sum(oth.astype(F32), axis=0, keepdims=True)
        bias = bias_ref[...].astype(F32)[None, :]
        gate_ref[...] = part + tokens * jnp.where(s_ref[0] == 0, bias[:, :half], bias[:, half:])

    @pl.when(step > 0)
    def _():
        gate_ref[...] += part

    gate = mod_ref[0:1, pl.ds(pl.multiple_of(5 * width + s_ref[0] * half, 128), half)]
    za, zb = lax.div(step, 2), lax.rem(step, 2)
    slot = jnp.where(s_ref[0] == 0, zb * 2 + za, za * 2 + zb)
    for other in range(2):
        for ref, bit in ((keep_ref, s_ref[1]), (send_ref, 1 - s_ref[1])):
            at = pl.ds(pl.multiple_of((other * s_ref[6] + bit * s_ref[5]) * r, 16), r)
            ref[other, slot] = (acc_ref[at, :] * gate).astype(BF16)


def wgrad2_call(order, hidden, hidden_o, wa, wb, mod, w2, bias):
    length, hf = hidden.shape
    span, width = wa.shape
    hw = width // 2
    r = hf // 8
    left = lambda first: pl.BlockSpec((length, 4 * r), lambda i, s: (0, jnp.clip(i - first(s[0]), 0, 1)))
    cols = pl.BlockSpec((span, hw), lambda i, s: (0, s[0]))
    return order.call(
        functools.partial(wgrad2_body, r), [hidden, hidden_o, wa, wb, mod, w2, bias], (4,),
        [left(lambda c: 2 * c), left(lambda c: 2 - 2 * c), cols, cols, whole(mod.shape), pl.BlockSpec((4 * r, hw), lambda i, s: (i, s[0])), whole(bias.shape)],
        [whole((2, 4, r, hw))] * 2 + [whole((1, hw))], [sds((2, 4, r, hw), BF16)] * 2 + [sds((1, hw), F32)],
        scratch=[pltpu.VMEM((4 * r, hw), F32)], mb=16, us=4.5, name="wgrad_fc2",
    )


def fold_body(s_ref, ka, ra, ks, rs, away_ref, stay_ref):
    away_ref[...] = ka[0] + ra[0]
    stay_ref[...] = ks[0] + rs[0]


def fold_call(order, step, keep, got):
    _, count, r, n = keep.shape
    blk = 768 if n % 768 == 0 else 384
    away = pl.BlockSpec((1, count, r, blk), lambda i, s: (1 - s[step], 0, 0, i))
    stay = pl.BlockSpec((1, count, r, blk), lambda i, s: (s[step], 0, 0, i))
    out = pl.BlockSpec((count, r, blk), lambda i, s: (0, 0, i))
    return order.call(
        fold_body, [keep, got, keep, got], (n // blk,), [away, away, stay, stay], [out] * 2,
        [sds((count, r, n), BF16)] * 2, mb=8, us=1.2, name="fold",
    )


def join_ff_body(s_ref, ka_ref, ga_ref, ks_ref, gs_ref, away_in, stay_in, away_ref, stay_ref):
    r = away_in.shape[1]
    width = ka_ref.shape[3]
    for out, one, k_ref, g_ref in ((away_ref, away_in, ka_ref, ga_ref), (stay_ref, stay_in, ks_ref, gs_ref)):
        out[:, :r] = one[...]
        two = k_ref[0] + g_ref[0]
        for q in range(two.shape[1] // r):
            out[:, r:, q * width : (q + 1) * width] = two[:, q * r : (q + 1) * r]


def join_ff_call(order, step, one, two):
    keep, got = two
    away_in, stay_in = one
    specs = []
    for away in (True, False):
        pick = (lambda i, s: (1 - s[step], 0, 0, 0)) if away else (lambda i, s: (s[step], 0, 0, 0))
        specs += [pl.BlockSpec((1,) + keep.shape[1:], pick)] * 2
    count, r, n = away_in.shape
    shape = (count, 2 * r, n)
    return order.call(
        join_ff_body, [keep, got, keep, got, away_in, stay_in], (1,),
        specs + [whole(away_in.shape)] * 2, [whole(shape)] * 2, [sds(shape, BF16)] * 2, mb=12, us=1.2, name="fold_ff",
    )


def relay(step, mine, keep, got):
    sources, rest = 2 ** (step - 2), 2 ** (4 - step)
    stay, away = [], []
    for read in (keep, got):
        for src in range(sources):
            both = [[read(src * 2 * rest + bit * rest + k) for k in range(rest)] for bit in range(2)]
            for k in range(rest):
                stay.append(jnp.where(mine == 0, both[0][k], both[1][k]))
                away.append(jnp.where(mine == 0, both[1][k], both[0][k]))
    return stay, away


def paired(packets):
    return [jnp.concatenate(packets[q : q + 2], axis=0).astype(BF16) for q in range(0, 8, 2)]


def single(pair):
    pairs = [pair(q).astype(F32) for q in range(4)]
    return lambda slot: pairs[slot // 2][(slot % 2) * 8 : (slot % 2) * 8 + 8]


def fold_last_body(s_ref, keep_ref, got_ref, sk_ref, sg_ref, away_ref, stay_ref, small_ref):
    mine = s_ref[2]
    r = keep_ref.shape[2]
    away_ref[:, :r] = keep_ref[1 - mine] + got_ref[1 - mine]
    stay_ref[...] = keep_ref[mine] + got_ref[mine]
    stay, away = relay(2, mine, lambda k: sk_ref[k], lambda k: sg_ref[k])
    for k in range(8):
        small_ref[k] = stay[k]
    for q, pair in enumerate(paired(away)):
        away_ref[q, r : r + 16] = pair


def fold_last_call(order, keep, got, small_keep, small_got):
    _, count, r, n = keep.shape
    args = [keep, got, small_keep, small_got]
    shapes = [((count, r + 16, n), BF16), ((count, r, n), BF16), (small_keep.shape, F32)]
    return order.call(
        fold_last_body, args, (1,), [whole(a.shape) for a in args], [whole(x) for x, _ in shapes],
        [sds(*x) for x in shapes], mb=14, us=1.2, name="fold_last",
    )


def fold_att_body(s_ref, k1_ref, g1_ref, k2_ref, g2_ref, sk_ref, away_ref, stay_ref, small_ref):
    mine = s_ref[3]
    count, r, n = k1_ref.shape[1:]
    for out, at in ((away_ref, 1 - mine), (stay_ref, mine)):
        for j in range(count):
            out[j * r : (j + 1) * r, :n] = k1_ref[at, j] + g1_ref[at, j]
            out[j * r : (j + 1) * r, n:] = k2_ref[at, j] + g2_ref[at * count + j, :r]
    got = single(lambda q: g2_ref[q, r : r + 16])
    stay, away = relay(3, mine, lambda k: sk_ref[k], got)
    for k in range(8):
        small_ref[k] = stay[k]
    w = sk_ref.shape[2]
    for q, pair in enumerate(paired(away)):
        away_ref[count * r :, q * w : (q + 1) * w] = pair


def fold_att_call(order, one, two, got, small_keep):
    _, count, r, n = one[0].shape
    full = n + two.shape[3]
    args = [*one, two, got, small_keep]
    shapes = [((count * r + 16, full), BF16), ((count * r, full), BF16), (small_keep.shape, F32)]
    return order.call(
        fold_att_body, args, (1,), [whole(a.shape) for a in args], [whole(x) for x, _ in shapes],
        [sds(*x) for x in shapes], mb=14, us=1.2, name="fold_att",
    )


def fold_end_body(s_ref, keep_ref, got_ref, sk_ref, away_ref, stay_ref, small_ref):
    mine = s_ref[4]
    r = stay_ref.shape[0]
    for out, at in ((away_ref, 1 - mine), (stay_ref, mine)):
        rows = pl.ds(pl.multiple_of(at * r, 16), r)
        out[:r] = keep_ref[rows] + got_ref[rows]
    w = sk_ref.shape[2]
    got = single(lambda q: got_ref[2 * r :, q * w : (q + 1) * w])
    stay, away = relay(4, mine, lambda k: sk_ref[k], got)
    for k in range(8):
        small_ref[k] = stay[k]
    for q, pair in enumerate(paired(away)):
        away_ref[r:, q * w : (q + 1) * w] = pair


def fold_end_call(order, keep, got, small_keep):
    r, n = keep.shape[0] // 2, keep.shape[1]
    args = [keep, got, small_keep]
    shapes = [((r + 16, n), BF16), ((r, n), BF16), (small_keep.shape, F32)]
    return order.call(
        fold_end_body, args, (1,), [whole(a.shape) for a in args], [whole(x) for x, _ in shapes],
        [sds(*x) for x in shapes], mb=14, us=1.2, name="fold_end",
    )


def add_body(s_ref, a_ref, b_ref, out_ref):
    out_ref[...] = a_ref[...] + b_ref[: out_ref.shape[0]]


def add_call(order, a, b):
    return order.call(
        add_body, [a, b], (1,), [whole(a.shape), whole(b.shape)], [whole(a.shape)], [sds(a.shape, BF16)], mb=8, us=1.0, name="add"
    )[0]


def place_ff_body(s_ref, mine_ref, other_ref, fc1_ref, fc2_ref):
    core = s_ref[0]
    r, n = fc1_ref.shape[0], mine_ref.shape[1]
    width = fc2_ref.shape[1] // 2
    for ref, at in ((mine_ref, core), (other_ref, 1 - core)):
        fc1_ref[:, pl.ds(pl.multiple_of(at * n, 128), n)] = ref[:r].astype(F32)
        cols = pl.ds(pl.multiple_of(at * width, 128), width)
        for q in range(n // width):
            fc2_ref[q * r : (q + 1) * r, cols] = ref[r:, q * width : (q + 1) * width].astype(F32)


def place_ff_call(order, mine, other, hw):
    r, n = mine.shape[0] // 2, mine.shape[1]
    shapes = [(r, 2 * n), (r * (n // hw), 2 * hw)]
    return order.call(
        place_ff_body, [mine, other], (1,), [whole(mine.shape)] * 2, [whole(x) for x in shapes],
        [sds(x, F32) for x in shapes], mb=8, us=1.0, name="place_ff",
    )


def place_att_body(s_ref, mine_ref, other_ref, out_ref, qkv_ref):
    core = s_ref[0]
    width = out_ref.shape[1]
    hw = width // 2
    for ref, at in ((mine_ref, core), (other_ref, 1 - core)):
        out_ref[:, pl.ds(pl.multiple_of(at * hw, 128), hw)] = ref[:, :hw].astype(F32)
        for p in range(hw // 128):
            for j in range(3):
                to = pl.ds(pl.multiple_of(j * width + at * hw + p * 128, 128), 128)
                src = hw + p * 384 + j * 128
                qkv_ref[:, to] = ref[:, src : src + 128].astype(F32)


def place_att_call(order, mine, other, width):
    r = mine.shape[0]
    shapes = [(r, width), (r, 3 * width)]
    return order.call(
        place_att_body, [mine, other], (1,), [whole(mine.shape)] * 2, [whole(x) for x in shapes],
        [sds(x, F32) for x in shapes], mb=8, us=1.0, name="place_att",
    )


def pack_body(
    s_ref, s1a_ref, s1b_ref, s2_ref, gate_ref, b1_ref, b2_ref, g1_ref, g2_ref, mod_ref, cond_ref, out_ref
):
    width = s2_ref.shape[1]
    h = width // 2
    core = s_ref[0]
    mine = jnp.where(core == 0, 1.0, 0.0)
    gain_one, gain_two = g1_ref[...].astype(F32)[None, :], g2_ref[...].astype(F32)[None, :]
    scale_one = 1.0 + mod_ref[0:1, width : 2 * width]
    scale_two = 1.0 + mod_ref[0:1, 4 * width : 5 * width]
    second_one, second_two = s1a_ref[1:2, :] + s1b_ref[1:2, :], s2_ref[1:2, :]
    gate = jnp.concatenate([gate_ref[...] * mine, gate_ref[...] * (1.0 - mine)], axis=1)
    flat = jnp.concatenate(
        [
            s1a_ref[0:1, :] + s1b_ref[0:1, :], second_one * gain_one, s2_ref[2:3, :],
            s2_ref[0:1, :], second_two * gain_two, gate,
        ],
        axis=1,
    )
    b1 = jnp.concatenate([b1_ref[...] * mine, b1_ref[...] * (1.0 - mine)], axis=1)
    sources = (flat, b1, second_one * scale_one, second_two * scale_two, 0.5 * b2_ref[...])
    out_ref[...] = jnp.zeros_like(out_ref)
    cond = 0.5 * cond_ref[...].astype(F32)
    ndp = out_ref.shape[0] - 2
    for d in range(ndp):
        for j, source in enumerate(sources):
            n = source.shape[1] // ndp
            out_ref[d, j : j + 1, 0:n] = source[:, d * n : (d + 1) * n]
        out_ref[d, 5:6, 0:128] = cond
    for j in range(12):
        out_ref[ndp + j // 8, j % 8 : j % 8 + 1, :] = flat[:, j * h : (j + 1) * h]


def pack_call(order, *args):
    h = args[2].shape[1] // 2
    shape = (18, 8, h)
    return order.call(
        pack_body, list(args), (1,), [whole(a.shape) for a in args], [whole(shape)], [sds(shape, F32)],
        mb=8, us=1.0, name="pack",
    )[0]


def deal_body(s_ref, a_ref, b_ref, ada_ref, cg_ref, keep_ref, send_ref, acc_ref):
    acc_ref[...] = a_ref[...] + b_ref[...]
    for i in range(8):
        rest = sum(((i >> (2 - j)) & 1) * s_ref[6 + j] for j in range(3))
        keep_ref[i] = acc_ref[rest + s_ref[1] * s_ref[5]]
        send_ref[i] = acc_ref[rest + (1 - s_ref[1]) * s_ref[5]]
    flat = jnp.concatenate([acc_ref[16 + j // 8, j % 8 : j % 8 + 1, :] for j in range(12)], axis=1)
    high = flat.astype(BF16)
    rest = flat - high.astype(F32)
    mid = rest.astype(BF16)
    low = (rest - mid.astype(F32)).astype(BF16)
    row_id = lax.broadcasted_iota(jnp.int32, (16, flat.shape[1]), 0)
    zero = jnp.zeros_like(high)
    terms = jnp.where(row_id == 0, high, jnp.where(row_id == 1, mid, jnp.where(row_id == 2, low, zero)))
    cg_ref[...] = jnp.sum(dot_nt(terms, ada_ref[...]), axis=0, keepdims=True)


def deal_call(order, mine, got, ada):
    shape = (8,) + mine.shape[1:]
    return order.call(
        deal_body, [mine, got, ada], (1,), [whole(mine.shape), whole(mine.shape), whole(ada.shape)],
        [whole((1, ada.shape[0])), whole(shape), whole(shape)],
        [sds((1, ada.shape[0]), F32), sds(shape, F32), sds(shape, F32)],
        scratch=[pltpu.VMEM(mine.shape, F32)], mb=8, us=1.0, name="deal",
    )


def last_body(s_ref, got_ref, sk_ref, ada_ref, adab_ref, b1_ref, g1_ref, g2_ref, b2_ref):
    r, w = got_ref.shape[0] - 16, sk_ref.shape[2]
    got = single(lambda q: got_ref[r:, q * w : (q + 1) * w])
    parts = [sk_ref[k] for k in range(8)] + [got(k) for k in range(8)]
    sums = parts[0]
    for part in parts[1:]:
        sums = sums + part
    cond = jnp.concatenate([part[5:6, 0:128] for part in parts], axis=0)
    grads = jnp.concatenate([part[0:1] for part in parts], axis=0)
    ada = lax.dot_general(
        cond, grads, (((0,), (0,)), ((), ())), precision=lax.Precision.HIGHEST, preferred_element_type=F32
    )
    ada_ref[...] = ada[:, : ada_ref.shape[1]]
    for j, ref in enumerate((adab_ref, b1_ref, g1_ref, g2_ref, b2_ref)):
        ref[...] = sums[j : j + 1, : ref.shape[1]]


def last_call(order, got, small_keep, ndp):
    h = small_keep.shape[2]
    na, nb, nc = 12 * h // ndp, 2 * h // ndp, 8 * h // ndp
    shapes = [(128, na), (1, na), (1, nc), (1, nb), (1, nb), (1, nb)]
    args = [got, small_keep]
    return order.call(
        last_body, args, (1,), [whole(a.shape) for a in args], [whole(x) for x in shapes],
        [sds(x, F32) for x in shapes], mb=8, us=1.0, name="small_last",
    )


def part_body(nt, s_ref, g_ref, w_ref, own_ref, oth_ref):
    step = pl.program_id(0)
    half = pl.num_programs(0) // 2
    part = dot_nt(g_ref[...], w_ref[...]) if nt else dot(g_ref[...], w_ref[...])

    @pl.when(step < half)
    def _():
        oth_ref[...] = part.astype(BF16)

    @pl.when(step >= half)
    def _():
        own_ref[...] = part


def part_call(order, nt, g, w):
    length, hf = g.shape
    width = w.shape[0] if nt else w.shape[1]
    blk = 512
    n = length // 2 // blk
    wspec = (
        pl.BlockSpec((width, hf), lambda i, s: (0, s[0]))
        if nt
        else pl.BlockSpec((hf, width), lambda i, s: (s[0], 0))
    )
    return order.call(
        functools.partial(part_body, nt), [g, w], (2 * n,),
        [pl.BlockSpec((blk, hf), lambda i, s: ((i + n) % (2 * n), 0)), wspec],
        [
            pl.BlockSpec((blk, width), lambda i, s: (jnp.maximum(i - n, 0), 0)),
            pl.BlockSpec((blk, width), lambda i, s: (jnp.minimum(i, n - 1), 0)),
        ],
        [sds((length // 2, width), F32), sds((length // 2, width), BF16)],
        mb=12, us=4.2, name="part",
    )


def norm2_body(s_ref, own_ref, got_ref, mid_ref, br_ref, wtd_ref, mod_ref, gain_ref, gmid_ref, gatt_ref, sum_ref):
    width = mid_ref.shape[1]
    g = own_ref[...] + got_ref[...].astype(F32)
    a_two, inv = layer_stats(mid_ref[...])
    ga = g * (gain_ref[...].astype(F32)[None, :] * (1.0 + mod_ref[0:1, 4 * width : 5 * width]))
    gaa = ga * a_two
    g_mid = wtd_ref[...].astype(F32) + inv * (
        ga - jnp.mean(ga, -1, keepdims=True) - a_two * jnp.mean(gaa, -1, keepdims=True)
    )
    gmid_ref[...] = g_mid
    gatt_ref[...] = (g_mid * mod_ref[0:1, 2 * width : 3 * width]).astype(BF16)
    sums = jnp.concatenate(
        [
            jnp.sum(g, axis=0, keepdims=True),
            jnp.sum(g * a_two, axis=0, keepdims=True),
            jnp.sum(g_mid * br_ref[...], axis=0, keepdims=True),
        ],
        axis=0,
    )

    @pl.when(pl.program_id(0) == 0)
    def _():
        sum_ref[...] = jnp.zeros_like(sum_ref)

    sum_ref[0:3, :] += sums


def norm2_call(order, own, got, mid, br, wtd, mod, gain):
    span, width = mid.shape
    blk = 512
    row = pl.BlockSpec((blk, width), lambda i, s: (i, 0))
    return order.call(
        norm2_body, [own, got, mid, br, wtd, mod, gain], (span // blk,),
        [row] * 5 + [whole(mod.shape), whole(gain.shape)],
        [row, row, whole((8, width))],
        [sds((span, width), F32), sds((span, width), BF16), sds((8, width), F32)],
        mb=12, us=3, name="norm2",
    )


def oproj_body(r, s_ref, w_ref, ga_ref, gb_ref, am_ref, ao_ref, gt_ref, keep_ref, send_ref, acc_ref):
    span = ga_ref.shape[0]
    half = am_ref.shape[0]
    core = s_ref[0]
    w = w_ref[...]
    gt_ref[:, :span] = dot_nt(w, ga_ref[...]).astype(BF16)
    gt_ref[:, span:] = dot_nt(w, gb_ref[...]).astype(BF16)
    cols = pl.ds(pl.multiple_of(core * half, 128), half)
    gac, gbc = ga_ref[:, cols], gb_ref[:, cols]
    mine = dot(am_ref[:, :span], gac) + dot(am_ref[:, span:], gbc)
    other = dot(ao_ref[:, span:], gac) + dot(ao_ref[:, :span], gbc)
    acc_ref[pl.ds(pl.multiple_of(core * half, 16), half), :] = mine.astype(BF16)
    acc_ref[pl.ds(pl.multiple_of((1 - core) * half, 16), half), :] = other.astype(BF16)
    store_parts(s_ref, acc_ref, r, keep_ref, send_ref)


def oproj_call(order, blocks, out_weight, ga, gb, att_t, att_o):
    span, width = ga.shape
    hw = width // 2
    r = width // 16
    out = pl.BlockSpec((2, 4, r, hw), lambda i, s: (0, 0, 0, 0))
    return order.call(
        functools.partial(oproj_body, r), [out_weight, ga, gb, att_t, att_o], (1,),
        [pl.BlockSpec((hw, width), lambda i, s: (s[0], 0)), whole(ga.shape), whole(ga.shape),
         whole(att_t.shape), whole(att_t.shape)],
        [whole((hw, 2 * span))] + [out] * 2,
        [sds((hw, 2 * span), BF16)] + [sds((2, 4, r, blocks * hw), BF16)] * 2,
        scratch=[pltpu.VMEM((width, hw), BF16)], mb=8, us=3, name="oproj",
    )


def norm1_body(s_ref, own_ref, got_ref, tok_ref, gmid_ref, mod_ref, gain_ref, out_ref):
    width = tok_ref.shape[1]
    g = own_ref[...] + got_ref[...].astype(F32)
    a_one, inv = layer_stats(tok_ref[...].astype(F32))
    ga = g * (gain_ref[...].astype(F32)[None, :] * (1.0 + mod_ref[0:1, width : 2 * width]))
    gaa = ga * a_one
    out_ref[...] = (
        gmid_ref[...]
        + inv * (ga - jnp.mean(ga, -1, keepdims=True) - a_one * jnp.mean(gaa, -1, keepdims=True))
    ).astype(BF16)


def norm1_call(order, own, got, tok, gmid, mod, gain):
    span, width = tok.shape
    blk = 256
    row = pl.BlockSpec((blk, width), lambda i, s: (i, 0))
    return order.call(
        norm1_body, [own, got, tok, gmid, mod, gain], (span // blk,),
        [row] * 4 + [whole(mod.shape), whole(gain.shape)], [row], [sds((span, width), BF16)],
        mb=12, us=3, name="norm1",
    )[0]


def dgrad_body(np_, s_ref, *refs):
    gs, (wq_ref, wk_ref, wv_ref), out_ref = refs[:np_], refs[np_ : np_ + 3], refs[np_ + 3]
    total = None
    for j, w_ref in enumerate((wq_ref, wk_ref, wv_ref)):
        left = jnp.concatenate(
            [g[:, at + j * 128 : at + (j + 1) * 128] for g in gs for at in range(0, g.shape[1], 384)], axis=1
        )
        part = dot_nt(left, w_ref[...])
        total = part if total is None else total + part
    out_ref[...] = total.astype(out_ref.dtype)


def dgrad_call(order, gs, qkv_weight, half):
    span = gs[0].shape[0] // 2
    width = qkv_weight.shape[0]
    hw = width // 2
    wspec = lambda j: pl.BlockSpec((width, hw), lambda i, s: (0, 2 * j + s[0]))
    return order.call(
        functools.partial(dgrad_body, len(gs)), [*gs, qkv_weight, qkv_weight, qkv_weight], (1,),
        [pl.BlockSpec((span, g.shape[1]), lambda i, s: (half, 0)) for g in gs] + [wspec(0), wspec(1), wspec(2)],
        [whole((span, width))], [sds((span, width), BF16 if half else F32)], mb=12, us=2.0, name="dgrad",
    )[0]


class Grid:
    ORDERS = ((1, 2, 4, 8), (2, 1, 8, 4))

    def __init__(self, ndp):
        self.index = lax.axis_index("dp")
        core = lax.axis_index("ctx")
        self.flip = lambda mask: [(i, i ^ mask) for i in range(ndp)]
        masks = [jnp.where(core == 0, a, b) for a, b in zip(*self.ORDERS)]
        bits = [jnp.where((self.index & m) > 0, 1, 0) for m in masks]
        self.place = jnp.stack([core, *bits, *masks, self.index // 4, self.index]).astype(jnp.int32)
        self.pairs = [
            [(2 * i + c, 2 * (i ^ self.ORDERS[c][step]) + c) for i in range(ndp) for c in range(2)] for step in range(4)
        ]


class Job:
    def __init__(self, pairs):
        self.pairs, self.step = pairs, 0

    def start(self, keep, send):
        self.keep = keep
        self.got = lax.ppermute(send, ("dp", "ctx"), self.pairs[self.step])
        self.step += 1

    def parts(self):
        shape = self.keep.shape
        if self.step > 1:
            shape = (2, shape[0] // 2) + shape[1:]
        return self.keep.reshape(shape), self.got.reshape(shape)

    def fold(self, order):
        away, stay = self.split(order)
        self.start(stay, away)

    def split(self, order):
        return fold_call(order, self.step + 1, *self.parts())

    def last(self):
        return self.keep[0], self.got[0]


def join(order, fold, one, two):
    job = Job(two.pairs)
    job.step = two.step
    away, stay = fold(order, job.step + 1, one if isinstance(one, tuple) else one.parts(), two.parts())
    job.start(stay, away)
    return job


def local_pair(
    tokens_in, cond_vec, positions, absorbed, cotangent, norm1_gain, qkv_weight, out_weight,
    norm2_gain, fc1_weight, fc1_bias, fc2_weight, fc2_bias, ada_weight, ada_bias, *, ndp,
):
    _, span, width = tokens_in.shape
    hw = width // 2
    grid = Grid(ndp)
    order = Order(grid.place)
    swap = lambda v: lax.ppermute(v, "ctx", [(0, 1), (1, 0)])

    tok = tokens_in[0]
    tok_o = swap(tok)
    pos_o = swap(positions)

    a_one, queries, keys, values, cos_t, sin_t, att_t, prob, inverse, mod, wtd = attend_call(
        order, tok, tok_o, cond_vec, ada_weight, ada_bias, norm1_gain, qkv_weight, positions, pos_o,
        cotangent[0], absorbed,
    )
    wtd_o = swap(wtd)
    att_o = swap(att_t)
    middle, branch, n2 = post_call(order, att_t, att_o, out_weight, hbm(tok), mod, norm2_gain)
    n2_o = swap(n2)
    hidden, g_pre, b1_sum, b2_sum = mlp_call(
        order, n2, n2_o, wtd, wtd_o, mod, fc1_weight, fc1_bias, fc2_weight
    )
    hidden_o = swap(hidden)
    fc1, fc2, rest, last = (Job(grid.pairs) for _ in range(4))
    fc1.start(*wgrad_call(order, n2, n2_o, g_pre, 768))
    pn_own, pn_oth = part_call(order, True, g_pre, fc1_weight)
    pn_got = swap(pn_oth)
    *bufs, gate_sum = wgrad2_call(order, hidden, hidden_o, wtd, wtd_o, mod, fc2_weight, fc2_bias)
    fc2.start(*bufs)
    pm_own, pm_oth = part_call(order, False, hidden, fc2_weight)
    pm_got = swap(pm_oth)
    fc1.fold(order)
    g_mid, g_att, sums2 = norm2_call(order, pn_own, pn_got, middle, branch, wtd, mod, norm2_gain)
    g_att_o = swap(g_att)
    g_attn_t, *bufs = oproj_call(order, 3, out_weight, g_att, g_att_o, att_t, att_o)

    def back(start, count, old, block, blocks):
        return attn_bwd(
            order, start, count, hbm(prob), inverse, g_attn_t, att_t, queries, keys, values, cos_t, sin_t,
            a_one, mod, norm1_gain, qkv_weight, old, block, blocks,
        )

    pairs = hw // 128
    g_a, sums_a, *bufs = back(0, pairs - 1, bufs, 1, pairs)
    rest.start(*bufs)
    fc2.fold(order)
    fc1.fold(order)
    g_b, sums_b, *bufs = back(pairs - 1, 1, None, 0, 1)
    last.start(*bufs)
    mixed = mix_call(order, pm_own, pm_got, middle, mod, fc2_bias)
    fc1_split = fc1.split(order)
    packet = pack_call(
        order, sums_a, sums_b, sums2, gate_sum, b1_sum, b2_sum, norm1_gain, norm2_gain, mod, cond_vec
    )
    packet_o = swap(packet)
    d_got = swap(dgrad_call(order, [g_a, g_b], qkv_weight, 1))
    fc2.fold(order)
    rest.fold(order)
    cond_grad, small_keep, send = deal_call(order, packet, packet_o, ada_weight)
    along = lambda step, v: lax.ppermute(v, ("dp", "ctx"), grid.pairs[step - 1])
    small_got = along(1, send)
    ff = join(order, join_ff_call, tuple(fc1_split), fc2)
    away, last_keep, small_keep = fold_last_call(order, *last.parts(), small_keep, small_got)
    last_got = along(2, away)
    d_own = dgrad_call(order, [g_a, g_b], qkv_weight, 0)
    input_grad = norm1_call(order, d_own, d_got, tok, g_mid, mod, norm1_gain)
    ff_sum = add_call(order, *ff.last())
    ff_other = swap(ff_sum)
    away, keep, small_keep = fold_att_call(
        order, rest.parts(), last_keep.reshape((2, 2) + last_keep.shape[1:]), last_got, small_keep
    )
    got = along(3, away)
    fc1_grad, fc2_grad = place_ff_call(order, ff_sum, ff_other, hw)
    away, keep, small_keep = fold_end_call(order, keep, got, small_keep)
    got = along(4, away)
    att_sum = add_call(order, keep, got)
    att_other = swap(att_sum)
    ada_grad, ada_bias_grad, fc1_bias_grad, norm1_grad, norm2_grad, fc2_bias_grad = last_call(
        order, got, small_keep, ndp
    )
    out_grad, qkv_grad = place_att_call(order, att_sum, att_other, width)
    return (
        mixed[None], input_grad[None], cond_grad, norm1_grad[0], qkv_grad, out_grad, norm2_grad[0],
        fc1_grad, fc1_bias_grad[0], fc2_grad, fc2_bias_grad[0], ada_grad, ada_bias_grad[0],
    )


def layer_norm(stream):
    row_mean = jnp.mean(stream, axis=-1, keepdims=True)
    centred = stream - row_mean
    variance = jnp.mean(centred * centred, axis=-1, keepdims=True)
    return centred * lax.rsqrt(variance + EPS)


def pre_norm(stream, norm_gain, shift_vec, scale_vec):
    return layer_norm(stream) * norm_gain * (1.0 + scale_vec[:, None, :]) + shift_vec[:, None, :]


def gelu_tanh(stream):
    return jax.nn.gelu(stream, approximate=True)


def block_rows(row_count):
    size_now = row_count
    while size_now > 512 and size_now % 2 == 0:
        size_now = size_now // 2
    return size_now


def rotary_tables(positions):
    inv_freq = 10000.0 ** (-jnp.arange(0, HEAD_DIM, 2).astype(jnp.float32) / HEAD_DIM)
    angles = positions.astype(jnp.float32)[..., None] * inv_freq
    cos_table = jnp.concatenate([jnp.cos(angles), jnp.cos(angles)], axis=-1)[..., None, :]
    sin_table = jnp.concatenate([jnp.sin(angles), jnp.sin(angles)], axis=-1)[..., None, :]
    return (cos_table, sin_table)


def rotate_pos(stream, cos_table, sin_table):
    half_dim = stream.shape[-1] // 2
    turned = jnp.concatenate([-stream[..., half_dim:], stream[..., :half_dim]], axis=-1)
    return stream * cos_table + turned * sin_table


def over_blocks(step_fn, fold_state, pieces):
    row_count = pieces[0].shape[1]
    size_now = block_rows(row_count)

    def one_turn(turn_idx, inner_state):
        part_list = tuple(
            (
                lax.dynamic_slice_in_dim(member, turn_idx * size_now, size_now, 1)
                for member in pieces
            )
        )
        return step_fn(inner_state, part_list, turn_idx * size_now)

    return lax.fori_loop(0, row_count // size_now, one_turn, fold_state)


def score_grads(query_blk, key_blk, value_blk, grad_blk, top_blk, total_blk, delta_blk):
    scores = (
        jnp.einsum("sqhd,skhd->sqhk", query_blk, key_blk, preferred_element_type=jnp.float32)
        * SCORE_SCALE
    )
    probability = jnp.exp(scores - top_blk[..., None]) / total_blk[..., None]
    grad_prob = jnp.einsum(
        "sqhd,skhd->sqhk", grad_blk, value_blk, preferred_element_type=jnp.float32
    )
    grad_scores = (probability * (grad_prob - delta_blk[..., None])).astype(jnp.bfloat16)
    return (probability, grad_scores)


def local_any(
    tokens_in,
    cond_vec,
    positions,
    absorbed,
    cotangent,
    norm1_gain,
    qkv_weight,
    out_weight,
    norm2_gain,
    fc1_weight,
    fc1_bias,
    fc2_weight,
    fc2_bias,
    ada_weight,
    ada_bias,
):
    seqs_here, span_len, model_width = tokens_in.shape
    head_shape = (seqs_here, span_len, HEADS, HEAD_DIM)
    stream = tokens_in.astype(jnp.float32)
    modulation = jnp.dot(
        cond_vec, ada_weight, preferred_element_type=jnp.float32
    ) + ada_bias.astype(jnp.float32)
    shift_one, scale_one, gate_one, shift_two, scale_two, gate_two = jnp.split(
        modulation, 6, axis=-1
    )
    gain_one = norm1_gain.astype(jnp.float32)
    gain_two = norm2_gain.astype(jnp.float32)
    normed_f, pull_one = jax.vjp(pre_norm, stream, gain_one, shift_one, scale_one)
    normed_one = normed_f.astype(jnp.bfloat16)
    projected = jnp.dot(normed_one, qkv_weight, preferred_element_type=jnp.float32)
    cos_table, sin_table = rotary_tables(positions)
    turned_pair, pull_rot = jax.vjp(
        lambda query_pre, key_pre: (
            rotate_pos(query_pre, cos_table, sin_table),
            rotate_pos(key_pre, cos_table, sin_table),
        ),
        projected[..., :model_width].reshape(head_shape),
        projected[..., model_width : 2 * model_width].reshape(head_shape),
    )
    queries = turned_pair[0].astype(jnp.bfloat16)
    key_loc = turned_pair[1].astype(jnp.bfloat16).reshape(seqs_here, span_len, model_width)
    value_loc = projected[..., 2 * model_width :].astype(jnp.bfloat16)

    def forward_step(fold_state, part_list, offset):
        run_max, run_sum, run_acc = fold_state
        key_blk = part_list[0].reshape(seqs_here, -1, HEADS, HEAD_DIM)
        value_blk = part_list[1].reshape(seqs_here, -1, HEADS, HEAD_DIM)
        scores = (
            jnp.einsum("sqhd,skhd->sqhk", queries, key_blk, preferred_element_type=jnp.float32)
            * SCORE_SCALE
        )
        new_max = jnp.maximum(run_max, jnp.max(scores, axis=-1))
        raised = jnp.exp(scores - new_max[..., None])
        shrink = jnp.exp(run_max - new_max)
        run_sum = run_sum * shrink + jnp.sum(raised, axis=-1)
        run_acc = run_acc * shrink[..., None] + jnp.einsum(
            "sqhk,skhd->sqhd",
            raised.astype(jnp.bfloat16),
            value_blk,
            preferred_element_type=jnp.float32,
        )
        return (new_max, run_sum, run_acc)

    empty_state = (
        jnp.full((seqs_here, span_len, HEADS), NEG_START, jnp.float32),
        jnp.zeros((seqs_here, span_len, HEADS), jnp.float32),
        jnp.zeros(head_shape, jnp.float32),
    )
    final_max, final_sum, final_acc = over_blocks(
        forward_step,
        empty_state,
        (
            lax.all_gather(key_loc, "ctx", axis=1, tiled=True),
            lax.all_gather(value_loc, "ctx", axis=1, tiled=True),
        ),
    )
    attn_out = final_acc / final_sum[..., None]
    attended = attn_out.reshape(seqs_here, span_len, model_width).astype(jnp.bfloat16)
    branch_att = jnp.dot(attended, out_weight, preferred_element_type=jnp.float32)
    middle = stream + gate_one[:, None, :] * branch_att
    normed_f2, pull_two = jax.vjp(pre_norm, middle, gain_two, shift_two, scale_two)
    normed_two = normed_f2.astype(jnp.bfloat16)
    hidden_pre = jnp.dot(
        normed_two, fc1_weight, preferred_element_type=jnp.float32
    ) + fc1_bias.astype(jnp.float32)
    hidden_f, pull_gelu = jax.vjp(gelu_tanh, hidden_pre)
    hidden = hidden_f.astype(jnp.bfloat16)
    branch_mlp = jnp.dot(hidden, fc2_weight, preferred_element_type=jnp.float32) + fc2_bias.astype(
        jnp.float32
    )
    mixed = (middle + gate_two[:, None, :] * branch_mlp).astype(jnp.bfloat16)
    weighted = cotangent.astype(jnp.float32) * absorbed.astype(jnp.float32)[..., None]
    grad_gate_two = jnp.sum(weighted * branch_mlp, axis=1)
    grad_mlp = (weighted * gate_two[:, None, :]).astype(jnp.bfloat16)
    grad_fc2b = jnp.sum(grad_mlp.astype(jnp.float32), axis=(0, 1))
    grad_fc2 = jnp.einsum("scf,scd->fd", hidden, grad_mlp, preferred_element_type=jnp.float32)
    grad_hidden = jnp.einsum(
        "scd,fd->scf", grad_mlp, fc2_weight, preferred_element_type=jnp.float32
    )
    grad_pre = pull_gelu(grad_hidden)[0].astype(jnp.bfloat16)
    grad_fc1b = jnp.sum(grad_pre.astype(jnp.float32), axis=(0, 1))
    grad_fc1 = jnp.einsum("scd,scf->df", normed_two, grad_pre, preferred_element_type=jnp.float32)
    grad_normed_two = jnp.einsum(
        "scf,df->scd", grad_pre, fc1_weight, preferred_element_type=jnp.float32
    )
    grad_mid_part, grad_gain_two, grad_shift_two, grad_scale_two = pull_two(grad_normed_two)
    grad_middle = weighted + grad_mid_part
    grad_gate_one = jnp.sum(grad_middle * branch_att, axis=1)
    grad_att = (grad_middle * gate_one[:, None, :]).astype(jnp.bfloat16)
    grad_out = jnp.einsum("scd,sce->de", attended, grad_att, preferred_element_type=jnp.float32)
    grad_attended = (
        jnp.einsum("sce,de->scd", grad_att, out_weight, preferred_element_type=jnp.float32)
        .astype(jnp.bfloat16)
        .reshape(head_shape)
    )
    row_delta = jnp.sum(grad_attended.astype(jnp.float32) * attn_out, axis=-1)

    def query_only_step(fold_state, part_list, offset):
        piece_len = part_list[0].shape[1]
        key_blk = part_list[0].reshape(seqs_here, piece_len, HEADS, HEAD_DIM)
        value_blk = part_list[1].reshape(seqs_here, piece_len, HEADS, HEAD_DIM)
        probability, grad_scores = score_grads(
            queries, key_blk, value_blk, grad_attended, final_max, final_sum, row_delta
        )
        return (
            fold_state
            + jnp.einsum(
                "sqhk,skhd->sqhd", grad_scores, key_blk, preferred_element_type=jnp.float32
            )
            * SCORE_SCALE
        )

    start_state = jnp.zeros(head_shape, jnp.float32)
    back_state = over_blocks(
        query_only_step,
        start_state,
        (
            lax.all_gather(key_loc, "ctx", axis=1, tiled=True),
            lax.all_gather(value_loc, "ctx", axis=1, tiled=True),
        ),
    )
    key_heads = key_loc.reshape(head_shape)
    value_heads = value_loc.reshape(head_shape)

    def local_key_step(fold_state, part_list, offset):
        grad_key_loc, grad_value_loc = fold_state
        query_blk = part_list[0].astype(jnp.bfloat16)
        grad_blk = part_list[1].astype(jnp.bfloat16)
        probability, grad_scores = score_grads(
            query_blk, key_heads, value_heads, grad_blk, part_list[2], part_list[3], part_list[4]
        )
        grad_value_loc = grad_value_loc + jnp.einsum(
            "sqhk,sqhd->skhd",
            probability.astype(jnp.bfloat16),
            grad_blk,
            preferred_element_type=jnp.float32,
        )
        grad_key_loc = (
            grad_key_loc
            + jnp.einsum(
                "sqhk,sqhd->skhd", grad_scores, query_blk, preferred_element_type=jnp.float32
            )
            * SCORE_SCALE
        )
        return (grad_key_loc, grad_value_loc)

    key_start = (jnp.zeros(head_shape, jnp.float32), jnp.zeros(head_shape, jnp.float32))
    grad_key_h, grad_value_h = over_blocks(
        local_key_step,
        key_start,
        (
            lax.all_gather(queries.astype(jnp.float32), "ctx", axis=1, tiled=True),
            lax.all_gather(grad_attended.astype(jnp.float32), "ctx", axis=1, tiled=True),
            lax.all_gather(final_max, "ctx", axis=1, tiled=True),
            lax.all_gather(final_sum, "ctx", axis=1, tiled=True),
            lax.all_gather(row_delta, "ctx", axis=1, tiled=True),
        ),
    )
    grad_key_loc = grad_key_h.reshape(seqs_here, span_len, model_width)
    grad_value_loc = grad_value_h.reshape(seqs_here, span_len, model_width)
    grad_query_pre, grad_key_pre = pull_rot((back_state, grad_key_loc.reshape(head_shape)))
    grad_proj = jnp.concatenate(
        [
            grad_query_pre.reshape(seqs_here, span_len, model_width),
            grad_key_pre.reshape(seqs_here, span_len, model_width),
            grad_value_loc,
        ],
        axis=-1,
    ).astype(jnp.bfloat16)
    grad_qkv = jnp.einsum("scd,sce->de", normed_one, grad_proj, preferred_element_type=jnp.float32)
    grad_normed_one = jnp.einsum(
        "sce,de->scd", grad_proj, qkv_weight, preferred_element_type=jnp.float32
    )
    grad_in_part, grad_gain_one, grad_shift_one, grad_scale_one = pull_one(grad_normed_one)
    input_grad = (grad_middle + grad_in_part).astype(jnp.bfloat16)
    partial_mod = jnp.concatenate(
        [
            grad_shift_one,
            grad_scale_one,
            grad_gate_one,
            grad_shift_two,
            grad_scale_two,
            grad_gate_two,
        ],
        axis=-1,
    )
    grad_mod = lax.psum(partial_mod, "ctx")
    cond_grad = jnp.einsum(
        "se,ce->sc",
        grad_mod,
        ada_weight.astype(jnp.float32),
        precision=lax.Precision.HIGHEST,
        preferred_element_type=jnp.float32,
    )
    first_cycle = (lax.axis_index("ctx") == 0).astype(jnp.float32)
    grad_ada = (
        jnp.einsum(
            "sc,se->ce",
            cond_vec.astype(jnp.float32),
            grad_mod,
            precision=lax.Precision.HIGHEST,
            preferred_element_type=jnp.float32,
        )
        * first_cycle
    )
    grad_adab = jnp.sum(grad_mod, axis=0) * first_cycle
    (
        part_g1,
        part_qkv,
        part_out,
        part_g2,
        part_fc1,
        part_fc1b,
        part_fc2,
        part_fc2b,
        part_ada,
        part_adab,
    ) = (
        lax.psum_scatter(grad_gain_one, "dp", scatter_dimension=0, tiled=True),
        lax.psum_scatter(grad_qkv, "dp", scatter_dimension=0, tiled=True),
        lax.psum_scatter(grad_out, "dp", scatter_dimension=0, tiled=True),
        lax.psum_scatter(grad_gain_two, "dp", scatter_dimension=0, tiled=True),
        lax.psum_scatter(grad_fc1, "dp", scatter_dimension=0, tiled=True),
        lax.psum_scatter(grad_fc1b, "dp", scatter_dimension=0, tiled=True),
        lax.psum_scatter(grad_fc2, "dp", scatter_dimension=0, tiled=True),
        lax.psum_scatter(grad_fc2b, "dp", scatter_dimension=0, tiled=True),
        lax.psum_scatter(grad_ada, "dp", scatter_dimension=1, tiled=True),
        lax.psum_scatter(grad_adab, "dp", scatter_dimension=0, tiled=True),
    )
    summed = lax.psum(
        (
            part_g1,
            part_qkv,
            part_out,
            part_g2,
            part_fc1,
            part_fc1b,
            part_fc2,
            part_fc2b,
            part_ada,
            part_adab,
        ),
        "ctx",
    )
    return (mixed, input_grad, cond_grad) + tuple(summed)


def local(*args, ndp, nctx):
    seqs, span, _ = args[0].shape
    if nctx == 2 and seqs == 1 and ndp == 16 and span == 512:
        return local_pair(*args, ndp=ndp)
    return local_any(*args)


def solution(mesh):
    in_specs = (
        P("dp", "ctx", None),
        P("dp", None),
        P("dp", "ctx"),
        P("dp", "ctx"),
        P("dp", "ctx", None),
        P(),
        P(),
        P(),
        P(),
        P(),
        P(),
        P(),
        P(),
        P(),
        P(),
    )
    out_specs = (
        P("dp", "ctx", None),
        P("dp", "ctx", None),
        P("dp", None),
        P("dp"),
        P("dp", None),
        P("dp", None),
        P("dp"),
        P("dp", None),
        P("dp"),
        P("dp", None),
        P("dp"),
        P(None, "dp"),
        P("dp"),
    )
    step = functools.partial(local, ndp=mesh.shape["dp"], nctx=mesh.shape["ctx"])
    return jax.shard_map(step, mesh=mesh, in_specs=in_specs, out_specs=out_specs, check_vma=False)
```

profile of v0, /device:TPU:0, one launch (start us, length us, event | category | flops | bytes accessed | tf_op | source)
XLA Modules:
  0.0 151.6 jit_solution(14740349783464140109)
XLA Ops:
  1.3 2.0 %collective-permute-done.1.refs_11_ = s32[1,512]{1,0:T(1,128)S(1)} collective-permute-done((s32[1,512]{1,0:T(1,128)}, s32[1,512]{1,0:T(1,128)S(1)}, u32[]{:S(2)}, u32[]{:S(2)}) %collective-permute-start.1) | collective-permute-done | bytes 2080 | tf_op jit(solution)/shard_map/ppermute | solution.py:1077
  3.3 17.9 %attend.1 = (bf16[1024,768]{1,0:T(8,128)(2,1)S(1)}, bf16[1024,384]{1,0:T(8,128)(2,1)S(1)}, bf16[1024,384]{1,0:T(8,128)(2,1)S(1)}, bf16[1024,384]{1,0:T(8,128)(2,...) custom-call(s32[11]{0:T(128)S(1)} %stack.47.refs_0_, ...), custom_call_target="tpu_custom_call" | custom-call | flops 4000000000 | bytes 65536 | tf_op jit(solution)/shard_map/attend/pallas_call | solution.py:57
  21.7 1.8 %collective-permute-done.2.refs_2_.refs_5_ = bf16[384,1024]{1,0:T(8,128)(2,1)S(1)} collective-permute-done((bf16[384,1024]{1,0:T(8,128)(2,1)S(1)}, bf16[384,1024]{1,0:T(8,128)(2,1)S(1)}, u32[]{:S(2)}, u32[]{:S(2)}) %collective-permute-start.2) | collective-permute-done | bytes 786464 | tf_op jit(solution)/shard_map/ppermute | solution.py:1077
  23.5 3.5 %post.1 = (f32[512,768]{1,0:T(8,128)S(1)}, f32[512,768]{1,0:T(8,128)S(1)}, bf16[512,768]{1,0:T(8,128)(2,1)S(1)}, f32[8,128]{1,0:T(8,128)S(1)}) custom-call(s32[11]{0:T(128)S(1)} %stack.47.refs_0_, bf16[384,1024]{1,0:T(8,128)(2,1)S(1)} %get-tuple-element.128.refs_1_.refs_4_, bf16[384,1024]{1,0:T(8,128)(2,1)S(1)} %collective-permute-done.2.refs_2_.refs_5_, ...), custom_call_target="tpu_custom_call" | custom-call | flops 600000000 | bytes 65536 | tf_op jit(solution)/shard_map/post/pallas_call | solution.py:57
  27.3 2.0 %collective-permute-done.3.refs_2_ = bf16[512,768]{1,0:T(8,128)(2,1)S(1)} collective-permute-done((bf16[512,768]{1,0:T(8,128)(2,1)S(1)}, bf16[512,768]{1,0:T(8,128)(2,1)S(1)}, u32[]{:S(2)}, u32[]{:S(2)}) %collective-permute-start.3) | collective-permute-done | bytes 786464 | tf_op jit(solution)/shard_map/ppermute | solution.py:1077
  29.3 7.7 %mlp.1 = (bf16[1024,1536]{1,0:T(8,128)(2,1)S(1)}, bf16[1024,1536]{1,0:T(8,128)(2,1)S(1)}, f32[1,1536]{1,0:T(1,128)S(1)}, f32[1,768]{1,0:T(1,128)S(1)}, f32[8,128]{1,0:T(8,128)S(1)}) custom-call(s32[11]{0:T(128)S(1)} %stack.47.refs_0_, bf16[512,768]{1,0:T(8,128)(2,1)S(1)} %get-tuple-element.131.refs_1_, bf16[512,768]{1,0:T(8,128)(2,1)S(1)} %collective-permute-done.3.refs_2_, ...), custom_call_target="tpu_custom_call" | custom-call | flops 1920000000 | bytes 65536 | tf_op jit(solution)/shard_map/mlp/pallas_call | solution.py:57
  37.4 4.1 %wgrad_fc1.1 = (bf16[2,4,48,1536]{3,2,1,0:T(8,128)(2,1)S(1)}, bf16[2,4,48,1536]{3,2,1,0:T(8,128)(2,1)S(1)}, f32[8,128]{1,0:T(8,128)S(1)}) custom-call(s32[11]{0:T(128)S(1)} %stack.47.refs_0_, bf16[512,768]{1,0:T(8,128)(2,1)S(1)} %get-tuple-element.131.refs_1_, bf16[512,768]{1,0:T(8,128)(2,1)S(1)} %collective-permute-done.3.refs_2_, ...), custom_call_target="tpu_custom_call" | custom-call | flops 840000000 | bytes 65536 | tf_op jit(solution)/shard_map/wgrad_fc1/pallas_call | solution.py:57
  41.5 2.7 %collective-permute-start.8 = (bf16[2,4,48,1536]{3,2,1,0:T(8,128)(2,1)S(1)}, bf16[2,4,48,1536]{3,2,1,0:T(8,128)(2,1)S(1)}, u32[]{:S(2)}, u32[]{:S(2)}) collective-permute-start(bf16[2,4,48,1536]{3,2,1,0:T(8,128)(2,1)S(1)} %get-tuple-element.149), channel_id=1, source_target_pairs={{0,2},{1,5},{2,0},{3,7},{4,6},{5,1},{6,4},{7,3},{8,10},{9,13},{10,... | collective-permute-start | bytes 3538952 | tf_op jit(solution)/shard_map/ppermute | solution.py:1041
  44.2 3.8 %part.2 = (f32[512,768]{1,0:T(8,128)S(1)}, bf16[512,768]{1,0:T(8,128)(2,1)S(1)}, f32[8,128]{1,0:T(8,128)S(1)}) custom-call(s32[11]{0:T(128)S(1)} %stack.47.refs_0_, bf16[1024,1536]{1,0:T(8,128)(2,1)S(1)} %get-tuple-element.135.refs_3_.refs_1_, bf16[768,3072]{1,0:T(8,128)(2,1)S(1)} %copy-done.2, f32[8,128]{1,0:T(8,128)S(1)} %get-tuple-element.137.refs_3_), custom_call_target="tpu_custom_call" | custom-call | flops 840000000 | bytes 65536 | tf_op jit(solution)/shard_map/part/pallas_call | solution.py:57
  48.2 6.8 %wgrad_fc2.1 = (bf16[2,4,192,384]{3,2,1,0:T(8,128)(2,1)S(1)}, bf16[2,4,192,384]{3,2,1,0:T(8,128)(2,1)S(1)}, f32[1,384]{1,0:T(1,128)S(1)}, f32[8,128]{1,0:T(8,128)S(1)}) custom-call(s32[11]{0:T(128)S(1)} %stack.47.refs_0_, bf16[1024,1536]{1,0:T(8,128)(2,1)S(1)} %get-tuple-element.134.refs_1_, bf16[1024,1536]{1,0:T(8,128)(2,1)S(1)} %collective-permute-done.5.refs_2_, ...), custom_call_target="tpu_custom_call" | custom-call | flops 900000000 | bytes 65536 | tf_op jit(solution)/shard_map/wgrad_fc2/pallas_call | solution.py:57
  55.0 4.4 %part.3 = (f32[512,768]{1,0:T(8,128)S(1)}, bf16[512,768]{1,0:T(8,128)(2,1)}, f32[8,128]{1,0:T(8,128)S(1)}) custom-call(s32[11]{0:T(128)S(1)} %stack.47.refs_0_, bf16[1024,1536]{1,0:T(8,128)(2,1)S(1)} %get-tuple-element.134.refs_1_, bf16[3072,768]{1,0:T(8,128)(2,1)S(1)} %copy-done.1, f32[8,128]{1,0:T(8,128)S(1)} %get-tuple-element.139.refs_3_), custom_call_target="tpu_custom_call" | custom-call | flops 840000000 | bytes 65536 | tf_op jit(solution)/shard_map/part/pallas_call | solution.py:57
  60.5 2.0 %norm2.1 = (f32[512,768]{1,0:T(8,128)S(1)}, bf16[512,768]{1,0:T(8,128)(2,1)S(1)}, f32[8,768]{1,0:T(8,128)S(1)}, f32[8,128]{1,0:T(8,128)S(1)}) custom-call(s32[11]{0:T(128)S(1)} %stack.47.refs_0_, f32[512,768]{1,0:T(8,128)S(1)} %get-tuple-element.145.refs_1_, bf16[512,768]{1,0:T(8,128)(2,1)S(1)} %collective-permute-done.7.refs_2_, ...), custom_call_target="tpu_custom_call" | custom-call | flops 600000000 | bytes 65536 | tf_op jit(solution)/shard_map/norm2/pallas_call | solution.py:57
  65.2 2.3 %oproj.1 = (bf16[384,1024]{1,0:T(8,128)(2,1)S(1)}, bf16[2,4,48,1152]{3,2,1,0:T(8,128)(2,1)S(1)}, bf16[2,4,48,1152]{3,2,1,0:T(8,128)(2,1)S(1)}, f32[8,128]{1,0:T(8,128)S(1)}) custom-call(s32[11]{0:T(128)S(1)} %stack.47.refs_0_, bf16[768,768]{1,0:T(8,128)(2,1)S(1)} %copy-done.3, bf16[512,768]{1,0:T(8,128)(2,1)S(1)} %get-tuple-element.152.refs_2_, ...), custom_call_target="tpu_custom_call" | custom-call | flops 600000000 | bytes 65536 | tf_op jit(solution)/shard_map/oproj/pallas_call | solution.py:57
  67.5 16.5 %attn_bwd.2 = (bf16[1024,768]{1,0:T(8,128)(2,1)S(1)}, f32[8,768]{1,0:T(8,128)S(1)}, bf16[2,4,48,1152]{3,2,1,0:T(8,128)(2,1)S(1)}, bf16[2,4,48,1152]{3,2,1,0:T(8,128)(2,1)S(1)}, f32[8,128]{1,0:T(8,128)S(1)}) custom-call(s32[11]{0:T(128)S(1)} %stack.47.refs_0_, ...), custom_call_target="tpu_custom_call", output_to_operand_aliasing={{2}: (16, {}), {3}: (17, {})} | custom-call | flops 3200000000 | bytes 65536 | tf_op jit(solution)/shard_map/attn_bwd/pallas_call | solution.py:57
  84.1 1.4 collective-permute-start.15
  88.1 1.6 %collective-permute-start.13 = (bf16[2,48,1536]{2,1,0:T(8,128)(2,1)S(1)}, bf16[2,48,1536]{2,1,0:T(8,128)(2,1)S(1)}, u32[]{:S(2)}, u32[]{:S(2)}) collective-permute-start(bf16[2,48,1536]{2,1,0:T(8,128)(2,1)S(1)} %get-tuple-element.184), channel_id=1, source_target_pairs={{0,8},{1,17},{2,10},{3,19},{4,12},{5,21},{6,14},{7,23},{8,0},{9,25... | collective-permute-start | bytes 884744 | tf_op jit(solution)/shard_map/ppermute | solution.py:1041
  89.8 8.9 %attn_bwd.3 = (bf16[1024,384]{1,0:T(8,128)(2,1)S(1)}, f32[8,768]{1,0:T(8,128)S(1)}, bf16[2,4,48,384]{3,2,1,0:T(8,128)(2,1)S(1)}, bf16[2,4,48,384]{3,2,1,0:T(8,128)(2,1)S(1)}, f32[8,128]{1,0:T(8,128)S(1)}) custom-call(s32[11]{0:T(128)S(1)} %stack.47.refs_0_, bf16[6,1024,1024]{2,1,0:T(8,128)(2,1)} %get-tuple-element.143.refs_1_, ...), custom_call_target="tpu_custom_call" | custom-call | flops 1600000000 | bytes 65536 | tf_op jit(solution)/shard_map/attn_bwd/pallas_call | solution.py:57
  98.7 1.7 %mix.1 = (bf16[512,768]{1,0:T(8,128)(2,1)}, f32[8,128]{1,0:T(8,128)S(1)}) custom-call(s32[11]{0:T(128)S(1)} %stack.47.refs_0_, f32[512,768]{1,0:T(8,128)S(1)} %get-tuple-element.140.refs_1_, bf16[512,768]{1,0:T(8,128)(2,1)S(1)} %collective-permute-done.6.refs_2_, f32[512,768]{1,0:T(8,128)S(1)} %get-tuple-element.142.refs_3_, ...), custom_call_target="tpu_custom_call" | custom-call | flops 500000000 | bytes 65536 | tf_op jit(solution)/shard_map/mix/pallas_call | solution.py:57
  101.8 2.0 %dgrad.2 = (bf16[512,768]{1,0:T(8,128)(2,1)S(1)}, f32[8,128]{1,0:T(8,128)S(1)}) custom-call(s32[11]{0:T(128)S(1)} %stack.47.refs_0_, bf16[1024,768]{1,0:T(8,128)(2,1)S(1)} %get-tuple-element.173.refs_1_, bf16[1024,384]{1,0:T(8,128)(2,1)S(1)} %get-tuple-element.174.refs_2_, bf16[768,2304]{1,0:T(8,128)(2,1)S(1)} %copy-done, bf16[768,2304]{1,0:T(8,128)(2,1)S(1)} %copy-done, ...), custom_call_target="tpu_custom_call" | custom-call | flops 400000000 | bytes 65536 | tf_op jit(solution)/shard_map/dgrad/pallas_call | solution.py:57
  104.9 1.6 %collective-permute-start.18 = (bf16[2,192,384]{2,1,0:T(8,128)(2,1)S(1)}, bf16[2,192,384]{2,1,0:T(8,128)(2,1)S(1)}, u32[]{:S(2)}, u32[]{:S(2)}) collective-permute-start(bf16[2,192,384]{2,1,0:T(8,128)(2,1)S(1)} %get-tuple-element.199), channel_id=1, source_target_pairs={{0,8},{1,17},{2,10},{3,19},{4,12},{5,21},{6,14},{7,23},{8,0},{9,25... | collective-permute-start | bytes 884744 | tf_op jit(solution)/shard_map/ppermute | solution.py:1041
  111.0 1.5 deal.1
  113.4 1.4 collective-permute-done.18
  115.4 1.7 %collective-permute-start.22 = (bf16[1,96,1536]{2,1,0:T(8,128)(2,1)S(1)}, bf16[1,96,1536]{2,1,0:T(8,128)(2,1)S(1)}, u32[]{:S(2)}, u32[]{:S(2)}) collective-permute-start(bf16[1,96,1536]{2,1,0:T(8,128)(2,1)S(1)} %get-tuple-element.217), channel_id=1, source_target_pairs={{0,16},{1,9},{2,18},{3,11},{4,20},{5,13},{6,22},{7,15},{8,24},{9,1... | collective-permute-start | bytes 884744 | tf_op jit(solution)/shard_map/ppermute | solution.py:1041
  119.0 1.4 collective-permute-start.21
  120.4 2.0 %dgrad.3 = (f32[512,768]{1,0:T(8,128)S(1)}, f32[8,128]{1,0:T(8,128)S(1)}) custom-call(s32[11]{0:T(128)S(1)} %stack.47.refs_0_, bf16[1024,768]{1,0:T(8,128)(2,1)S(1)} %get-tuple-element.173.refs_1_, bf16[1024,384]{1,0:T(8,128)(2,1)S(1)} %get-tuple-element.174.refs_2_, bf16[768,2304]{1,0:T(8,128)(2,1)S(1)} %copy-done, bf16[768,2304]{1,0:T(8,128)(2,1)S(1)} %copy-done, ...), custom_call_target="tpu_custom_call" | custom-call | flops 400000000 | bytes 65536 | tf_op jit(solution)/shard_map/dgrad/pallas_call | solution.py:57
  122.5 2.4 %norm1.1 = (bf16[512,768]{1,0:T(8,128)(2,1)}, f32[8,128]{1,0:T(8,128)S(1)}) custom-call(s32[11]{0:T(128)S(1)} %stack.47.refs_0_, f32[512,768]{1,0:T(8,128)S(1)} %get-tuple-element.205.refs_1_, bf16[512,768]{1,0:T(8,128)(2,1)S(1)} %collective-permute-done.19.refs_2_, bf16[512,768]{1,0:T(8,128)(2,1)S(1)} %bitcast.35, ...), custom_call_target="tpu_custom_call" | custom-call | flops 600000000 | bytes 65536 | tf_op jit(solution)/shard_map/norm1/pallas_call | solution.py:57
  124.8 1.4 collective-permute-done.22
  128.0 1.6 %collective-permute-done.24.refs_2_ = bf16[96,1536]{1,0:T(8,128)(2,1)S(1)} collective-permute-done((bf16[96,1536]{1,0:T(8,128)(2,1)S(1)}, bf16[96,1536]{1,0:T(8,128)(2,1)S(1)}, u32[]{:S(2)}, u32[]{:S(2)}) %collective-permute-start.24) | collective-permute-done | bytes 294944 | tf_op jit(solution)/shard_map/ppermute | solution.py:1077
  129.6 1.6 %place_ff.1 = (f32[48,3072]{1,0:T(8,128)}, f32[192,768]{1,0:T(8,128)}, f32[8,128]{1,0:T(8,128)S(1)}) custom-call(s32[11]{0:T(128)S(1)} %stack.47.refs_0_, bf16[96,1536]{1,0:T(8,128)(2,1)S(1)} %get-tuple-element.223.refs_1_, bf16[96,1536]{1,0:T(8,128)(2,1)S(1)} %collective-permute-done.24.refs_2_, f32[8,128]{1,0:T(8,128)S(1)} %get-tuple-element.224.refs_3_), custom_call_target="tpu_custom_call" | custom-call | flops 200000000 | bytes 65536 | tf_op jit(solution)/shard_map/place_ff/pallas_call | solution.py:57
  131.2 7.3 %collective-permute-done.23.refs_2_ = bf16[112,1536]{1,0:T(8,128)(2,1)S(1)} collective-permute-done((bf16[112,1536]{1,0:T(8,128)(2,1)S(1)}, bf16[112,1536]{1,0:T(8,128)(2,1)S(1)}, u32[]{:S(2)}, u32[]{:S(2)}) %collective-permute-start.23) | collective-permute-done | bytes 344096 | tf_op jit(solution)/shard_map/ppermute | solution.py:1131
  139.2 7.6 %collective-permute-done.25.refs_2_.refs_1_ = bf16[64,1536]{1,0:T(8,128)(2,1)S(1)} collective-permute-done((bf16[64,1536]{1,0:T(8,128)(2,1)S(1)}, bf16[64,1536]{1,0:T(8,128)(2,1)S(1)}, u32[]{:S(2)}, u32[]{:S(2)}) %collective-permute-start.25) | collective-permute-done | bytes 196640 | tf_op jit(solution)/shard_map/ppermute | solution.py:1131
  147.5 1.4 small_last.1
  (79 shorter events, 24.8 us)
Async XLA Ops:
  0.6 2.6 %collective-permute-start = (bf16[512,768]{1,0:T(8,128)(2,1)}, bf16[512,768]{1,0:T(8,128)(2,1)S(1)}, u32[]{:S(2)}, u32[]{:S(2)}) collective-permute-start(bf16[512,768]{1,0:T(8,128)(2,1)} %bitcast.32), channel_id=1, source_target_pairs={{0,1},{1,0},{2,3},{3,2},{4,5},{5,4},{6,7},{7,6},{8,9},{9,8},{10,11... | collective-permute-start | bytes 2359304 | tf_op jit(solution)/shard_map/ppermute | solution.py:1077
  1.2 2.1 %collective-permute-start.1 = (s32[1,512]{1,0:T(1,128)}, s32[1,512]{1,0:T(1,128)S(1)}, u32[]{:S(2)}, u32[]{:S(2)}) collective-permute-start(s32[1,512]{1,0:T(1,128)} %refs_10_.2), channel_id=1, source_target_pairs={{0,1},{1,0},{2,3},{3,2},{4,5},{5,4},{6,7},{7,6},{8,9},{9,8},{10,11... | collective-permute-start | bytes 6152 | tf_op jit(solution)/shard_map/ppermute | solution.py:1077
  3.3 20.2 %copy-start.3 = (bf16[768,768]{1,0:T(8,128)(2,1)S(1)}, bf16[768,768]{1,0:T(8,128)(2,1)}, u32[]{:S(2)}) copy-start(bf16[768,768]{1,0:T(8,128)(2,1)} %refs_1_.1) | copy-start | bytes 3538948
  3.3 20.2 %copy-start.8 = (bf16[768]{0:T(1024)(128)(2,1)S(1)}, bf16[768]{0:T(1024)(128)(2,1)}, u32[]{:S(2)}) copy-start(bf16[768]{0:T(1024)(128)(2,1)} %refs_8_.5) | copy-start | bytes 4612
  3.3 26.0 %copy-start.2 = (bf16[768,3072]{1,0:T(8,128)(2,1)S(1)}, bf16[768,3072]{1,0:T(8,128)(2,1)}, u32[]{:S(2)}) copy-start(bf16[768,3072]{1,0:T(8,128)(2,1)} %refs_2_.2) | copy-start | bytes 14155780
  21.2 2.3 %collective-permute-start.2 = (bf16[384,1024]{1,0:T(8,128)(2,1)S(1)}, bf16[384,1024]{1,0:T(8,128)(2,1)S(1)}, u32[]{:S(2)}, u32[]{:S(2)}) collective-permute-start(bf16[384,1024]{1,0:T(8,128)(2,1)S(1)} %get-tuple-element.128.refs_1_.refs_4_), channel_id=1, source_target_pairs={{0,1},{1,0},{2,3},{3,2},{4,5},{5,4},{6,7},{7,6},{8,9},{9,8},{10,11... | collective-permute-start | bytes 2359304 | tf_op jit(solution)/shard_map/ppermute | solution.py:1077
  21.5 5.8 %collective-permute-start.4 = (bf16[512,768]{1,0:T(8,128)(2,1)S(1)}, bf16[512,768]{1,0:T(8,128)(2,1)S(1)}, u32[]{:S(2)}, u32[]{:S(2)}) collective-permute-start(bf16[512,768]{1,0:T(8,128)(2,1)S(1)} %get-tuple-element.132.refs_3_.refs_5_), channel_id=1, source_target_pairs={{0,1},{1,0},{2,3},{3,2},{4,5},{5,4},{6,7},{7,6},{8,9},{9,8},{10,11... | collective-permute-start | bytes 2359304 | tf_op jit(solution)/shard_map/ppermute | solution.py:1077
  23.5 5.8 %copy-start.1 = (bf16[3072,768]{1,0:T(8,128)(2,1)S(1)}, bf16[3072,768]{1,0:T(8,128)(2,1)}, u32[]{:S(2)}) copy-start(bf16[3072,768]{1,0:T(8,128)(2,1)} %refs_2_.3) | copy-start | bytes 14155780
  23.5 5.8 %copy-start.9 = (bf16[3072]{0:T(1024)(128)(2,1)S(1)}, bf16[3072]{0:T(1024)(128)(2,1)}, u32[]{:S(2)}) copy-start(bf16[3072]{0:T(1024)(128)(2,1)} %refs_7_.8) | copy-start | bytes 18436
  26.9 2.4 %collective-permute-start.3 = (bf16[512,768]{1,0:T(8,128)(2,1)S(1)}, bf16[512,768]{1,0:T(8,128)(2,1)S(1)}, u32[]{:S(2)}, u32[]{:S(2)}) collective-permute-start(bf16[512,768]{1,0:T(8,128)(2,1)S(1)} %get-tuple-element.131.refs_1_), channel_id=1, source_target_pairs={{0,1},{1,0},{2,3},{3,2},{4,5},{5,4},{6,7},{7,6},{8,9},{9,8},{10,11... | collective-permute-start | bytes 2359304 | tf_op jit(solution)/shard_map/ppermute | solution.py:1077
  37.0 11.2 %collective-permute-start.5 = (bf16[1024,1536]{1,0:T(8,128)(2,1)S(1)}, bf16[1024,1536]{1,0:T(8,128)(2,1)S(1)}, u32[]{:S(2)}, u32[]{:S(2)}) collective-permute-start(bf16[1024,1536]{1,0:T(8,128)(2,1)S(1)} %get-tuple-element.134.refs_1_), channel_id=1, source_target_pairs={{0,1},{1,0},{2,3},{3,2},{4,5},{5,4},{6,7},{7,6},{8,9},{9,8},{10,11... | collective-permute-start | bytes 9437192 | tf_op jit(solution)/shard_map/ppermute | solution.py:1077
  41.5 17.9 %collective-permute-start.8 = (bf16[2,4,48,1536]{3,2,1,0:T(8,128)(2,1)S(1)}, bf16[2,4,48,1536]{3,2,1,0:T(8,128)(2,1)S(1)}, u32[]{:S(2)}, u32[]{:S(2)}) collective-permute-start(bf16[2,4,48,1536]{3,2,1,0:T(8,128)(2,1)S(1)} %get-tuple-element.149), channel_id=1, source_target_pairs={{0,2},{1,5},{2,0},{3,7},{4,6},{5,1},{6,4},{7,3},{8,10},{9,13},{10,... | collective-permute-start | bytes 3538952 | tf_op jit(solution)/shard_map/ppermute | solution.py:1041
  48.0 12.5 %collective-permute-start.7 = (bf16[512,768]{1,0:T(8,128)(2,1)S(1)}, bf16[512,768]{1,0:T(8,128)(2,1)S(1)}, u32[]{:S(2)}, u32[]{:S(2)}) collective-permute-start(bf16[512,768]{1,0:T(8,128)(2,1)S(1)} %get-tuple-element.146), channel_id=1, source_target_pairs={{0,1},{1,0},{2,3},{3,2},{4,5},{5,4},{6,7},{7,6},{8,9},{9,8},{10,11... | collective-permute-start | bytes 2359304 | tf_op jit(solution)/shard_map/ppermute | solution.py:1077
  62.6 2.7 %collective-permute-start.9 = (bf16[512,768]{1,0:T(8,128)(2,1)S(1)}, bf16[512,768]{1,0:T(8,128)(2,1)S(1)}, u32[]{:S(2)}, u32[]{:S(2)}) collective-permute-start(bf16[512,768]{1,0:T(8,128)(2,1)S(1)} %get-tuple-element.152.refs_2_), channel_id=1, source_target_pairs={{0,1},{1,0},{2,3},{3,2},{4,5},{5,4},{6,7},{7,6},{8,9},{9,8},{10,11... | collective-permute-start | bytes 2359304 | tf_op jit(solution)/shard_map/ppermute | solution.py:1077
  63.0 22.5 %collective-permute-start.11 = (bf16[2,4,192,384]{3,2,1,0:T(8,128)(2,1)S(1)}, bf16[2,4,192,384]{3,2,1,0:T(8,128)(2,1)S(1)}, u32[]{:S(2)}, u32[]{:S(2)}) collective-permute-start(bf16[2,4,192,384]{3,2,1,0:T(8,128)(2,1)S(1)} %get-tuple-element.164), channel_id=1, source_target_pairs={{0,2},{1,5},{2,0},{3,7},{4,6},{5,1},{6,4},{7,3},{8,10},{9,13},{10,... | collective-permute-start | bytes 3538952 | tf_op jit(solution)/shard_map/ppermute | solution.py:1041
  64.2 23.0 %collective-permute-start.10 = (bf16[4,48,1536]{2,1,0:T(8,128)(2,1)S(1)}, bf16[4,48,1536]{2,1,0:T(8,128)(2,1)S(1)}, u32[]{:S(2)}, u32[]{:S(2)}) collective-permute-start(bf16[4,48,1536]{2,1,0:T(8,128)(2,1)S(1)} %get-tuple-element.162), channel_id=1, source_target_pairs={{0,4},{1,3},{2,6},{3,1},{4,0},{5,7},{6,2},{7,5},{8,12},{9,11},{10,... | collective-permute-start | bytes 1769480 | tf_op jit(solution)/shard_map/ppermute | solution.py:1041
  65.2 33.4 %collective-permute-start.6 = (bf16[512,768]{1,0:T(8,128)(2,1)}, bf16[512,768]{1,0:T(8,128)(2,1)S(1)}, u32[]{:S(2)}, u32[]{:S(2)}) collective-permute-start(bf16[512,768]{1,0:T(8,128)(2,1)} %get-tuple-element.141), channel_id=1, source_target_pairs={{0,1},{1,0},{2,3},{3,2},{4,5},{5,4},{6,7},{7,6},{8,9},{9,8},{10,11... | collective-permute-start | bytes 2359304 | tf_op jit(solution)/shard_map/ppermute | solution.py:1077
  84.1 24.7 %collective-permute-start.15 = (bf16[2,4,48,1152]{3,2,1,0:T(8,128)(2,1)S(1)}, bf16[2,4,48,1152]{3,2,1,0:T(8,128)(2,1)S(1)}, u32[]{:S(2)}, u32[]{:S(2)}) collective-permute-start(bf16[2,4,48,1152]{3,2,1,0:T(8,128)(2,1)S(1)} %get-tuple-element.189), channel_id=1, source_target_pairs={{0,2},{1,5},{2,0},{3,7},{4,6},{5,1},{6,4},{7,3},{8,10},{9,13},{10,... | collective-permute-start | bytes 2654216 | tf_op jit(solution)/shard_map/ppermute | solution.py:1041
  86.3 18.0 %collective-permute-start.16 = (bf16[4,192,384]{2,1,0:T(8,128)(2,1)S(1)}, bf16[4,192,384]{2,1,0:T(8,128)(2,1)S(1)}, u32[]{:S(2)}, u32[]{:S(2)}) collective-permute-start(bf16[4,192,384]{2,1,0:T(8,128)(2,1)S(1)} %get-tuple-element.191), channel_id=1, source_target_pairs={{0,4},{1,3},{2,6},{3,1},{4,0},{5,7},{6,2},{7,5},{8,12},{9,11},{10,... | collective-permute-start | bytes 1769480 | tf_op jit(solution)/shard_map/ppermute | solution.py:1041
  88.1 12.2 %collective-permute-start.13 = (bf16[2,48,1536]{2,1,0:T(8,128)(2,1)S(1)}, bf16[2,48,1536]{2,1,0:T(8,128)(2,1)S(1)}, u32[]{:S(2)}, u32[]{:S(2)}) collective-permute-start(bf16[2,48,1536]{2,1,0:T(8,128)(2,1)S(1)} %get-tuple-element.184), channel_id=1, source_target_pairs={{0,8},{1,17},{2,10},{3,19},{4,12},{5,21},{6,14},{7,23},{8,0},{9,25... | collective-permute-start | bytes 884744 | tf_op jit(solution)/shard_map/ppermute | solution.py:1041
  103.9 18.6 %collective-permute-start.19 = (bf16[512,768]{1,0:T(8,128)(2,1)S(1)}, bf16[512,768]{1,0:T(8,128)(2,1)S(1)}, u32[]{:S(2)}, u32[]{:S(2)}) collective-permute-start(bf16[512,768]{1,0:T(8,128)(2,1)S(1)} %get-tuple-element.206), channel_id=1, source_target_pairs={{0,1},{1,0},{2,3},{3,2},{4,5},{5,4},{6,7},{7,6},{8,9},{9,8},{10,11... | collective-permute-start | bytes 2359304 | tf_op jit(solution)/shard_map/ppermute | solution.py:1077
  104.9 9.9 %collective-permute-start.18 = (bf16[2,192,384]{2,1,0:T(8,128)(2,1)S(1)}, bf16[2,192,384]{2,1,0:T(8,128)(2,1)S(1)}, u32[]{:S(2)}, u32[]{:S(2)}) collective-permute-start(bf16[2,192,384]{2,1,0:T(8,128)(2,1)S(1)} %get-tuple-element.199), channel_id=1, source_target_pairs={{0,8},{1,17},{2,10},{3,19},{4,12},{5,21},{6,14},{7,23},{8,0},{9,25... | collective-permute-start | bytes 884744 | tf_op jit(solution)/shard_map/ppermute | solution.py:1041
  106.5 4.5 %collective-permute-start.14 = (f32[18,8,384]{2,1,0:T(8,128)S(1)}, f32[18,8,384]{2,1,0:T(8,128)S(1)}, u32[]{:S(2)}, u32[]{:S(2)}) collective-permute-start(f32[18,8,384]{2,1,0:T(8,128)S(1)} %get-tuple-element.187.refs_1_), channel_id=1, source_target_pairs={{0,1},{1,0},{2,3},{3,2},{4,5},{5,4},{6,7},{7,6},{8,9},{9,8},{10,11... | collective-permute-start | bytes 663560 | tf_op jit(solution)/shard_map/ppermute | solution.py:1077
  107.5 9.6 %collective-permute-start.12 = (bf16[2,4,48,384]{3,2,1,0:T(8,128)(2,1)S(1)}, bf16[2,4,48,384]{3,2,1,0:T(8,128)(2,1)S(1)}, u32[]{:S(2)}, u32[]{:S(2)}) collective-permute-start(bf16[2,4,48,384]{3,2,1,0:T(8,128)(2,1)S(1)} %get-tuple-element.176), channel_id=1, source_target_pairs={{0,2},{1,5},{2,0},{3,7},{4,6},{5,1},{6,4},{7,3},{8,10},{9,13},{10,... | collective-permute-start | bytes 884744 | tf_op jit(solution)/shard_map/ppermute | solution.py:1041
  109.9 16.9 %collective-permute-start.20 = (bf16[4,48,1152]{2,1,0:T(8,128)(2,1)S(1)}, bf16[4,48,1152]{2,1,0:T(8,128)(2,1)S(1)}, u32[]{:S(2)}, u32[]{:S(2)}) collective-permute-start(bf16[4,48,1152]{2,1,0:T(8,128)(2,1)S(1)} %get-tuple-element.212), channel_id=1, source_target_pairs={{0,4},{1,3},{2,6},{3,1},{4,0},{5,7},{6,2},{7,5},{8,12},{9,11},{10,... | collective-permute-start | bytes 1327112 | tf_op jit(solution)/shard_map/ppermute | solution.py:1041
  112.5 5.9 %collective-permute-start.17 = (f32[8,8,384]{2,1,0:T(8,128)S(1)}, f32[8,8,384]{2,1,0:T(8,128)S(1)}, u32[]{:S(2)}, u32[]{:S(2)}) collective-permute-start(f32[8,8,384]{2,1,0:T(8,128)S(1)} %get-tuple-element.197), channel_id=1, source_target_pairs={{0,2},{1,5},{2,0},{3,7},{4,6},{5,1},{6,4},{7,3},{8,10},{9,13},{10,... | collective-permute-start | bytes 294920 | tf_op jit(solution)/shard_map/ppermute | solution.py:1131
  115.4 10.8 %collective-permute-start.22 = (bf16[1,96,1536]{2,1,0:T(8,128)(2,1)S(1)}, bf16[1,96,1536]{2,1,0:T(8,128)(2,1)S(1)}, u32[]{:S(2)}, u32[]{:S(2)}) collective-permute-start(bf16[1,96,1536]{2,1,0:T(8,128)(2,1)S(1)} %get-tuple-element.217), channel_id=1, source_target_pairs={{0,16},{1,9},{2,18},{3,11},{4,20},{5,13},{6,22},{7,15},{8,24},{9,1... | collective-permute-start | bytes 884744 | tf_op jit(solution)/shard_map/ppermute | solution.py:1041
  119.0 7.8 %collective-permute-start.21 = (bf16[4,64,384]{2,1,0:T(8,128)(2,1)S(1)}, bf16[4,64,384]{2,1,0:T(8,128)(2,1)S(1)}, u32[]{:S(2)}, u32[]{:S(2)}) collective-permute-start(bf16[4,64,384]{2,1,0:T(8,128)(2,1)S(1)} %get-tuple-element.214), channel_id=1, source_target_pairs={{0,4},{1,3},{2,6},{3,1},{4,0},{5,7},{6,2},{7,5},{8,12},{9,11},{10,... | collective-permute-start | bytes 589832 | tf_op jit(solution)/shard_map/ppermute | solution.py:1131
  127.5 11.1 %collective-permute-start.23 = (bf16[112,1536]{1,0:T(8,128)(2,1)S(1)}, bf16[112,1536]{1,0:T(8,128)(2,1)S(1)}, u32[]{:S(2)}, u32[]{:S(2)}) collective-permute-start(bf16[112,1536]{1,0:T(8,128)(2,1)S(1)} %get-tuple-element.221), channel_id=1, source_target_pairs={{0,8},{1,17},{2,10},{3,19},{4,12},{5,21},{6,14},{7,23},{8,0},{9,25... | collective-permute-start | bytes 1032200 | tf_op jit(solution)/shard_map/ppermute | solution.py:1131
  128.0 1.6 %collective-permute-start.24 = (bf16[96,1536]{1,0:T(8,128)(2,1)S(1)}, bf16[96,1536]{1,0:T(8,128)(2,1)S(1)}, u32[]{:S(2)}, u32[]{:S(2)}) collective-permute-start(bf16[96,1536]{1,0:T(8,128)(2,1)S(1)} %get-tuple-element.223.refs_1_), channel_id=1, source_target_pairs={{0,1},{1,0},{2,3},{3,2},{4,5},{5,4},{6,7},{7,6},{8,9},{9,8},{10,11... | collective-permute-start | bytes 884744 | tf_op jit(solution)/shard_map/ppermute | solution.py:1077
  139.2 7.7 %collective-permute-start.25 = (bf16[64,1536]{1,0:T(8,128)(2,1)S(1)}, bf16[64,1536]{1,0:T(8,128)(2,1)S(1)}, u32[]{:S(2)}, u32[]{:S(2)}) collective-permute-start(bf16[64,1536]{1,0:T(8,128)(2,1)S(1)} %get-tuple-element.226), channel_id=1, source_target_pairs={{0,16},{1,9},{2,18},{3,11},{4,20},{5,13},{6,22},{7,15},{8,24},{9,1... | collective-permute-start | bytes 589832 | tf_op jit(solution)/shard_map/ppermute | solution.py:1131
  147.4 2.8 %collective-permute-start.26 = (bf16[48,1536]{1,0:T(8,128)(2,1)S(1)}, bf16[48,1536]{1,0:T(8,128)(2,1)S(1)}, u32[]{:S(2)}, u32[]{:S(2)}) collective-permute-start(bf16[48,1536]{1,0:T(8,128)(2,1)S(1)} %get-tuple-element.232.refs_1_), channel_id=1, source_target_pairs={{0,1},{1,0},{2,3},{3,2},{4,5},{5,4},{6,7},{7,6},{8,9},{9,8},{10,11... | collective-permute-start | bytes 442376 | tf_op jit(solution)/shard_map/ppermute | solution.py:1077
  (6 other events, 15.3 us)
where the time goes:
time: 152 us
  Pallas kernels  101 us (66%)
  waiting for transfers between devices  26.5 us (17%)
  starting transfers between devices  21.5 us (14%)
    pallas_call x32, Pallas kernels, call(): pl.pallas_call(inner, grid_spec=pltpu.PrefetchScalarGridSpec(num_scalar_p...  101 us
    ppermute x4, waiting for transfers between devices, local_pair(): along = lambda step, v: lax.ppermute(v, ('dp', 'ctx'), grid.pairs[step - 1])  16.3 us
    ppermute x10, starting transfers between devices, start(): self.got = lax.ppermute(send, ('dp', 'ctx'), self.pairs[self.step])  14.5 us
    ppermute x13, waiting for transfers between devices, local_pair(): swap = lambda v: lax.ppermute(v, 'ctx', [(0, 1), (1, 0)])  7.29 us
    ppermute x13, starting transfers between devices, local_pair(): swap = lambda v: lax.ppermute(v, 'ctx', [(0, 1), (1, 0)])  3.96 us
  transfers between devices with their start and end apart: 27, of which 10 were waited for; matrix products, arithmetic and copies ran while one was open for 1% of the time, Pallas kernels for 47%

commit v1 on v0

--- a/solution.py
+++ b/solution.py
@@ -15,8 +15,9 @@
 NEG_START = -1e30
 F32, BF16 = jnp.float32, jnp.bfloat16
 COST = 2e8
+FF = 10
 MLP_COLS = 1536
-BWD_BLK = 512
+BWD_BLK = 1024
 
 
 def dot(a, b):
@@ -370,7 +371,7 @@
             pltpu.VMEM((length, 128), F32),
             pltpu.VMEM((width, 384), BF16),
         ],
-        mb=36, us=8.0 * count, aliases=aliases, after=after, name="attn_bwd",
+        mb=40, us=8.0 * count, aliases=aliases, after=after, name="attn_bwd",
     )
 
 
@@ -477,7 +478,7 @@
 def mlp_call(order, n2a, n2b, wa, wb, mod, w1, b1, w2):
     span, width = n2a.shape
     hf = w1.shape[1] // 2
-    blk = 512
+    blk = 256
     n = span // blk
     row = lambda w: pl.BlockSpec((blk, w), lambda i, s: (i, 0))
     return order.call(
@@ -496,18 +497,19 @@
     )
 
 
-def store_parts(s_ref, acc_ref, r, keep_ref, send_ref):
+def store_parts(s_ref, acc_ref, r, keep_ref, send_ref, base=0):
+    mine = s_ref[base + 1]
     for i in range(8):
-        rest = sum(((i >> (2 - j)) & 1) * s_ref[6 + j] for j in range(3))
-        for ref, bit in ((keep_ref, s_ref[1]), (send_ref, 1 - s_ref[1])):
-            at = pl.ds(pl.multiple_of((rest + bit * s_ref[5]) * r, 16), r)
+        rest = sum(((i >> (2 - j)) & 1) * s_ref[base + 6 + j] for j in range(3))
+        for ref, bit in ((keep_ref, mine), (send_ref, 1 - mine)):
+            at = pl.ds(pl.multiple_of((rest + bit * s_ref[base + 5]) * r, 16), r)
             ref[i // 4, i % 4] = acc_ref[at, :]
 
 
 def wgrad_body(r, s_ref, la_ref, lb_ref, g_ref, keep_ref, send_ref, acc_ref):
     span = la_ref.shape[0]
     acc_ref[...] = (dot_tn(la_ref[...], g_ref[:span]) + dot_tn(lb_ref[...], g_ref[span:])).astype(BF16)
-    store_parts(s_ref, acc_ref, r, keep_ref, send_ref)
+    store_parts(s_ref, acc_ref, r, keep_ref, send_ref, FF)
 
 
 def wgrad_call(order, left_a, left_b, right, blk):
@@ -555,11 +557,11 @@
 
     gate = mod_ref[0:1, pl.ds(pl.multiple_of(5 * width + s_ref[0] * half, 128), half)]
     za, zb = lax.div(step, 2), lax.rem(step, 2)
-    slot = jnp.where(s_ref[0] == 0, zb * 2 + za, za * 2 + zb)
+    two, four = jnp.where(s_ref[0] == 0, zb, za), jnp.where(s_ref[0] == 0, za, zb)
     for other in range(2):
-        for ref, bit in ((keep_ref, s_ref[1]), (send_ref, 1 - s_ref[1])):
-            at = pl.ds(pl.multiple_of((other * s_ref[6] + bit * s_ref[5]) * r, 16), r)
-            ref[other, slot] = (acc_ref[at, :] * gate).astype(BF16)
+        for ref, bit in ((keep_ref, s_ref[FF + 1]), (send_ref, 1 - s_ref[FF + 1])):
+            at = pl.ds(pl.multiple_of((other * s_ref[FF + 7] + bit * s_ref[FF + 5]) * r, 16), r)
+            ref[two, other * 2 + four] = (acc_ref[at, :] * gate).astype(BF16)
 
 
 def wgrad2_call(order, hidden, hidden_o, wa, wb, mod, w2, bias):
@@ -1018,23 +1020,27 @@
 
 
 class Grid:
-    ORDERS = ((1, 2, 4, 8), (2, 1, 8, 4))
+    ATT_ORDERS = ((1, 2, 4, 8), (2, 1, 8, 4))
+    FF_ORDERS = ((1, 4, 2, 8), (2, 8, 1, 4))
 
     def __init__(self, ndp):
         self.index = lax.axis_index("dp")
         core = lax.axis_index("ctx")
-        self.flip = lambda mask: [(i, i ^ mask) for i in range(ndp)]
-        masks = [jnp.where(core == 0, a, b) for a, b in zip(*self.ORDERS)]
-        bits = [jnp.where((self.index & m) > 0, 1, 0) for m in masks]
-        self.place = jnp.stack([core, *bits, *masks, self.index // 4, self.index]).astype(jnp.int32)
-        self.pairs = [
-            [(2 * i + c, 2 * (i ^ self.ORDERS[c][step]) + c) for i in range(ndp) for c in range(2)] for step in range(4)
-        ]
+        place = [core]
+        self.pairs = []
+        for orders in (self.ATT_ORDERS, self.FF_ORDERS):
+            masks = [jnp.where(core == 0, a, b) for a, b in zip(*orders)]
+            bits = [jnp.where((self.index & m) > 0, 1, 0) for m in masks]
+            place += [*bits, *masks, self.index // 4, self.index]
+            self.pairs.append(
+                [[(2 * i + c, 2 * (i ^ orders[c][step]) + c) for i in range(ndp) for c in range(2)] for step in range(4)]
+            )
+        self.place = jnp.stack(place).astype(jnp.int32)
 
 
 class Job:
-    def __init__(self, pairs):
-        self.pairs, self.step = pairs, 0
+    def __init__(self, pairs, base):
+        self.pairs, self.base, self.step = pairs, base, 0
 
     def start(self, keep, send):
         self.keep = keep
@@ -1052,16 +1058,16 @@
         self.start(stay, away)
 
     def split(self, order):
-        return fold_call(order, self.step + 1, *self.parts())
+        return fold_call(order, self.base + self.step + 1, *self.parts())
 
     def last(self):
         return self.keep[0], self.got[0]
 
 
 def join(order, fold, one, two):
-    job = Job(two.pairs)
+    job = Job(two.pairs, two.base)
     job.step = two.step
-    away, stay = fold(order, job.step + 1, one if isinstance(one, tuple) else one.parts(), two.parts())
+    away, stay = fold(order, job.base + job.step + 1, one if isinstance(one, tuple) else one.parts(), two.parts())
     job.start(stay, away)
     return job
 
@@ -1092,7 +1098,8 @@
         order, n2, n2_o, wtd, wtd_o, mod, fc1_weight, fc1_bias, fc2_weight
     )
     hidden_o = swap(hidden)
-    fc1, fc2, rest, last = (Job(grid.pairs) for _ in range(4))
+    fc1, fc2 = (Job(grid.pairs[1], FF) for _ in range(2))
+    rest, last = (Job(grid.pairs[0], 0) for _ in range(2))
     fc1.start(*wgrad_call(order, n2, n2_o, g_pre, 768))
     pn_own, pn_oth = part_call(order, True, g_pre, fc1_weight)
     pn_got = swap(pn_oth)
@@ -1128,19 +1135,19 @@
     fc2.fold(order)
     rest.fold(order)
     cond_grad, small_keep, send = deal_call(order, packet, packet_o, ada_weight)
-    along = lambda step, v: lax.ppermute(v, ("dp", "ctx"), grid.pairs[step - 1])
+    along = lambda step, v: lax.ppermute(v, ("dp", "ctx"), grid.pairs[0][step - 1])
     small_got = along(1, send)
+    d_own = dgrad_call(order, [g_a, g_b], qkv_weight, 0)
     ff = join(order, join_ff_call, tuple(fc1_split), fc2)
     away, last_keep, small_keep = fold_last_call(order, *last.parts(), small_keep, small_got)
     last_got = along(2, away)
-    d_own = dgrad_call(order, [g_a, g_b], qkv_weight, 0)
     input_grad = norm1_call(order, d_own, d_got, tok, g_mid, mod, norm1_gain)
+    away, keep, small_keep = fold_att_call(
+        order, rest.parts(), last_keep.reshape((2, 2) + last_keep.shape[1:]), last_got, small_keep
+    )
+    got = along(3, away)
     ff_sum = add_call(order, *ff.last())
     ff_other = swap(ff_sum)
-    away, keep, small_keep = fold_att_call(
-        order, rest.parts(), last_keep.reshape((2, 2) + last_keep.shape[1:]), last_got, small_keep
-    )
-    got = along(3, away)
     fc1_grad, fc2_grad = place_ff_call(order, ff_sum, ff_other, hw)
     away, keep, small_keep = fold_end_call(order, keep, got, small_keep)
     got = along(4, away)

time: 152 us -> 149 us (0.980)
  waiting for transfers between devices: 26.5 us -> 24.1 us
    ppermute x10, waiting for transfers between devices: 2.87 us -> 0.99 us  [start(): self.got = lax.ppermute(send, ('dp', 'ctx'), self.pairs[self.step])]
    ppermute x4, starting transfers between devices: 2.95 us -> 4.69 us  [local_pair(): lax.ppermute(v, ('dp', 'ctx'), grid.pairs[0][step - 1])]
where the time goes in v1:
time: 149 us
  Pallas kernels  100 us (67%)
  waiting for transfers between devices  24.1 us (16%)
  starting transfers between devices  22.1 us (15%)
    pallas_call x32, Pallas kernels, call(): pl.pallas_call(inner, grid_spec=pltpu.PrefetchScalarGridSpec(num_scalar_p...  100 us
    ppermute x4, waiting for transfers between devices, local_pair(): lax.ppermute(v, ('dp', 'ctx'), grid.pairs[0][step - 1])  15.9 us
    ppermute x10, starting transfers between devices, start(): self.got = lax.ppermute(send, ('dp', 'ctx'), self.pairs[self.step])  13.5 us
    ppermute x13, waiting for transfers between devices, local_pair(): swap = lambda v: lax.ppermute(v, 'ctx', [(0, 1), (1, 0)])  7.22 us
    ppermute x4, starting transfers between devices, local_pair(): lax.ppermute(v, ('dp', 'ctx'), grid.pairs[0][step - 1])  4.69 us
    ppermute x13, starting transfers between devices, local_pair(): swap = lambda v: lax.ppermute(v, 'ctx', [(0, 1), (1, 0)])  3.9 us
  transfers between devices with their start and end apart: 27, of which 10 were waited for; matrix products, arithmetic and copies ran while one was open for 1% of the time, Pallas kernels for 47%

profile of v1, /device:TPU:0, one launch (start us, length us, event | category | flops | bytes accessed | tf_op | source)
XLA Modules:
  0.0 148.8 jit_solution(7040101571140746417)
XLA Ops:
  1.3 1.9 %collective-permute-done.1.refs_11_ = s32[1,512]{1,0:T(1,128)S(1)} collective-permute-done((s32[1,512]{1,0:T(1,128)}, s32[1,512]{1,0:T(1,128)S(1)}, u32[]{:S(2)}, u32[]{:S(2)}) %collective-permute-start.1) | collective-permute-done | bytes 2080 | tf_op jit(solution)/shard_map/ppermute | solution.py:1083
  3.3 17.8 %attend.1 = (bf16[1024,768]{1,0:T(8,128)(2,1)S(1)}, bf16[1024,384]{1,0:T(8,128)(2,1)S(1)}, bf16[1024,384]{1,0:T(8,128)(2,1)S(1)}, bf16[1024,384]{1,0:T(8,128)(2,...) custom-call(s32[21]{0:T(128)S(1)} %stack.57.refs_0_, ...), custom_call_target="tpu_custom_call" | custom-call | flops 4000000000 | bytes 65536 | tf_op jit(solution)/shard_map/attend/pallas_call | solution.py:58
  21.6 1.8 %collective-permute-done.2.refs_2_.refs_5_ = bf16[384,1024]{1,0:T(8,128)(2,1)S(1)} collective-permute-done((bf16[384,1024]{1,0:T(8,128)(2,1)S(1)}, bf16[384,1024]{1,0:T(8,128)(2,1)S(1)}, u32[]{:S(2)}, u32[]{:S(2)}) %collective-permute-start.2) | collective-permute-done | bytes 786464 | tf_op jit(solution)/shard_map/ppermute | solution.py:1083
  23.4 3.4 %post.1 = (f32[512,768]{1,0:T(8,128)S(1)}, f32[512,768]{1,0:T(8,128)S(1)}, bf16[512,768]{1,0:T(8,128)(2,1)S(1)}, f32[8,128]{1,0:T(8,128)S(1)}) custom-call(s32[21]{0:T(128)S(1)} %stack.57.refs_0_, bf16[384,1024]{1,0:T(8,128)(2,1)S(1)} %get-tuple-element.128.refs_1_.refs_4_, bf16[384,1024]{1,0:T(8,128)(2,1)S(1)} %collective-permute-done.2.refs_2_.refs_5_, ...), custom_call_target="tpu_custom_call" | custom-call | flops 600000000 | bytes 65536 | tf_op jit(solution)/shard_map/post/pallas_call | solution.py:58
  27.3 1.9 %collective-permute-done.3.refs_2_ = bf16[512,768]{1,0:T(8,128)(2,1)S(1)} collective-permute-done((bf16[512,768]{1,0:T(8,128)(2,1)S(1)}, bf16[512,768]{1,0:T(8,128)(2,1)S(1)}, u32[]{:S(2)}, u32[]{:S(2)}) %collective-permute-start.3) | collective-permute-done | bytes 786464 | tf_op jit(solution)/shard_map/ppermute | solution.py:1083
  29.2 7.9 %mlp.1 = (bf16[1024,1536]{1,0:T(8,128)(2,1)S(1)}, bf16[1024,1536]{1,0:T(8,128)(2,1)S(1)}, f32[1,1536]{1,0:T(1,128)S(1)}, f32[1,768]{1,0:T(1,128)S(1)}, f32[8,128]{1,0:T(8,128)S(1)}) custom-call(s32[21]{0:T(128)S(1)} %stack.57.refs_0_, bf16[512,768]{1,0:T(8,128)(2,1)S(1)} %get-tuple-element.131.refs_1_, bf16[512,768]{1,0:T(8,128)(2,1)S(1)} %collective-permute-done.3.refs_2_, ...), custom_call_target="tpu_custom_call" | custom-call | flops 1920000000 | bytes 65536 | tf_op jit(solution)/shard_map/mlp/pallas_call | solution.py:58
  37.6 4.0 %wgrad_fc1.1 = (bf16[2,4,48,1536]{3,2,1,0:T(8,128)(2,1)S(1)}, bf16[2,4,48,1536]{3,2,1,0:T(8,128)(2,1)S(1)}, f32[8,128]{1,0:T(8,128)S(1)}) custom-call(s32[21]{0:T(128)S(1)} %stack.57.refs_0_, bf16[512,768]{1,0:T(8,128)(2,1)S(1)} %get-tuple-element.131.refs_1_, bf16[512,768]{1,0:T(8,128)(2,1)S(1)} %collective-permute-done.3.refs_2_, ...), custom_call_target="tpu_custom_call" | custom-call | flops 840000000 | bytes 65536 | tf_op jit(solution)/shard_map/wgrad_fc1/pallas_call | solution.py:58
  41.6 2.7 %collective-permute-start.8 = (bf16[2,4,48,1536]{3,2,1,0:T(8,128)(2,1)S(1)}, bf16[2,4,48,1536]{3,2,1,0:T(8,128)(2,1)S(1)}, u32[]{:S(2)}, u32[]{:S(2)}) collective-permute-start(bf16[2,4,48,1536]{3,2,1,0:T(8,128)(2,1)S(1)} %get-tuple-element.149), channel_id=1, source_target_pairs={{0,2},{1,5},{2,0},{3,7},{4,6},{5,1},{6,4},{7,3},{8,10},{9,13},{10,... | collective-permute-start | bytes 3538952 | tf_op jit(solution)/shard_map/ppermute | solution.py:1047
  44.3 3.8 %part.2 = (f32[512,768]{1,0:T(8,128)S(1)}, bf16[512,768]{1,0:T(8,128)(2,1)S(1)}, f32[8,128]{1,0:T(8,128)S(1)}) custom-call(s32[21]{0:T(128)S(1)} %stack.57.refs_0_, bf16[1024,1536]{1,0:T(8,128)(2,1)S(1)} %get-tuple-element.135.refs_3_.refs_1_, bf16[768,3072]{1,0:T(8,128)(2,1)S(1)} %copy-done.2, f32[8,128]{1,0:T(8,128)S(1)} %get-tuple-element.137.refs_3_), custom_call_target="tpu_custom_call" | custom-call | flops 840000000 | bytes 65536 | tf_op jit(solution)/shard_map/part/pallas_call | solution.py:58
  48.2 7.0 %wgrad_fc2.1 = (bf16[2,4,192,384]{3,2,1,0:T(8,128)(2,1)S(1)}, bf16[2,4,192,384]{3,2,1,0:T(8,128)(2,1)S(1)}, f32[1,384]{1,0:T(1,128)S(1)}, f32[8,128]{1,0:T(8,128)S(1)}) custom-call(s32[21]{0:T(128)S(1)} %stack.57.refs_0_, bf16[1024,1536]{1,0:T(8,128)(2,1)S(1)} %get-tuple-element.134.refs_1_, bf16[1024,1536]{1,0:T(8,128)(2,1)S(1)} %collective-permute-done.5.refs_2_, ...), custom_call_target="tpu_custom_call" | custom-call | flops 900000000 | bytes 65536 | tf_op jit(solution)/shard_map/wgrad_fc2/pallas_call | solution.py:58
  55.2 4.4 %part.3 = (f32[512,768]{1,0:T(8,128)S(1)}, bf16[512,768]{1,0:T(8,128)(2,1)}, f32[8,128]{1,0:T(8,128)S(1)}) custom-call(s32[21]{0:T(128)S(1)} %stack.57.refs_0_, bf16[1024,1536]{1,0:T(8,128)(2,1)S(1)} %get-tuple-element.134.refs_1_, bf16[3072,768]{1,0:T(8,128)(2,1)S(1)} %copy-done.1, f32[8,128]{1,0:T(8,128)S(1)} %get-tuple-element.139.refs_3_), custom_call_target="tpu_custom_call" | custom-call | flops 840000000 | bytes 65536 | tf_op jit(solution)/shard_map/part/pallas_call | solution.py:58
  60.7 2.0 %norm2.1 = (f32[512,768]{1,0:T(8,128)S(1)}, bf16[512,768]{1,0:T(8,128)(2,1)S(1)}, f32[8,768]{1,0:T(8,128)S(1)}, f32[8,128]{1,0:T(8,128)S(1)}) custom-call(s32[21]{0:T(128)S(1)} %stack.57.refs_0_, f32[512,768]{1,0:T(8,128)S(1)} %get-tuple-element.145.refs_1_, bf16[512,768]{1,0:T(8,128)(2,1)S(1)} %collective-permute-done.7.refs_2_, ...), custom_call_target="tpu_custom_call" | custom-call | flops 600000000 | bytes 65536 | tf_op jit(solution)/shard_map/norm2/pallas_call | solution.py:58
  64.4 1.6 %collective-permute-start.10 = (bf16[4,48,1536]{2,1,0:T(8,128)(2,1)S(1)}, bf16[4,48,1536]{2,1,0:T(8,128)(2,1)S(1)}, u32[]{:S(2)}, u32[]{:S(2)}) collective-permute-start(bf16[4,48,1536]{2,1,0:T(8,128)(2,1)S(1)} %get-tuple-element.162), channel_id=1, source_target_pairs={{0,8},{1,17},{2,10},{3,19},{4,12},{5,21},{6,14},{7,23},{8,0},{9,25... | collective-permute-start | bytes 1769480 | tf_op jit(solution)/shard_map/ppermute | solution.py:1047
  66.9 2.3 %oproj.1 = (bf16[384,1024]{1,0:T(8,128)(2,1)S(1)}, bf16[2,4,48,1152]{3,2,1,0:T(8,128)(2,1)S(1)}, bf16[2,4,48,1152]{3,2,1,0:T(8,128)(2,1)S(1)}, f32[8,128]{1,0:T(8,128)S(1)}) custom-call(s32[21]{0:T(128)S(1)} %stack.57.refs_0_, bf16[768,768]{1,0:T(8,128)(2,1)S(1)} %copy-done.3, bf16[512,768]{1,0:T(8,128)(2,1)S(1)} %get-tuple-element.152.refs_2_, ...), custom_call_target="tpu_custom_call" | custom-call | flops 600000000 | bytes 65536 | tf_op jit(solution)/shard_map/oproj/pallas_call | solution.py:58
  69.1 14.0 %attn_bwd.2 = (bf16[1024,768]{1,0:T(8,128)(2,1)S(1)}, f32[8,768]{1,0:T(8,128)S(1)}, bf16[2,4,48,1152]{3,2,1,0:T(8,128)(2,1)S(1)}, bf16[2,4,48,1152]{3,2,1,0:T(8,128)(2,1)S(1)}, f32[8,128]{1,0:T(8,128)S(1)}) custom-call(s32[21]{0:T(128)S(1)} %stack.57.refs_0_, ...), custom_call_target="tpu_custom_call", output_to_operand_aliasing={{2}: (16, {}), {3}: (17, {})} | custom-call | flops 3200000000 | bytes 65536 | tf_op jit(solution)/shard_map/attn_bwd/pallas_call | solution.py:58
  84.1 1.5 %fold.7 = (bf16[4,192,384]{2,1,0:T(8,128)(2,1)}, bf16[4,192,384]{2,1,0:T(8,128)(2,1)S(1)}, f32[8,128]{1,0:T(8,128)S(1)}) custom-call(s32[21]{0:T(128)S(1)} %stack.57.refs_0_, bf16[2,4,192,384]{3,2,1,0:T(8,128)(2,1)S(1)} %get-tuple-element.163.refs_1_.refs_3_, bf16[2,4,192,384]{3,2,1,0:T(8,128)(2,1)S(1)} %collective-permute-done.11.refs_2_.refs_4_, ...), custom_call_target="tpu_custom_call" | custom-call | flops 240000000 | bytes 65536 | tf_op jit(solution)/shard_map/fold/pallas_call | solution.py:58
  88.0 1.5 %collective-permute-start.15 = (bf16[4,192,384]{2,1,0:T(8,128)(2,1)}, bf16[4,192,384]{2,1,0:T(8,128)(2,1)S(1)}, u32[]{:S(2)}, u32[]{:S(2)}) collective-permute-start(bf16[4,192,384]{2,1,0:T(8,128)(2,1)} %get-tuple-element.189), channel_id=1, source_target_pairs={{0,8},{1,17},{2,10},{3,19},{4,12},{5,21},{6,14},{7,23},{8,0},{9,25... | collective-permute-start | bytes 1769480 | tf_op jit(solution)/shard_map/ppermute | solution.py:1047
  89.6 8.1 %attn_bwd.3 = (bf16[1024,384]{1,0:T(8,128)(2,1)S(1)}, f32[8,768]{1,0:T(8,128)S(1)}, bf16[2,4,48,384]{3,2,1,0:T(8,128)(2,1)S(1)}, bf16[2,4,48,384]{3,2,1,0:T(8,128)(2,1)S(1)}, f32[8,128]{1,0:T(8,128)S(1)}) custom-call(s32[21]{0:T(128)S(1)} %stack.57.refs_0_, bf16[6,1024,1024]{2,1,0:T(8,128)(2,1)} %get-tuple-element.143.refs_1_, ...), custom_call_target="tpu_custom_call" | custom-call | flops 1600000000 | bytes 65536 | tf_op jit(solution)/shard_map/attn_bwd/pallas_call | solution.py:58
  97.7 2.6 %mix.1 = (bf16[512,768]{1,0:T(8,128)(2,1)}, f32[8,128]{1,0:T(8,128)S(1)}) custom-call(s32[21]{0:T(128)S(1)} %stack.57.refs_0_, f32[512,768]{1,0:T(8,128)S(1)} %get-tuple-element.140.refs_1_, bf16[512,768]{1,0:T(8,128)(2,1)} %collective-permute-done.6.refs_2_, f32[512,768]{1,0:T(8,128)S(1)} %get-tuple-element.142.refs_3_, ...), custom_call_target="tpu_custom_call" | custom-call | flops 500000000 | bytes 65536 | tf_op jit(solution)/shard_map/mix/pallas_call | solution.py:58
  101.8 2.0 %dgrad.2 = (bf16[512,768]{1,0:T(8,128)(2,1)S(1)}, f32[8,128]{1,0:T(8,128)S(1)}) custom-call(s32[21]{0:T(128)S(1)} %stack.57.refs_0_, bf16[1024,768]{1,0:T(8,128)(2,1)S(1)} %get-tuple-element.173.refs_1_, bf16[1024,384]{1,0:T(8,128)(2,1)S(1)} %get-tuple-element.174.refs_2_, bf16[768,2304]{1,0:T(8,128)(2,1)S(1)} %copy-done, bf16[768,2304]{1,0:T(8,128)(2,1)S(1)} %copy-done, ...), custom_call_target="tpu_custom_call" | custom-call | flops 400000000 | bytes 65536 | tf_op jit(solution)/shard_map/dgrad/pallas_call | solution.py:58
  105.5 1.4 collective-permute-start.17
  109.0 1.5 deal.1
  111.7 2.0 %dgrad.3 = (f32[512,768]{1,0:T(8,128)S(1)}, f32[8,128]{1,0:T(8,128)S(1)}) custom-call(s32[21]{0:T(128)S(1)} %stack.57.refs_0_, bf16[1024,768]{1,0:T(8,128)(2,1)S(1)} %get-tuple-element.173.refs_1_, bf16[1024,384]{1,0:T(8,128)(2,1)S(1)} %get-tuple-element.174.refs_2_, bf16[768,2304]{1,0:T(8,128)(2,1)S(1)} %copy-done, bf16[768,2304]{1,0:T(8,128)(2,1)S(1)} %copy-done, ...), custom_call_target="tpu_custom_call" | custom-call | flops 400000000 | bytes 65536 | tf_op jit(solution)/shard_map/dgrad/pallas_call | solution.py:58
  118.2 1.5 %collective-permute-start.21 = (bf16[4,64,384]{2,1,0:T(8,128)(2,1)S(1)}, bf16[4,64,384]{2,1,0:T(8,128)(2,1)S(1)}, u32[]{:S(2)}, u32[]{:S(2)}) collective-permute-start(bf16[4,64,384]{2,1,0:T(8,128)(2,1)S(1)} %get-tuple-element.214), channel_id=1, source_target_pairs={{0,4},{1,3},{2,6},{3,1},{4,0},{5,7},{6,2},{7,5},{8,12},{9,11},{10,... | collective-permute-start | bytes 589832 | tf_op jit(solution)/shard_map/ppermute | solution.py:1138
  119.6 2.5 %norm1.1 = (bf16[512,768]{1,0:T(8,128)(2,1)}, f32[8,128]{1,0:T(8,128)S(1)}) custom-call(s32[21]{0:T(128)S(1)} %stack.57.refs_0_, f32[512,768]{1,0:T(8,128)S(1)} %get-tuple-element.195.refs_1_, bf16[512,768]{1,0:T(8,128)(2,1)S(1)} %collective-permute-done.16.refs_2_, bf16[512,768]{1,0:T(8,128)(2,1)S(1)} %bitcast.35, ...), custom_call_target="tpu_custom_call" | custom-call | flops 600000000 | bytes 65536 | tf_op jit(solution)/shard_map/norm1/pallas_call | solution.py:58
  122.1 1.8 %collective-permute-done.21.refs_4_ = bf16[4,64,384]{2,1,0:T(8,128)(2,1)S(1)} collective-permute-done((bf16[4,64,384]{2,1,0:T(8,128)(2,1)S(1)}, bf16[4,64,384]{2,1,0:T(8,128)(2,1)S(1)}, u32[]{:S(2)}, u32[]{:S(2)}) %collective-permute-start.21) | collective-permute-done | bytes 196640 | tf_op jit(solution)/shard_map/ppermute | solution.py:1138
  126.6 1.6 %collective-permute-done.24.refs_2_ = bf16[96,1536]{1,0:T(8,128)(2,1)S(1)} collective-permute-done((bf16[96,1536]{1,0:T(8,128)(2,1)S(1)}, bf16[96,1536]{1,0:T(8,128)(2,1)S(1)}, u32[]{:S(2)}, u32[]{:S(2)}) %collective-permute-start.24) | collective-permute-done | bytes 294944 | tf_op jit(solution)/shard_map/ppermute | solution.py:1083
  128.2 1.6 %place_ff.1 = (f32[48,3072]{1,0:T(8,128)}, f32[192,768]{1,0:T(8,128)}, f32[8,128]{1,0:T(8,128)S(1)}) custom-call(s32[21]{0:T(128)S(1)} %stack.57.refs_0_, bf16[96,1536]{1,0:T(8,128)(2,1)S(1)} %get-tuple-element.223.refs_1_, bf16[96,1536]{1,0:T(8,128)(2,1)S(1)} %collective-permute-done.24.refs_2_, f32[8,128]{1,0:T(8,128)S(1)} %get-tuple-element.224.refs_3_), custom_call_target="tpu_custom_call" | custom-call | flops 200000000 | bytes 65536 | tf_op jit(solution)/shard_map/place_ff/pallas_call | solution.py:58
  129.8 5.1 %collective-permute-done.22.refs_2_ = bf16[112,1536]{1,0:T(8,128)(2,1)S(1)} collective-permute-done((bf16[112,1536]{1,0:T(8,128)(2,1)S(1)}, bf16[112,1536]{1,0:T(8,128)(2,1)S(1)}, u32[]{:S(2)}, u32[]{:S(2)}) %collective-permute-start.22) | collective-permute-done | bytes 344096 | tf_op jit(solution)/shard_map/ppermute | solution.py:1138
  136.2 7.8 %collective-permute-done.25.refs_2_.refs_1_ = bf16[64,1536]{1,0:T(8,128)(2,1)S(1)} collective-permute-done((bf16[64,1536]{1,0:T(8,128)(2,1)S(1)}, bf16[64,1536]{1,0:T(8,128)(2,1)S(1)}, u32[]{:S(2)}, u32[]{:S(2)}) %collective-permute-start.25) | collective-permute-done | bytes 196640 | tf_op jit(solution)/shard_map/ppermute | solution.py:1138
  144.7 1.4 small_last.1
  147.4 1.4 place_att.1
  (79 shorter events, 26.1 us)
Async XLA Ops:
  0.6 2.6 %collective-permute-start = (bf16[512,768]{1,0:T(8,128)(2,1)}, bf16[512,768]{1,0:T(8,128)(2,1)S(1)}, u32[]{:S(2)}, u32[]{:S(2)}) collective-permute-start(bf16[512,768]{1,0:T(8,128)(2,1)} %bitcast.32), channel_id=1, source_target_pairs={{0,1},{1,0},{2,3},{3,2},{4,5},{5,4},{6,7},{7,6},{8,9},{9,8},{10,11... | collective-permute-start | bytes 2359304 | tf_op jit(solution)/shard_map/ppermute | solution.py:1083
  1.2 2.1 %collective-permute-start.1 = (s32[1,512]{1,0:T(1,128)}, s32[1,512]{1,0:T(1,128)S(1)}, u32[]{:S(2)}, u32[]{:S(2)}) collective-permute-start(s32[1,512]{1,0:T(1,128)} %refs_10_.2), channel_id=1, source_target_pairs={{0,1},{1,0},{2,3},{3,2},{4,5},{5,4},{6,7},{7,6},{8,9},{9,8},{10,11... | collective-permute-start | bytes 6152 | tf_op jit(solution)/shard_map/ppermute | solution.py:1083
  3.3 20.1 %copy-start.3 = (bf16[768,768]{1,0:T(8,128)(2,1)S(1)}, bf16[768,768]{1,0:T(8,128)(2,1)}, u32[]{:S(2)}) copy-start(bf16[768,768]{1,0:T(8,128)(2,1)} %refs_1_.1) | copy-start | bytes 3538948
  3.3 20.1 %copy-start.8 = (bf16[768]{0:T(1024)(128)(2,1)S(1)}, bf16[768]{0:T(1024)(128)(2,1)}, u32[]{:S(2)}) copy-start(bf16[768]{0:T(1024)(128)(2,1)} %refs_8_.5) | copy-start | bytes 4612
  3.3 25.9 %copy-start.2 = (bf16[768,3072]{1,0:T(8,128)(2,1)S(1)}, bf16[768,3072]{1,0:T(8,128)(2,1)}, u32[]{:S(2)}) copy-start(bf16[768,3072]{1,0:T(8,128)(2,1)} %refs_2_.2) | copy-start | bytes 14155780
  21.1 2.3 %collective-permute-start.2 = (bf16[384,1024]{1,0:T(8,128)(2,1)S(1)}, bf16[384,1024]{1,0:T(8,128)(2,1)S(1)}, u32[]{:S(2)}, u32[]{:S(2)}) collective-permute-start(bf16[384,1024]{1,0:T(8,128)(2,1)S(1)} %get-tuple-element.128.refs_1_.refs_4_), channel_id=1, source_target_pairs={{0,1},{1,0},{2,3},{3,2},{4,5},{5,4},{6,7},{7,6},{8,9},{9,8},{10,11... | collective-permute-start | bytes 2359304 | tf_op jit(solution)/shard_map/ppermute | solution.py:1083
  21.5 5.8 %collective-permute-start.4 = (bf16[512,768]{1,0:T(8,128)(2,1)S(1)}, bf16[512,768]{1,0:T(8,128)(2,1)S(1)}, u32[]{:S(2)}, u32[]{:S(2)}) collective-permute-start(bf16[512,768]{1,0:T(8,128)(2,1)S(1)} %get-tuple-element.132.refs_3_.refs_5_), channel_id=1, source_target_pairs={{0,1},{1,0},{2,3},{3,2},{4,5},{5,4},{6,7},{7,6},{8,9},{9,8},{10,11... | collective-permute-start | bytes 2359304 | tf_op jit(solution)/shard_map/ppermute | solution.py:1083
  23.4 5.8 %copy-start.9 = (bf16[3072]{0:T(1024)(128)(2,1)S(1)}, bf16[3072]{0:T(1024)(128)(2,1)}, u32[]{:S(2)}) copy-start(bf16[3072]{0:T(1024)(128)(2,1)} %refs_7_.8) | copy-start | bytes 18436
  26.9 2.4 %collective-permute-start.3 = (bf16[512,768]{1,0:T(8,128)(2,1)S(1)}, bf16[512,768]{1,0:T(8,128)(2,1)S(1)}, u32[]{:S(2)}, u32[]{:S(2)}) collective-permute-start(bf16[512,768]{1,0:T(8,128)(2,1)S(1)} %get-tuple-element.131.refs_1_), channel_id=1, source_target_pairs={{0,1},{1,0},{2,3},{3,2},{4,5},{5,4},{6,7},{7,6},{8,9},{9,8},{10,11... | collective-permute-start | bytes 2359304 | tf_op jit(solution)/shard_map/ppermute | solution.py:1083
  37.2 11.1 %collective-permute-start.5 = (bf16[1024,1536]{1,0:T(8,128)(2,1)S(1)}, bf16[1024,1536]{1,0:T(8,128)(2,1)S(1)}, u32[]{:S(2)}, u32[]{:S(2)}) collective-permute-start(bf16[1024,1536]{1,0:T(8,128)(2,1)S(1)} %get-tuple-element.134.refs_1_), channel_id=1, source_target_pairs={{0,1},{1,0},{2,3},{3,2},{4,5},{5,4},{6,7},{7,6},{8,9},{9,8},{10,11... | collective-permute-start | bytes 9437192 | tf_op jit(solution)/shard_map/ppermute | solution.py:1083
  41.6 18.1 %collective-permute-start.8 = (bf16[2,4,48,1536]{3,2,1,0:T(8,128)(2,1)S(1)}, bf16[2,4,48,1536]{3,2,1,0:T(8,128)(2,1)S(1)}, u32[]{:S(2)}, u32[]{:S(2)}) collective-permute-start(bf16[2,4,48,1536]{3,2,1,0:T(8,128)(2,1)S(1)} %get-tuple-element.149), channel_id=1, source_target_pairs={{0,2},{1,5},{2,0},{3,7},{4,6},{5,1},{6,4},{7,3},{8,10},{9,13},{10,... | collective-permute-start | bytes 3538952 | tf_op jit(solution)/shard_map/ppermute | solution.py:1047
  48.0 12.7 %collective-permute-start.7 = (bf16[512,768]{1,0:T(8,128)(2,1)S(1)}, bf16[512,768]{1,0:T(8,128)(2,1)S(1)}, u32[]{:S(2)}, u32[]{:S(2)}) collective-permute-start(bf16[512,768]{1,0:T(8,128)(2,1)S(1)} %get-tuple-element.146), channel_id=1, source_target_pairs={{0,1},{1,0},{2,3},{3,2},{4,5},{5,4},{6,7},{7,6},{8,9},{9,8},{10,11... | collective-permute-start | bytes 2359304 | tf_op jit(solution)/shard_map/ppermute | solution.py:1083
  62.8 4.1 %collective-permute-start.9 = (bf16[512,768]{1,0:T(8,128)(2,1)S(1)}, bf16[512,768]{1,0:T(8,128)(2,1)S(1)}, u32[]{:S(2)}, u32[]{:S(2)}) collective-permute-start(bf16[512,768]{1,0:T(8,128)(2,1)S(1)} %get-tuple-element.152.refs_2_), channel_id=1, source_target_pairs={{0,1},{1,0},{2,3},{3,2},{4,5},{5,4},{6,7},{7,6},{8,9},{9,8},{10,11... | collective-permute-start | bytes 2359304 | tf_op jit(solution)/shard_map/ppermute | solution.py:1083
  63.2 20.8 %collective-permute-start.11 = (bf16[2,4,192,384]{3,2,1,0:T(8,128)(2,1)S(1)}, bf16[2,4,192,384]{3,2,1,0:T(8,128)(2,1)S(1)}, u32[]{:S(2)}, u32[]{:S(2)}) collective-permute-start(bf16[2,4,192,384]{3,2,1,0:T(8,128)(2,1)S(1)} %get-tuple-element.164), channel_id=1, source_target_pairs={{0,2},{1,5},{2,0},{3,7},{4,6},{5,1},{6,4},{7,3},{8,10},{9,13},{10,... | collective-permute-start | bytes 3538952 | tf_op jit(solution)/shard_map/ppermute | solution.py:1047
  64.4 21.2 %collective-permute-start.10 = (bf16[4,48,1536]{2,1,0:T(8,128)(2,1)S(1)}, bf16[4,48,1536]{2,1,0:T(8,128)(2,1)S(1)}, u32[]{:S(2)}, u32[]{:S(2)}) collective-permute-start(bf16[4,48,1536]{2,1,0:T(8,128)(2,1)S(1)} %get-tuple-element.162), channel_id=1, source_target_pairs={{0,8},{1,17},{2,10},{3,19},{4,12},{5,21},{6,14},{7,23},{8,0},{9,25... | collective-permute-start | bytes 1769480 | tf_op jit(solution)/shard_map/ppermute | solution.py:1047
  66.0 31.7 %collective-permute-start.6 = (bf16[512,768]{1,0:T(8,128)(2,1)}, bf16[512,768]{1,0:T(8,128)(2,1)}, u32[]{:S(2)}, u32[]{:S(2)}) collective-permute-start(bf16[512,768]{1,0:T(8,128)(2,1)} %get-tuple-element.141), channel_id=1, source_target_pairs={{0,1},{1,0},{2,3},{3,2},{4,5},{5,4},{6,7},{7,6},{8,9},{9,8},{10,11... | collective-permute-start | bytes 2359304 | tf_op jit(solution)/shard_map/ppermute | solution.py:1083
  83.2 23.7 %collective-permute-start.14 = (bf16[2,4,48,1152]{3,2,1,0:T(8,128)(2,1)S(1)}, bf16[2,4,48,1152]{3,2,1,0:T(8,128)(2,1)S(1)}, u32[]{:S(2)}, u32[]{:S(2)}) collective-permute-start(bf16[2,4,48,1152]{3,2,1,0:T(8,128)(2,1)S(1)} %get-tuple-element.187), channel_id=1, source_target_pairs={{0,2},{1,5},{2,0},{3,7},{4,6},{5,1},{6,4},{7,3},{8,10},{9,13},{10,... | collective-permute-start | bytes 2654216 | tf_op jit(solution)/shard_map/ppermute | solution.py:1047
  86.7 13.6 %collective-permute-start.12 = (bf16[2,48,1536]{2,1,0:T(8,128)(2,1)S(1)}, bf16[2,48,1536]{2,1,0:T(8,128)(2,1)S(1)}, u32[]{:S(2)}, u32[]{:S(2)}) collective-permute-start(bf16[2,48,1536]{2,1,0:T(8,128)(2,1)S(1)} %get-tuple-element.182), channel_id=1, source_target_pairs={{0,4},{1,3},{2,6},{3,1},{4,0},{5,7},{6,2},{7,5},{8,12},{9,11},{10,... | collective-permute-start | bytes 884744 | tf_op jit(solution)/shard_map/ppermute | solution.py:1047
  88.0 16.1 %collective-permute-start.15 = (bf16[4,192,384]{2,1,0:T(8,128)(2,1)}, bf16[4,192,384]{2,1,0:T(8,128)(2,1)S(1)}, u32[]{:S(2)}, u32[]{:S(2)}) collective-permute-start(bf16[4,192,384]{2,1,0:T(8,128)(2,1)} %get-tuple-element.189), channel_id=1, source_target_pairs={{0,8},{1,17},{2,10},{3,19},{4,12},{5,21},{6,14},{7,23},{8,0},{9,25... | collective-permute-start | bytes 1769480 | tf_op jit(solution)/shard_map/ppermute | solution.py:1047
  103.9 15.8 %collective-permute-start.16 = (bf16[512,768]{1,0:T(8,128)(2,1)S(1)}, bf16[512,768]{1,0:T(8,128)(2,1)S(1)}, u32[]{:S(2)}, u32[]{:S(2)}) collective-permute-start(bf16[512,768]{1,0:T(8,128)(2,1)S(1)} %get-tuple-element.196), channel_id=1, source_target_pairs={{0,1},{1,0},{2,3},{3,2},{4,5},{5,4},{6,7},{7,6},{8,9},{9,8},{10,11... | collective-permute-start | bytes 2359304 | tf_op jit(solution)/shard_map/ppermute | solution.py:1083
  104.8 9.7 %collective-permute-start.19 = (bf16[2,192,384]{2,1,0:T(8,128)(2,1)S(1)}, bf16[2,192,384]{2,1,0:T(8,128)(2,1)S(1)}, u32[]{:S(2)}, u32[]{:S(2)}) collective-permute-start(bf16[2,192,384]{2,1,0:T(8,128)(2,1)S(1)} %get-tuple-element.203), channel_id=1, source_target_pairs={{0,4},{1,3},{2,6},{3,1},{4,0},{5,7},{6,2},{7,5},{8,12},{9,11},{10,... | collective-permute-start | bytes 884744 | tf_op jit(solution)/shard_map/ppermute | solution.py:1047
  105.5 3.5 %collective-permute-start.13 = (f32[18,8,384]{2,1,0:T(8,128)S(1)}, f32[18,8,384]{2,1,0:T(8,128)S(1)}, u32[]{:S(2)}, u32[]{:S(2)}) collective-permute-start(f32[18,8,384]{2,1,0:T(8,128)S(1)} %get-tuple-element.185.refs_1_), channel_id=1, source_target_pairs={{0,1},{1,0},{2,3},{3,2},{4,5},{5,4},{6,7},{7,6},{8,9},{9,8},{10,11... | collective-permute-start | bytes 663560 | tf_op jit(solution)/shard_map/ppermute | solution.py:1083
  105.5 10.8 %collective-permute-start.17 = (bf16[2,4,48,384]{3,2,1,0:T(8,128)(2,1)S(1)}, bf16[2,4,48,384]{3,2,1,0:T(8,128)(2,1)S(1)}, u32[]{:S(2)}, u32[]{:S(2)}) collective-permute-start(bf16[2,4,48,384]{3,2,1,0:T(8,128)(2,1)S(1)} %get-tuple-element.199), channel_id=1, source_target_pairs={{0,2},{1,5},{2,0},{3,7},{4,6},{5,1},{6,4},{7,3},{8,10},{9,13},{10,... | collective-permute-start | bytes 884744 | tf_op jit(solution)/shard_map/ppermute | solution.py:1047
  108.1 14.1 %collective-permute-start.20 = (bf16[4,48,1152]{2,1,0:T(8,128)(2,1)S(1)}, bf16[4,48,1152]{2,1,0:T(8,128)(2,1)S(1)}, u32[]{:S(2)}, u32[]{:S(2)}) collective-permute-start(bf16[4,48,1152]{2,1,0:T(8,128)(2,1)S(1)} %get-tuple-element.212), channel_id=1, source_target_pairs={{0,4},{1,3},{2,6},{3,1},{4,0},{5,7},{6,2},{7,5},{8,12},{9,11},{10,... | collective-permute-start | bytes 1327112 | tf_op jit(solution)/shard_map/ppermute | solution.py:1047
  110.5 7.1 %collective-permute-start.18 = (f32[8,8,384]{2,1,0:T(8,128)S(1)}, f32[8,8,384]{2,1,0:T(8,128)S(1)}, u32[]{:S(2)}, u32[]{:S(2)}) collective-permute-start(f32[8,8,384]{2,1,0:T(8,128)S(1)} %get-tuple-element.201), channel_id=1, source_target_pairs={{0,2},{1,5},{2,0},{3,7},{4,6},{5,1},{6,4},{7,3},{8,10},{9,13},{10,... | collective-permute-start | bytes 294920 | tf_op jit(solution)/shard_map/ppermute | solution.py:1138
  113.7 6.0 %copy-start.4 = (bf16[1,512,768]{2,1,0:T(8,128)(2,1)S(1)}, bf16[1,512,768]{2,1,0:T(8,128)(2,1)}, u32[]{:S(2)}) copy-start(bf16[1,512,768]{2,1,0:T(8,128)(2,1)} %param.16) | copy-start | bytes 2359300
  115.1 10.8 %collective-permute-start.23 = (bf16[1,96,1536]{2,1,0:T(8,128)(2,1)S(1)}, bf16[1,96,1536]{2,1,0:T(8,128)(2,1)S(1)}, u32[]{:S(2)}, u32[]{:S(2)}) collective-permute-start(bf16[1,96,1536]{2,1,0:T(8,128)(2,1)S(1)} %get-tuple-element.221), channel_id=1, source_target_pairs={{0,16},{1,9},{2,18},{3,11},{4,20},{5,13},{6,22},{7,15},{8,24},{9,1... | collective-permute-start | bytes 884744 | tf_op jit(solution)/shard_map/ppermute | solution.py:1047
  118.2 5.7 %collective-permute-start.21 = (bf16[4,64,384]{2,1,0:T(8,128)(2,1)S(1)}, bf16[4,64,384]{2,1,0:T(8,128)(2,1)S(1)}, u32[]{:S(2)}, u32[]{:S(2)}) collective-permute-start(bf16[4,64,384]{2,1,0:T(8,128)(2,1)S(1)} %get-tuple-element.214), channel_id=1, source_target_pairs={{0,4},{1,3},{2,6},{3,1},{4,0},{5,7},{6,2},{7,5},{8,12},{9,11},{10,... | collective-permute-start | bytes 589832 | tf_op jit(solution)/shard_map/ppermute | solution.py:1138
  124.5 10.3 %collective-permute-start.22 = (bf16[112,1536]{1,0:T(8,128)(2,1)S(1)}, bf16[112,1536]{1,0:T(8,128)(2,1)S(1)}, u32[]{:S(2)}, u32[]{:S(2)}) collective-permute-start(bf16[112,1536]{1,0:T(8,128)(2,1)S(1)} %get-tuple-element.218), channel_id=1, source_target_pairs={{0,8},{1,17},{2,10},{3,19},{4,12},{5,21},{6,14},{7,23},{8,0},{9,25... | collective-permute-start | bytes 1032200 | tf_op jit(solution)/shard_map/ppermute | solution.py:1138
  126.5 1.6 %collective-permute-start.24 = (bf16[96,1536]{1,0:T(8,128)(2,1)S(1)}, bf16[96,1536]{1,0:T(8,128)(2,1)S(1)}, u32[]{:S(2)}, u32[]{:S(2)}) collective-permute-start(bf16[96,1536]{1,0:T(8,128)(2,1)S(1)} %get-tuple-element.223.refs_1_), channel_id=1, source_target_pairs={{0,1},{1,0},{2,3},{3,2},{4,5},{5,4},{6,7},{7,6},{8,9},{9,8},{10,11... | collective-permute-start | bytes 884744 | tf_op jit(solution)/shard_map/ppermute | solution.py:1083
  135.5 8.6 %collective-permute-start.25 = (bf16[64,1536]{1,0:T(8,128)(2,1)S(1)}, bf16[64,1536]{1,0:T(8,128)(2,1)S(1)}, u32[]{:S(2)}, u32[]{:S(2)}) collective-permute-start(bf16[64,1536]{1,0:T(8,128)(2,1)S(1)} %get-tuple-element.226), channel_id=1, source_target_pairs={{0,16},{1,9},{2,18},{3,11},{4,20},{5,13},{6,22},{7,15},{8,24},{9,1... | collective-permute-start | bytes 589832 | tf_op jit(solution)/shard_map/ppermute | solution.py:1138
  144.6 2.8 %collective-permute-start.26 = (bf16[48,1536]{1,0:T(8,128)(2,1)S(1)}, bf16[48,1536]{1,0:T(8,128)(2,1)S(1)}, u32[]{:S(2)}, u32[]{:S(2)}) collective-permute-start(bf16[48,1536]{1,0:T(8,128)(2,1)S(1)} %get-tuple-element.232.refs_1_), channel_id=1, source_target_pairs={{0,1},{1,0},{2,3},{3,2},{4,5},{5,4},{6,7},{7,6},{8,9},{9,8},{10,11... | collective-permute-start | bytes 442376 | tf_op jit(solution)/shard_map/ppermute | solution.py:1083
  (6 other events, 19.9 us)

commit v2 on v1

--- a/solution.py
+++ b/solution.py
@@ -1125,7 +1125,6 @@
     fc1.fold(order)
     g_b, sums_b, *bufs = back(pairs - 1, 1, None, 0, 1)
     last.start(*bufs)
-    mixed = mix_call(order, pm_own, pm_got, middle, mod, fc2_bias)
     fc1_split = fc1.split(order)
     packet = pack_call(
         order, sums_a, sums_b, sums2, gate_sum, b1_sum, b2_sum, norm1_gain, norm2_gain, mod, cond_vec
@@ -1151,6 +1150,7 @@
     fc1_grad, fc2_grad = place_ff_call(order, ff_sum, ff_other, hw)
     away, keep, small_keep = fold_end_call(order, keep, got, small_keep)
     got = along(4, away)
+    mixed = mix_call(order, pm_own, pm_got, middle, mod, fc2_bias)
     att_sum = add_call(order, keep, got)
     att_other = swap(att_sum)
     ada_grad, ada_bias_grad, fc1_bias_grad, norm1_grad, norm2_grad, fc2_bias_grad = last_call(

time: 149 us -> 149 us (level)
  Pallas kernels: 100 us -> 98.4 us
    ppermute x10, waiting for transfers between devices: 0.99 us -> 4.74 us  [start(): self.got = lax.ppermute(send, ('dp', 'ctx'), self.pairs[self.step])]
    ppermute x4, waiting for transfers between devices: 15.9 us -> 12.7 us  [local_pair(): lax.ppermute(v, ('dp', 'ctx'), grid.pairs[0][step - 1])]
    pallas_call x32, Pallas kernels: 100 us -> 98.4 us  [call(): pl.pallas_call(inner, grid_spec=pltpu.PrefetchScalarGridSpec(num_scalar_p...]
  transfers between devices with their start and end apart: 27 -> 27, of which waited for: 10 -> 11; matrix products, arithmetic and copies ran while one was open for 1% -> 1% of each run, Pallas kernels for 47% -> 46%
where the time goes in v2:
time: 149 us; the launch traced here: 148 us
  Pallas kernels  98.4 us (66%)
  waiting for transfers between devices  24.6 us (17%)
  starting transfers between devices  21.9 us (15%)
  local copies, waits for them, and re-layouts  1.78 us (1%)
    pallas_call x32, Pallas kernels, call(): pl.pallas_call(inner, grid_spec=pltpu.PrefetchScalarGridSpec(num_scalar_p...  98.4 us
    ppermute x10, starting transfers between devices, start(): self.got = lax.ppermute(send, ('dp', 'ctx'), self.pairs[self.step])  12.9 us
    ppermute x4, waiting for transfers between devices, local_pair(): lax.ppermute(v, ('dp', 'ctx'), grid.pairs[0][step - 1])  12.7 us
    ppermute x13, waiting for transfers between devices, local_pair(): swap = lambda v: lax.ppermute(v, 'ctx', [(0, 1), (1, 0)])  7.22 us
    ppermute x4, starting transfers between devices, local_pair(): lax.ppermute(v, ('dp', 'ctx'), grid.pairs[0][step - 1])  5.9 us
    ppermute x10, waiting for transfers between devices, start(): self.got = lax.ppermute(send, ('dp', 'ctx'), self.pairs[self.step])  4.74 us
    ppermute x13, starting transfers between devices, local_pair(): swap = lambda v: lax.ppermute(v, 'ctx', [(0, 1), (1, 0)])  3.19 us
  transfers between devices with their start and end apart: 27, of which 11 were waited for; matrix products, arithmetic and copies ran while one was open for 1% of the time, Pallas kernels for 46%

profile of v2, /device:TPU:0, one launch (start us, length us, event | category | flops | bytes accessed | tf_op | source)
XLA Modules:
  0.0 148.3 jit_solution(5063064090511600215)
XLA Ops:
  1.3 1.9 %collective-permute-done.1.refs_11_ = s32[1,512]{1,0:T(1,128)S(1)} collective-permute-done((s32[1,512]{1,0:T(1,128)}, s32[1,512]{1,0:T(1,128)S(1)}, u32[]{:S(2)}, u32[]{:S(2)}) %collective-permute-start.1) | collective-permute-done | bytes 2080 | tf_op jit(solution)/shard_map/ppermute | solution.py:1083
  3.3 17.8 %attend.1 = (bf16[1024,768]{1,0:T(8,128)(2,1)S(1)}, bf16[1024,384]{1,0:T(8,128)(2,1)S(1)}, bf16[1024,384]{1,0:T(8,128)(2,1)S(1)}, bf16[1024,384]{1,0:T(8,128)(2,...) custom-call(s32[21]{0:T(128)S(1)} %stack.57.refs_0_, ...), custom_call_target="tpu_custom_call" | custom-call | flops 4000000000 | bytes 65536 | tf_op jit(solution)/shard_map/attend/pallas_call | solution.py:58
  21.6 1.8 %collective-permute-done.2.refs_2_.refs_5_ = bf16[384,1024]{1,0:T(8,128)(2,1)S(1)} collective-permute-done((bf16[384,1024]{1,0:T(8,128)(2,1)S(1)}, bf16[384,1024]{1,0:T(8,128)(2,1)S(1)}, u32[]{:S(2)}, u32[]{:S(2)}) %collective-permute-start.2) | collective-permute-done | bytes 786464 | tf_op jit(solution)/shard_map/ppermute | solution.py:1083
  23.4 3.4 %post.1 = (f32[512,768]{1,0:T(8,128)S(1)}, f32[512,768]{1,0:T(8,128)S(1)}, bf16[512,768]{1,0:T(8,128)(2,1)S(1)}, f32[8,128]{1,0:T(8,128)S(1)}) custom-call(s32[21]{0:T(128)S(1)} %stack.57.refs_0_, bf16[384,1024]{1,0:T(8,128)(2,1)S(1)} %get-tuple-element.128.refs_1_.refs_4_, bf16[384,1024]{1,0:T(8,128)(2,1)S(1)} %collective-permute-done.2.refs_2_.refs_5_, ...), custom_call_target="tpu_custom_call" | custom-call | flops 600000000 | bytes 65536 | tf_op jit(solution)/shard_map/post/pallas_call | solution.py:58
  27.3 1.9 %collective-permute-done.3.refs_2_ = bf16[512,768]{1,0:T(8,128)(2,1)S(1)} collective-permute-done((bf16[512,768]{1,0:T(8,128)(2,1)S(1)}, bf16[512,768]{1,0:T(8,128)(2,1)S(1)}, u32[]{:S(2)}, u32[]{:S(2)}) %collective-permute-start.3) | collective-permute-done | bytes 786464 | tf_op jit(solution)/shard_map/ppermute | solution.py:1083
  29.2 7.9 %mlp.1 = (bf16[1024,1536]{1,0:T(8,128)(2,1)S(1)}, bf16[1024,1536]{1,0:T(8,128)(2,1)S(1)}, f32[1,1536]{1,0:T(1,128)S(1)}, f32[1,768]{1,0:T(1,128)S(1)}, f32[8,128]{1,0:T(8,128)S(1)}) custom-call(s32[21]{0:T(128)S(1)} %stack.57.refs_0_, bf16[512,768]{1,0:T(8,128)(2,1)S(1)} %get-tuple-element.131.refs_1_, bf16[512,768]{1,0:T(8,128)(2,1)S(1)} %collective-permute-done.3.refs_2_, ...), custom_call_target="tpu_custom_call" | custom-call | flops 1920000000 | bytes 65536 | tf_op jit(solution)/shard_map/mlp/pallas_call | solution.py:58
  37.6 4.0 %wgrad_fc1.1 = (bf16[2,4,48,1536]{3,2,1,0:T(8,128)(2,1)S(1)}, bf16[2,4,48,1536]{3,2,1,0:T(8,128)(2,1)S(1)}, f32[8,128]{1,0:T(8,128)S(1)}) custom-call(s32[21]{0:T(128)S(1)} %stack.57.refs_0_, bf16[512,768]{1,0:T(8,128)(2,1)S(1)} %get-tuple-element.131.refs_1_, bf16[512,768]{1,0:T(8,128)(2,1)S(1)} %collective-permute-done.3.refs_2_, ...), custom_call_target="tpu_custom_call" | custom-call | flops 840000000 | bytes 65536 | tf_op jit(solution)/shard_map/wgrad_fc1/pallas_call | solution.py:58
  41.6 2.7 %collective-permute-start.8 = (bf16[2,4,48,1536]{3,2,1,0:T(8,128)(2,1)S(1)}, bf16[2,4,48,1536]{3,2,1,0:T(8,128)(2,1)S(1)}, u32[]{:S(2)}, u32[]{:S(2)}) collective-permute-start(bf16[2,4,48,1536]{3,2,1,0:T(8,128)(2,1)S(1)} %get-tuple-element.149), channel_id=1, source_target_pairs={{0,2},{1,5},{2,0},{3,7},{4,6},{5,1},{6,4},{7,3},{8,10},{9,13},{10,... | collective-permute-start | bytes 3538952 | tf_op jit(solution)/shard_map/ppermute | solution.py:1047
  44.3 3.8 %part.2 = (f32[512,768]{1,0:T(8,128)S(1)}, bf16[512,768]{1,0:T(8,128)(2,1)S(1)}, f32[8,128]{1,0:T(8,128)S(1)}) custom-call(s32[21]{0:T(128)S(1)} %stack.57.refs_0_, bf16[1024,1536]{1,0:T(8,128)(2,1)S(1)} %get-tuple-element.135.refs_3_.refs_1_, bf16[768,3072]{1,0:T(8,128)(2,1)S(1)} %copy-done.2, f32[8,128]{1,0:T(8,128)S(1)} %get-tuple-element.137.refs_3_), custom_call_target="tpu_custom_call" | custom-call | flops 840000000 | bytes 65536 | tf_op jit(solution)/shard_map/part/pallas_call | solution.py:58
  48.2 7.0 %wgrad_fc2.1 = (bf16[2,4,192,384]{3,2,1,0:T(8,128)(2,1)S(1)}, bf16[2,4,192,384]{3,2,1,0:T(8,128)(2,1)S(1)}, f32[1,384]{1,0:T(1,128)S(1)}, f32[8,128]{1,0:T(8,128)S(1)}) custom-call(s32[21]{0:T(128)S(1)} %stack.57.refs_0_, bf16[1024,1536]{1,0:T(8,128)(2,1)S(1)} %get-tuple-element.134.refs_1_, bf16[1024,1536]{1,0:T(8,128)(2,1)S(1)} %collective-permute-done.5.refs_2_, ...), custom_call_target="tpu_custom_call" | custom-call | flops 900000000 | bytes 65536 | tf_op jit(solution)/shard_map/wgrad_fc2/pallas_call | solution.py:58
  55.2 3.5 %part.3 = (f32[512,768]{1,0:T(8,128)S(1)}, bf16[512,768]{1,0:T(8,128)(2,1)S(1)}, f32[8,128]{1,0:T(8,128)S(1)}) custom-call(s32[21]{0:T(128)S(1)} %stack.57.refs_0_, bf16[1024,1536]{1,0:T(8,128)(2,1)S(1)} %get-tuple-element.134.refs_1_, bf16[3072,768]{1,0:T(8,128)(2,1)S(1)} %copy-done.1, f32[8,128]{1,0:T(8,128)S(1)} %get-tuple-element.139.refs_3_), custom_call_target="tpu_custom_call" | custom-call | flops 840000000 | bytes 65536 | tf_op jit(solution)/shard_map/part/pallas_call | solution.py:58
  60.7 2.0 %norm2.1 = (f32[512,768]{1,0:T(8,128)S(1)}, bf16[512,768]{1,0:T(8,128)(2,1)S(1)}, f32[8,768]{1,0:T(8,128)S(1)}, f32[8,128]{1,0:T(8,128)S(1)}) custom-call(s32[21]{0:T(128)S(1)} %stack.57.refs_0_, f32[512,768]{1,0:T(8,128)S(1)} %get-tuple-element.145.refs_1_, bf16[512,768]{1,0:T(8,128)(2,1)S(1)} %collective-permute-done.7.refs_2_, ...), custom_call_target="tpu_custom_call" | custom-call | flops 600000000 | bytes 65536 | tf_op jit(solution)/shard_map/norm2/pallas_call | solution.py:58
  64.4 1.6 %collective-permute-start.13 = (bf16[4,48,1536]{2,1,0:T(8,128)(2,1)S(1)}, bf16[4,48,1536]{2,1,0:T(8,128)(2,1)S(1)}, u32[]{:S(2)}, u32[]{:S(2)}) collective-permute-start(bf16[4,48,1536]{2,1,0:T(8,128)(2,1)S(1)} %get-tuple-element.173), channel_id=1, source_target_pairs={{0,8},{1,17},{2,10},{3,19},{4,12},{5,21},{6,14},{7,23},{8,0},{9,25... | collective-permute-start | bytes 1769480 | tf_op jit(solution)/shard_map/ppermute | solution.py:1047
  66.0 2.2 %oproj.1 = (bf16[384,1024]{1,0:T(8,128)(2,1)S(1)}, bf16[2,4,48,1152]{3,2,1,0:T(8,128)(2,1)S(1)}, bf16[2,4,48,1152]{3,2,1,0:T(8,128)(2,1)S(1)}, f32[8,128]{1,0:T(8,128)S(1)}) custom-call(s32[21]{0:T(128)S(1)} %stack.57.refs_0_, bf16[768,768]{1,0:T(8,128)(2,1)S(1)} %copy-done.3, bf16[512,768]{1,0:T(8,128)(2,1)S(1)} %get-tuple-element.152.refs_2_, ...), custom_call_target="tpu_custom_call" | custom-call | flops 600000000 | bytes 65536 | tf_op jit(solution)/shard_map/oproj/pallas_call | solution.py:58
  68.3 14.0 %attn_bwd.2 = (bf16[1024,768]{1,0:T(8,128)(2,1)S(1)}, f32[8,768]{1,0:T(8,128)S(1)}, bf16[2,4,48,1152]{3,2,1,0:T(8,128)(2,1)S(1)}, bf16[2,4,48,1152]{3,2,1,0:T(8,128)(2,1)S(1)}, f32[8,128]{1,0:T(8,128)S(1)}) custom-call(s32[21]{0:T(128)S(1)} %stack.57.refs_0_, ...), custom_call_target="tpu_custom_call", output_to_operand_aliasing={{2}: (16, {}), {3}: (17, {})} | custom-call | flops 3200000000 | bytes 65536 | tf_op jit(solution)/shard_map/attn_bwd/pallas_call | solution.py:58
  83.2 1.5 %fold.7 = (bf16[4,192,384]{2,1,0:T(8,128)(2,1)}, bf16[4,192,384]{2,1,0:T(8,128)(2,1)S(1)}, f32[8,128]{1,0:T(8,128)S(1)}) custom-call(s32[21]{0:T(128)S(1)} %stack.57.refs_0_, bf16[2,4,192,384]{3,2,1,0:T(8,128)(2,1)S(1)} %get-tuple-element.166.refs_1_.refs_3_, bf16[2,4,192,384]{3,2,1,0:T(8,128)(2,1)S(1)} %collective-permute-done.11.refs_2_.refs_4_, ...), custom_call_target="tpu_custom_call" | custom-call | flops 240000000 | bytes 65536 | tf_op jit(solution)/shard_map/fold/pallas_call | solution.py:58
  85.9 1.6 %collective-permute-start.14 = (bf16[2,48,1536]{2,1,0:T(8,128)(2,1)S(1)}, bf16[2,48,1536]{2,1,0:T(8,128)(2,1)S(1)}, u32[]{:S(2)}, u32[]{:S(2)}) collective-permute-start(bf16[2,48,1536]{2,1,0:T(8,128)(2,1)S(1)} %get-tuple-element.184), channel_id=1, source_target_pairs={{0,4},{1,3},{2,6},{3,1},{4,0},{5,7},{6,2},{7,5},{8,12},{9,11},{10,... | collective-permute-start | bytes 884744 | tf_op jit(solution)/shard_map/ppermute | solution.py:1047
  88.1 8.1 %attn_bwd.3 = (bf16[1024,384]{1,0:T(8,128)(2,1)S(1)}, f32[8,768]{1,0:T(8,128)S(1)}, bf16[2,4,48,384]{3,2,1,0:T(8,128)(2,1)S(1)}, bf16[2,4,48,384]{3,2,1,0:T(8,128)(2,1)S(1)}, f32[8,128]{1,0:T(8,128)S(1)}) custom-call(s32[21]{0:T(128)S(1)} %stack.57.refs_0_, bf16[6,1024,1024]{2,1,0:T(8,128)(2,1)} %get-tuple-element.143.refs_1_, ...), custom_call_target="tpu_custom_call" | custom-call | flops 1600000000 | bytes 65536 | tf_op jit(solution)/shard_map/attn_bwd/pallas_call | solution.py:58
  97.8 2.0 %dgrad.2 = (bf16[512,768]{1,0:T(8,128)(2,1)S(1)}, f32[8,128]{1,0:T(8,128)S(1)}) custom-call(s32[21]{0:T(128)S(1)} %stack.57.refs_0_, bf16[1024,768]{1,0:T(8,128)(2,1)S(1)} %get-tuple-element.171.refs_1_, bf16[1024,384]{1,0:T(8,128)(2,1)S(1)} %get-tuple-element.176.refs_2_, bf16[768,2304]{1,0:T(8,128)(2,1)S(1)} %copy-done, bf16[768,2304]{1,0:T(8,128)(2,1)S(1)} %copy-done, ...), custom_call_target="tpu_custom_call" | custom-call | flops 400000000 | bytes 65536 | tf_op jit(solution)/shard_map/dgrad/pallas_call | solution.py:58
  100.2 3.6 %collective-permute-done.12 = bf16[4,192,384]{2,1,0:T(8,128)(2,1)S(1)} collective-permute-done((bf16[4,192,384]{2,1,0:T(8,128)(2,1)}, bf16[4,192,384]{2,1,0:T(8,128)(2,1)S(1)}, u32[]{:S(2)}, u32[]{:S(2)}) %collective-permute-start.12) | collective-permute-done | bytes 589856 | tf_op jit(solution)/shard_map/ppermute | solution.py:1047
  108.3 1.5 %deal.1 = (f32[1,128]{1,0:T(1,128)}, f32[8,8,384]{2,1,0:T(8,128)S(1)}, f32[8,8,384]{2,1,0:T(8,128)S(1)}, f32[8,128]{1,0:T(8,128)S(1)}) custom-call(s32[21]{0:T(128)S(1)} %stack.57.refs_0_, f32[18,8,384]{2,1,0:T(8,128)S(1)} %get-tuple-element.194.refs_1_, f32[18,8,384]{2,1,0:T(8,128)S(1)} %collective-permute-done.17.refs_2_, bf16[128,4608]{1,0:T(8,128)(2,1)S(1)} %copy-done.5, ...), custom_call_target="tpu_custom_call" | custom-call | flops 200000000 | bytes 65536 | tf_op jit(solution)/shard_map/deal/pallas_call | solution.py:58
  111.2 2.0 %dgrad.3 = (f32[512,768]{1,0:T(8,128)S(1)}, f32[8,128]{1,0:T(8,128)S(1)}) custom-call(s32[21]{0:T(128)S(1)} %stack.57.refs_0_, bf16[1024,768]{1,0:T(8,128)(2,1)S(1)} %get-tuple-element.171.refs_1_, bf16[1024,384]{1,0:T(8,128)(2,1)S(1)} %get-tuple-element.176.refs_2_, bf16[768,2304]{1,0:T(8,128)(2,1)S(1)} %copy-done, bf16[768,2304]{1,0:T(8,128)(2,1)S(1)} %copy-done, ...), custom_call_target="tpu_custom_call" | custom-call | flops 400000000 | bytes 65536 | tf_op jit(solution)/shard_map/dgrad/pallas_call | solution.py:58
  114.9 1.5 %collective-permute-start.23 = (bf16[1,96,1536]{2,1,0:T(8,128)(2,1)S(1)}, bf16[1,96,1536]{2,1,0:T(8,128)(2,1)S(1)}, u32[]{:S(2)}, u32[]{:S(2)}) collective-permute-start(bf16[1,96,1536]{2,1,0:T(8,128)(2,1)S(1)} %get-tuple-element.217), channel_id=1, source_target_pairs={{0,16},{1,9},{2,18},{3,11},{4,20},{5,13},{6,22},{7,15},{8,24},{9,1... | collective-permute-start | bytes 884744 | tf_op jit(solution)/shard_map/ppermute | solution.py:1047
  117.7 1.5 %collective-permute-start.20 = (bf16[4,64,384]{2,1,0:T(8,128)(2,1)S(1)}, bf16[4,64,384]{2,1,0:T(8,128)(2,1)S(1)}, u32[]{:S(2)}, u32[]{:S(2)}) collective-permute-start(bf16[4,64,384]{2,1,0:T(8,128)(2,1)S(1)} %get-tuple-element.206), channel_id=1, source_target_pairs={{0,4},{1,3},{2,6},{3,1},{4,0},{5,7},{6,2},{7,5},{8,12},{9,11},{10,... | collective-permute-start | bytes 589832 | tf_op jit(solution)/shard_map/ppermute | solution.py:1137
  119.2 2.5 %norm1.1 = (bf16[512,768]{1,0:T(8,128)(2,1)}, f32[8,128]{1,0:T(8,128)S(1)}) custom-call(s32[21]{0:T(128)S(1)} %stack.57.refs_0_, f32[512,768]{1,0:T(8,128)S(1)} %get-tuple-element.208.refs_1_, bf16[512,768]{1,0:T(8,128)(2,1)S(1)} %collective-permute-done.21.refs_2_, bf16[512,768]{1,0:T(8,128)(2,1)S(1)} %bitcast.35, ...), custom_call_target="tpu_custom_call" | custom-call | flops 600000000 | bytes 65536 | tf_op jit(solution)/shard_map/norm1/pallas_call | solution.py:58
  121.7 1.7 %collective-permute-done.20.refs_4_ = bf16[4,64,384]{2,1,0:T(8,128)(2,1)S(1)} collective-permute-done((bf16[4,64,384]{2,1,0:T(8,128)(2,1)S(1)}, bf16[4,64,384]{2,1,0:T(8,128)(2,1)S(1)}, u32[]{:S(2)}, u32[]{:S(2)}) %collective-permute-start.20) | collective-permute-done | bytes 196640 | tf_op jit(solution)/shard_map/ppermute | solution.py:1137
  126.0 1.6 %collective-permute-done.24.refs_2_ = bf16[96,1536]{1,0:T(8,128)(2,1)S(1)} collective-permute-done((bf16[96,1536]{1,0:T(8,128)(2,1)S(1)}, bf16[96,1536]{1,0:T(8,128)(2,1)S(1)}, u32[]{:S(2)}, u32[]{:S(2)}) %collective-permute-start.24) | collective-permute-done | bytes 294944 | tf_op jit(solution)/shard_map/ppermute | solution.py:1083
  127.6 1.6 %place_ff.1 = (f32[48,3072]{1,0:T(8,128)}, f32[192,768]{1,0:T(8,128)}, f32[8,128]{1,0:T(8,128)S(1)}) custom-call(s32[21]{0:T(128)S(1)} %stack.57.refs_0_, bf16[96,1536]{1,0:T(8,128)(2,1)S(1)} %get-tuple-element.219.refs_1_, bf16[96,1536]{1,0:T(8,128)(2,1)S(1)} %collective-permute-done.24.refs_2_, f32[8,128]{1,0:T(8,128)S(1)} %get-tuple-element.220.refs_3_), custom_call_target="tpu_custom_call" | custom-call | flops 200000000 | bytes 65536 | tf_op jit(solution)/shard_map/place_ff/pallas_call | solution.py:58
  129.2 5.0 %collective-permute-done.22.refs_2_ = bf16[112,1536]{1,0:T(8,128)(2,1)S(1)} collective-permute-done((bf16[112,1536]{1,0:T(8,128)(2,1)S(1)}, bf16[112,1536]{1,0:T(8,128)(2,1)S(1)}, u32[]{:S(2)}, u32[]{:S(2)}) %collective-permute-start.22) | collective-permute-done | bytes 344096 | tf_op jit(solution)/shard_map/ppermute | solution.py:1137
  134.8 1.8 %collective-permute-start.25 = (bf16[64,1536]{1,0:T(8,128)(2,1)S(1)}, bf16[64,1536]{1,0:T(8,128)(2,1)S(1)}, u32[]{:S(2)}, u32[]{:S(2)}) collective-permute-start(bf16[64,1536]{1,0:T(8,128)(2,1)S(1)} %get-tuple-element.226), channel_id=1, source_target_pairs={{0,16},{1,9},{2,18},{3,11},{4,20},{5,13},{6,22},{7,15},{8,24},{9,1... | collective-permute-start | bytes 589832 | tf_op jit(solution)/shard_map/ppermute | solution.py:1137
  136.6 1.7 %mix.1 = (bf16[512,768]{1,0:T(8,128)(2,1)}, f32[8,128]{1,0:T(8,128)S(1)}) custom-call(s32[21]{0:T(128)S(1)} %stack.57.refs_0_, f32[512,768]{1,0:T(8,128)S(1)} %get-tuple-element.140.refs_1_, bf16[512,768]{1,0:T(8,128)(2,1)S(1)} %collective-permute-done.6.refs_2_, f32[512,768]{1,0:T(8,128)S(1)} %get-tuple-element.142.refs_3_, ...), custom_call_target="tpu_custom_call" | custom-call | flops 500000000 | bytes 65536 | tf_op jit(solution)/shard_map/mix/pallas_call | solution.py:58
  138.2 5.3 %collective-permute-done.25.refs_2_.refs_1_ = bf16[64,1536]{1,0:T(8,128)(2,1)S(1)} collective-permute-done((bf16[64,1536]{1,0:T(8,128)(2,1)S(1)}, bf16[64,1536]{1,0:T(8,128)(2,1)S(1)}, u32[]{:S(2)}, u32[]{:S(2)}) %collective-permute-start.25) | collective-permute-done | bytes 196640 | tf_op jit(solution)/shard_map/ppermute | solution.py:1137
  (83 shorter events, 27.2 us)
Async XLA Ops:
  0.6 2.6 %collective-permute-start = (bf16[512,768]{1,0:T(8,128)(2,1)}, bf16[512,768]{1,0:T(8,128)(2,1)S(1)}, u32[]{:S(2)}, u32[]{:S(2)}) collective-permute-start(bf16[512,768]{1,0:T(8,128)(2,1)} %bitcast.32), channel_id=1, source_target_pairs={{0,1},{1,0},{2,3},{3,2},{4,5},{5,4},{6,7},{7,6},{8,9},{9,8},{10,11... | collective-permute-start | bytes 2359304 | tf_op jit(solution)/shard_map/ppermute | solution.py:1083
  1.2 2.1 %collective-permute-start.1 = (s32[1,512]{1,0:T(1,128)}, s32[1,512]{1,0:T(1,128)S(1)}, u32[]{:S(2)}, u32[]{:S(2)}) collective-permute-start(s32[1,512]{1,0:T(1,128)} %refs_10_.2), channel_id=1, source_target_pairs={{0,1},{1,0},{2,3},{3,2},{4,5},{5,4},{6,7},{7,6},{8,9},{9,8},{10,11... | collective-permute-start | bytes 6152 | tf_op jit(solution)/shard_map/ppermute | solution.py:1083
  3.3 20.1 %copy-start.3 = (bf16[768,768]{1,0:T(8,128)(2,1)S(1)}, bf16[768,768]{1,0:T(8,128)(2,1)}, u32[]{:S(2)}) copy-start(bf16[768,768]{1,0:T(8,128)(2,1)} %refs_1_.1) | copy-start | bytes 3538948
  3.3 20.1 %copy-start.7 = (bf16[768]{0:T(1024)(128)(2,1)S(1)}, bf16[768]{0:T(1024)(128)(2,1)}, u32[]{:S(2)}) copy-start(bf16[768]{0:T(1024)(128)(2,1)} %refs_8_.5) | copy-start | bytes 4612
  3.3 25.9 %copy-start.2 = (bf16[768,3072]{1,0:T(8,128)(2,1)S(1)}, bf16[768,3072]{1,0:T(8,128)(2,1)}, u32[]{:S(2)}) copy-start(bf16[768,3072]{1,0:T(8,128)(2,1)} %refs_2_.2) | copy-start | bytes 14155780
  21.1 2.3 %collective-permute-start.2 = (bf16[384,1024]{1,0:T(8,128)(2,1)S(1)}, bf16[384,1024]{1,0:T(8,128)(2,1)S(1)}, u32[]{:S(2)}, u32[]{:S(2)}) collective-permute-start(bf16[384,1024]{1,0:T(8,128)(2,1)S(1)} %get-tuple-element.128.refs_1_.refs_4_), channel_id=1, source_target_pairs={{0,1},{1,0},{2,3},{3,2},{4,5},{5,4},{6,7},{7,6},{8,9},{9,8},{10,11... | collective-permute-start | bytes 2359304 | tf_op jit(solution)/shard_map/ppermute | solution.py:1083
  21.5 5.8 %collective-permute-start.4 = (bf16[512,768]{1,0:T(8,128)(2,1)S(1)}, bf16[512,768]{1,0:T(8,128)(2,1)S(1)}, u32[]{:S(2)}, u32[]{:S(2)}) collective-permute-start(bf16[512,768]{1,0:T(8,128)(2,1)S(1)} %get-tuple-element.132.refs_3_.refs_5_), channel_id=1, source_target_pairs={{0,1},{1,0},{2,3},{3,2},{4,5},{5,4},{6,7},{7,6},{8,9},{9,8},{10,11... | collective-permute-start | bytes 2359304 | tf_op jit(solution)/shard_map/ppermute | solution.py:1083
  26.9 2.4 %collective-permute-start.3 = (bf16[512,768]{1,0:T(8,128)(2,1)S(1)}, bf16[512,768]{1,0:T(8,128)(2,1)S(1)}, u32[]{:S(2)}, u32[]{:S(2)}) collective-permute-start(bf16[512,768]{1,0:T(8,128)(2,1)S(1)} %get-tuple-element.131.refs_1_), channel_id=1, source_target_pairs={{0,1},{1,0},{2,3},{3,2},{4,5},{5,4},{6,7},{7,6},{8,9},{9,8},{10,11... | collective-permute-start | bytes 2359304 | tf_op jit(solution)/shard_map/ppermute | solution.py:1083
  37.1 11.1 %collective-permute-start.5 = (bf16[1024,1536]{1,0:T(8,128)(2,1)S(1)}, bf16[1024,1536]{1,0:T(8,128)(2,1)S(1)}, u32[]{:S(2)}, u32[]{:S(2)}) collective-permute-start(bf16[1024,1536]{1,0:T(8,128)(2,1)S(1)} %get-tuple-element.134.refs_1_), channel_id=1, source_target_pairs={{0,1},{1,0},{2,3},{3,2},{4,5},{5,4},{6,7},{7,6},{8,9},{9,8},{10,11... | collective-permute-start | bytes 9437192 | tf_op jit(solution)/shard_map/ppermute | solution.py:1083
  41.6 18.1 %collective-permute-start.8 = (bf16[2,4,48,1536]{3,2,1,0:T(8,128)(2,1)S(1)}, bf16[2,4,48,1536]{3,2,1,0:T(8,128)(2,1)S(1)}, u32[]{:S(2)}, u32[]{:S(2)}) collective-permute-start(bf16[2,4,48,1536]{3,2,1,0:T(8,128)(2,1)S(1)} %get-tuple-element.149), channel_id=1, source_target_pairs={{0,2},{1,5},{2,0},{3,7},{4,6},{5,1},{6,4},{7,3},{8,10},{9,13},{10,... | collective-permute-start | bytes 3538952 | tf_op jit(solution)/shard_map/ppermute | solution.py:1047
  48.0 12.7 %collective-permute-start.7 = (bf16[512,768]{1,0:T(8,128)(2,1)S(1)}, bf16[512,768]{1,0:T(8,128)(2,1)S(1)}, u32[]{:S(2)}, u32[]{:S(2)}) collective-permute-start(bf16[512,768]{1,0:T(8,128)(2,1)S(1)} %get-tuple-element.146), channel_id=1, source_target_pairs={{0,1},{1,0},{2,3},{3,2},{4,5},{5,4},{6,7},{7,6},{8,9},{9,8},{10,11... | collective-permute-start | bytes 2359304 | tf_op jit(solution)/shard_map/ppermute | solution.py:1083
  62.8 3.2 %collective-permute-start.9 = (bf16[512,768]{1,0:T(8,128)(2,1)S(1)}, bf16[512,768]{1,0:T(8,128)(2,1)S(1)}, u32[]{:S(2)}, u32[]{:S(2)}) collective-permute-start(bf16[512,768]{1,0:T(8,128)(2,1)S(1)} %get-tuple-element.152.refs_2_), channel_id=1, source_target_pairs={{0,1},{1,0},{2,3},{3,2},{4,5},{5,4},{6,7},{7,6},{8,9},{9,8},{10,11... | collective-permute-start | bytes 2359304 | tf_op jit(solution)/shard_map/ppermute | solution.py:1083
  63.2 20.0 %collective-permute-start.11 = (bf16[2,4,192,384]{3,2,1,0:T(8,128)(2,1)S(1)}, bf16[2,4,192,384]{3,2,1,0:T(8,128)(2,1)S(1)}, u32[]{:S(2)}, u32[]{:S(2)}) collective-permute-start(bf16[2,4,192,384]{3,2,1,0:T(8,128)(2,1)S(1)} %get-tuple-element.167), channel_id=1, source_target_pairs={{0,2},{1,5},{2,0},{3,7},{4,6},{5,1},{6,4},{7,3},{8,10},{9,13},{10,... | collective-permute-start | bytes 3538952 | tf_op jit(solution)/shard_map/ppermute | solution.py:1047
  64.4 20.3 %collective-permute-start.13 = (bf16[4,48,1536]{2,1,0:T(8,128)(2,1)S(1)}, bf16[4,48,1536]{2,1,0:T(8,128)(2,1)S(1)}, u32[]{:S(2)}, u32[]{:S(2)}) collective-permute-start(bf16[4,48,1536]{2,1,0:T(8,128)(2,1)S(1)} %get-tuple-element.173), channel_id=1, source_target_pairs={{0,8},{1,17},{2,10},{3,19},{4,12},{5,21},{6,14},{7,23},{8,0},{9,25... | collective-permute-start | bytes 1769480 | tf_op jit(solution)/shard_map/ppermute | solution.py:1047
  82.3 23.9 %collective-permute-start.10 = (bf16[2,4,48,1152]{3,2,1,0:T(8,128)(2,1)S(1)}, bf16[2,4,48,1152]{3,2,1,0:T(8,128)(2,1)S(1)}, u32[]{:S(2)}, u32[]{:S(2)}) collective-permute-start(bf16[2,4,48,1152]{3,2,1,0:T(8,128)(2,1)S(1)} %get-tuple-element.165), channel_id=1, source_target_pairs={{0,2},{1,5},{2,0},{3,7},{4,6},{5,1},{6,4},{7,3},{8,10},{9,13},{10,... | collective-permute-start | bytes 2654216 | tf_op jit(solution)/shard_map/ppermute | solution.py:1047
  85.9 10.4 %collective-permute-start.14 = (bf16[2,48,1536]{2,1,0:T(8,128)(2,1)S(1)}, bf16[2,48,1536]{2,1,0:T(8,128)(2,1)S(1)}, u32[]{:S(2)}, u32[]{:S(2)}) collective-permute-start(bf16[2,48,1536]{2,1,0:T(8,128)(2,1)S(1)} %get-tuple-element.184), channel_id=1, source_target_pairs={{0,4},{1,3},{2,6},{3,1},{4,0},{5,7},{6,2},{7,5},{8,12},{9,11},{10,... | collective-permute-start | bytes 884744 | tf_op jit(solution)/shard_map/ppermute | solution.py:1047
  87.5 16.3 %collective-permute-start.12 = (bf16[4,192,384]{2,1,0:T(8,128)(2,1)}, bf16[4,192,384]{2,1,0:T(8,128)(2,1)S(1)}, u32[]{:S(2)}, u32[]{:S(2)}) collective-permute-start(bf16[4,192,384]{2,1,0:T(8,128)(2,1)} %get-tuple-element.170), channel_id=1, source_target_pairs={{0,8},{1,17},{2,10},{3,19},{4,12},{5,21},{6,14},{7,23},{8,0},{9,25... | collective-permute-start | bytes 1769480 | tf_op jit(solution)/shard_map/ppermute | solution.py:1047
  88.1 9.0 %copy-start.12 = (bf16[1,128]{1,0:T(2,128)(2,1)S(1)}, bf16[1,128]{1,0:T(2,128)(2,1)}, u32[]{:S(2)}) copy-start(bf16[1,128]{1,0:T(2,128)(2,1)} %refs_10_.3) | copy-start | bytes 772
  99.8 19.4 %collective-permute-start.21 = (bf16[512,768]{1,0:T(8,128)(2,1)S(1)}, bf16[512,768]{1,0:T(8,128)(2,1)S(1)}, u32[]{:S(2)}, u32[]{:S(2)}) collective-permute-start(bf16[512,768]{1,0:T(8,128)(2,1)S(1)} %get-tuple-element.209), channel_id=1, source_target_pairs={{0,1},{1,0},{2,3},{3,2},{4,5},{5,4},{6,7},{7,6},{8,9},{9,8},{10,11... | collective-permute-start | bytes 2359304 | tf_op jit(solution)/shard_map/ppermute | solution.py:1083
  104.4 9.8 %collective-permute-start.19 = (bf16[2,192,384]{2,1,0:T(8,128)(2,1)S(1)}, bf16[2,192,384]{2,1,0:T(8,128)(2,1)S(1)}, u32[]{:S(2)}, u32[]{:S(2)}) collective-permute-start(bf16[2,192,384]{2,1,0:T(8,128)(2,1)S(1)} %get-tuple-element.199), channel_id=1, source_target_pairs={{0,4},{1,3},{2,6},{3,1},{4,0},{5,7},{6,2},{7,5},{8,12},{9,11},{10,... | collective-permute-start | bytes 884744 | tf_op jit(solution)/shard_map/ppermute | solution.py:1047
  105.0 3.3 %collective-permute-start.17 = (f32[18,8,384]{2,1,0:T(8,128)S(1)}, f32[18,8,384]{2,1,0:T(8,128)S(1)}, u32[]{:S(2)}, u32[]{:S(2)}) collective-permute-start(f32[18,8,384]{2,1,0:T(8,128)S(1)} %get-tuple-element.194.refs_1_), channel_id=1, source_target_pairs={{0,1},{1,0},{2,3},{3,2},{4,5},{5,4},{6,7},{7,6},{8,9},{9,8},{10,11... | collective-permute-start | bytes 663560 | tf_op jit(solution)/shard_map/ppermute | solution.py:1083
  105.0 11.4 %collective-permute-start.16 = (bf16[2,4,48,384]{3,2,1,0:T(8,128)(2,1)S(1)}, bf16[2,4,48,384]{3,2,1,0:T(8,128)(2,1)S(1)}, u32[]{:S(2)}, u32[]{:S(2)}) collective-permute-start(bf16[2,4,48,384]{3,2,1,0:T(8,128)(2,1)S(1)} %get-tuple-element.193), channel_id=1, source_target_pairs={{0,2},{1,5},{2,0},{3,7},{4,6},{5,1},{6,4},{7,3},{8,10},{9,13},{10,... | collective-permute-start | bytes 884744 | tf_op jit(solution)/shard_map/ppermute | solution.py:1047
  107.4 14.3 %collective-permute-start.15 = (bf16[4,48,1152]{2,1,0:T(8,128)(2,1)S(1)}, bf16[4,48,1152]{2,1,0:T(8,128)(2,1)S(1)}, u32[]{:S(2)}, u32[]{:S(2)}) collective-permute-start(bf16[4,48,1152]{2,1,0:T(8,128)(2,1)S(1)} %get-tuple-element.191), channel_id=1, source_target_pairs={{0,4},{1,3},{2,6},{3,1},{4,0},{5,7},{6,2},{7,5},{8,12},{9,11},{10,... | collective-permute-start | bytes 1327112 | tf_op jit(solution)/shard_map/ppermute | solution.py:1047
  109.8 7.3 %collective-permute-start.18 = (f32[8,8,384]{2,1,0:T(8,128)S(1)}, f32[8,8,384]{2,1,0:T(8,128)S(1)}, u32[]{:S(2)}, u32[]{:S(2)}) collective-permute-start(f32[8,8,384]{2,1,0:T(8,128)S(1)} %get-tuple-element.197), channel_id=1, source_target_pairs={{0,2},{1,5},{2,0},{3,7},{4,6},{5,1},{6,4},{7,3},{8,10},{9,13},{10,... | collective-permute-start | bytes 294920 | tf_op jit(solution)/shard_map/ppermute | solution.py:1137
  113.2 6.0 %copy-start.4 = (bf16[1,512,768]{2,1,0:T(8,128)(2,1)S(1)}, bf16[1,512,768]{2,1,0:T(8,128)(2,1)}, u32[]{:S(2)}) copy-start(bf16[1,512,768]{2,1,0:T(8,128)(2,1)} %param.16) | copy-start | bytes 2359300
  114.9 10.5 %collective-permute-start.23 = (bf16[1,96,1536]{2,1,0:T(8,128)(2,1)S(1)}, bf16[1,96,1536]{2,1,0:T(8,128)(2,1)S(1)}, u32[]{:S(2)}, u32[]{:S(2)}) collective-permute-start(bf16[1,96,1536]{2,1,0:T(8,128)(2,1)S(1)} %get-tuple-element.217), channel_id=1, source_target_pairs={{0,16},{1,9},{2,18},{3,11},{4,20},{5,13},{6,22},{7,15},{8,24},{9,1... | collective-permute-start | bytes 884744 | tf_op jit(solution)/shard_map/ppermute | solution.py:1047
  116.4 20.2 %collective-permute-start.6 = (bf16[512,768]{1,0:T(8,128)(2,1)S(1)}, bf16[512,768]{1,0:T(8,128)(2,1)S(1)}, u32[]{:S(2)}, u32[]{:S(2)}) collective-permute-start(bf16[512,768]{1,0:T(8,128)(2,1)S(1)} %copy-done.11), channel_id=1, source_target_pairs={{0,1},{1,0},{2,3},{3,2},{4,5},{5,4},{6,7},{7,6},{8,9},{9,8},{10,11... | collective-permute-start | bytes 2359304 | tf_op jit(solution)/shard_map/ppermute | solution.py:1083
  117.7 5.7 %collective-permute-start.20 = (bf16[4,64,384]{2,1,0:T(8,128)(2,1)S(1)}, bf16[4,64,384]{2,1,0:T(8,128)(2,1)S(1)}, u32[]{:S(2)}, u32[]{:S(2)}) collective-permute-start(bf16[4,64,384]{2,1,0:T(8,128)(2,1)S(1)} %get-tuple-element.206), channel_id=1, source_target_pairs={{0,4},{1,3},{2,6},{3,1},{4,0},{5,7},{6,2},{7,5},{8,12},{9,11},{10,... | collective-permute-start | bytes 589832 | tf_op jit(solution)/shard_map/ppermute | solution.py:1137
  124.1 10.1 %collective-permute-start.22 = (bf16[112,1536]{1,0:T(8,128)(2,1)S(1)}, bf16[112,1536]{1,0:T(8,128)(2,1)S(1)}, u32[]{:S(2)}, u32[]{:S(2)}) collective-permute-start(bf16[112,1536]{1,0:T(8,128)(2,1)S(1)} %get-tuple-element.214), channel_id=1, source_target_pairs={{0,8},{1,17},{2,10},{3,19},{4,12},{5,21},{6,14},{7,23},{8,0},{9,25... | collective-permute-start | bytes 1032200 | tf_op jit(solution)/shard_map/ppermute | solution.py:1137
  125.9 1.6 %collective-permute-start.24 = (bf16[96,1536]{1,0:T(8,128)(2,1)S(1)}, bf16[96,1536]{1,0:T(8,128)(2,1)S(1)}, u32[]{:S(2)}, u32[]{:S(2)}) collective-permute-start(bf16[96,1536]{1,0:T(8,128)(2,1)S(1)} %get-tuple-element.219.refs_1_), channel_id=1, source_target_pairs={{0,1},{1,0},{2,3},{3,2},{4,5},{5,4},{6,7},{7,6},{8,9},{9,8},{10,11... | collective-permute-start | bytes 884744 | tf_op jit(solution)/shard_map/ppermute | solution.py:1083
  134.8 8.7 %collective-permute-start.25 = (bf16[64,1536]{1,0:T(8,128)(2,1)S(1)}, bf16[64,1536]{1,0:T(8,128)(2,1)S(1)}, u32[]{:S(2)}, u32[]{:S(2)}) collective-permute-start(bf16[64,1536]{1,0:T(8,128)(2,1)S(1)} %get-tuple-element.226), channel_id=1, source_target_pairs={{0,16},{1,9},{2,18},{3,11},{4,20},{5,13},{6,22},{7,15},{8,24},{9,1... | collective-permute-start | bytes 589832 | tf_op jit(solution)/shard_map/ppermute | solution.py:1137
  144.1 2.8 %collective-permute-start.26 = (bf16[48,1536]{1,0:T(8,128)(2,1)S(1)}, bf16[48,1536]{1,0:T(8,128)(2,1)S(1)}, u32[]{:S(2)}, u32[]{:S(2)}) collective-permute-start(bf16[48,1536]{1,0:T(8,128)(2,1)S(1)} %get-tuple-element.232.refs_1_), channel_id=1, source_target_pairs={{0,1},{1,0},{2,3},{3,2},{4,5},{5,4},{6,7},{7,6},{8,9},{9,8},{10,11... | collective-permute-start | bytes 442376 | tf_op jit(solution)/shard_map/ppermute | solution.py:1083
  (8 other events, 28.2 us)
